TPU v7x, 32 devices: a whole 2x2x4 slice. The times are simulated.
32 devices in a mesh: dp: 8 (over z, core), ctx: 4 (over y, x).
Axes of the slice: x: 2, y: 2, z: 4, core: 2. Of those that a mesh axis runs over, the one named last changes fastest.
Arguments:
- hidden: bfloat16 [8, 512, 5120], P('dp', 'ctx'), may hold values from -6 to 6
- queries: bfloat16 [8, 512, 4096], P('dp', 'ctx'), may hold values from -6 to 6
- key_states: bfloat16 [8, 512, 512], P('dp', 'ctx'), may hold values from -6 to 6
- out_grad: bfloat16 [8, 512, 4096], P('dp', 'ctx'), may hold values from -6 to 6
- w_value: bfloat16 [5120, 512], replicated, may hold values from -0.078125 to 0.078125
- q_gain: float32 [128], replicated, may hold values from 0.1 to 1.9
- k_gain: float32 [128], replicated, may hold values from 0.1 to 1.9
- dest_rows: int32 [8, 512], P('dp', 'ctx'), may hold values from 0 to 511, as said below
- doc_ids: int32 [8, 512], P('dp', 'ctx'), may hold values from 0 to 3, never falling along the last dimension, each value on 1 to 256 neighbouring positions
Outputs:
- hidden_grad: bfloat16 [8, 512, 5120], P('dp', 'ctx')
- query_grad: bfloat16 [8, 512, 4096], P('dp', 'ctx')
- key_grad: bfloat16 [8, 512, 512], P('dp', 'ctx')
- weight_grad: float32 [5120, 512], P(('dp', 'ctx'))
Inputs may be any that keep to these rules, and one draw needn't show every extreme that they name: `dest_rows`: within each data group the entries are a permutation of the slab's rows; the 128 entries of one block of arrival rows name exactly 64 or no rows of each block of 128 slab rows. `doc_ids`: ids never fall along a slab.
All inputs are finite; a program needn't handle non-finite values.
Results may differ from a plain program's by a relative error of at most 0.017.
Values may be sent and summed in bfloat16 or wider, within the bound.
No kernel may reach another device: no remote copies, remote signals or barrier semaphores. Data moves between devices by JAX's collectives and lax.ppermute only.
A program may use at most 128 MiB of HBM per device.

v0:
```python
import jax
import jax.numpy as jnp
from jax import lax
from jax.sharding import PartitionSpec as P

epsilon = 1e-06
rope_base = 1000000.0


def doc_positions(doc_ids):
    position_index = jnp.arange(doc_ids.shape[0], dtype=jnp.int32)
    change = jnp.concatenate([jnp.ones((1,), dtype=bool), doc_ids[1:] != doc_ids[:-1]])
    starts = lax.cummax(jnp.where(change, position_index, 0), axis=0)
    return position_index - starts


def rope_tables(positions, head_width):
    half_width = head_width // 2
    frequency = rope_base ** (-(jnp.arange(half_width, dtype=jnp.float32) * 2.0 / head_width))
    angles = positions.astype(jnp.float32)[:, None] * frequency[None, :]
    return (jnp.cos(angles), jnp.sin(angles))


def norm_rope(vector, gain_vector, cosine, sine_table):
    inverse_rms = lax.rsqrt(jnp.mean(vector * vector, axis=-1, keepdims=True) + epsilon)
    normed = vector * inverse_rms * gain_vector
    half_width = vector.shape[-1] // 2
    first_half = normed[..., :half_width]
    second_half = normed[..., half_width:]
    cos_rows = cosine[:, None, :]
    sin_rows = sine_table[:, None, :]
    return jnp.concatenate(
        [
            first_half * cos_rows - second_half * sin_rows,
            second_half * cos_rows + first_half * sin_rows,
        ],
        axis=-1,
    )


def tile_mask(doc_ids, i, j, tile_rows):
    query_docs = doc_ids[i * tile_rows : (i + 1) * tile_rows]
    key_docs = doc_ids[j * tile_rows : (j + 1) * tile_rows]
    allowed = query_docs[:, None] == key_docs[None, :]
    if i == j:
        tile_index = jnp.arange(tile_rows, dtype=jnp.int32)
        allowed = allowed & (tile_index[:, None] >= tile_index[None, :])
    return allowed


def attention(q_normed, k_normed, v_heads, g_heads, doc_ids, tile_rows):
    length, head_count, head_width = q_normed.shape
    tile_count = length // tile_rows
    factor = head_width ** (-0.5)

    def tile(array, i):
        return array[i * tile_rows : (i + 1) * tile_rows]

    def weights(i, j):
        logits = (
            jnp.einsum(
                "qhd,kd->hqk",
                tile(q_normed, i),
                tile(k_normed, j),
                preferred_element_type=jnp.float32,
            )
            * factor
        )
        return jnp.where(tile_mask(doc_ids, i, j, tile_rows)[None], jnp.exp(logits), 0.0)

    totals = []
    outputs = []
    for i in range(tile_count):
        denominator = jnp.zeros((head_count, tile_rows), jnp.float32)
        accumulated = jnp.zeros((head_count, tile_rows, head_width), jnp.float32)
        for j in range(i + 1):
            exponent = weights(i, j)
            add_denominator = jnp.sum(exponent, axis=-1)
            add_accumulated = jnp.einsum(
                "hqk,kd->hqd",
                exponent.astype(jnp.bfloat16),
                tile(v_heads, j),
                preferred_element_type=jnp.float32,
            )
            denominator = denominator + add_denominator
            accumulated = accumulated + add_accumulated
        totals.append(denominator)
        outputs.append(accumulated / denominator[..., None])
    q_grads = [
        jnp.zeros((tile_rows, head_count, head_width), jnp.float32) for i in range(tile_count)
    ]
    k_grads = [jnp.zeros((tile_rows, head_width), jnp.float32) for i in range(tile_count)]
    v_grads = [jnp.zeros((tile_rows, head_width), jnp.float32) for i in range(tile_count)]
    for i in range(tile_count):
        g_block = tile(g_heads, i).astype(jnp.float32)
        delta_row = jnp.sum(jnp.swapaxes(g_block, 0, 1) * outputs[i], axis=-1)
        for j in range(i + 1):
            probability = weights(i, j) / totals[i][..., None]
            g_tile = tile(g_heads, i)
            v_part = jnp.einsum(
                "hqk,qhd->kd",
                probability.astype(jnp.bfloat16),
                g_tile,
                preferred_element_type=jnp.float32,
            )
            prob_grad = jnp.einsum(
                "qhd,kd->hqk", g_tile, tile(v_heads, j), preferred_element_type=jnp.float32
            )
            dlogit = (probability * (prob_grad - delta_row[..., None])).astype(jnp.bfloat16)
            q_part = (
                jnp.einsum(
                    "hqk,kd->qhd", dlogit, tile(k_normed, j), preferred_element_type=jnp.float32
                )
                * factor
            )
            k_part = (
                jnp.einsum(
                    "hqk,qhd->kd", dlogit, tile(q_normed, i), preferred_element_type=jnp.float32
                )
                * factor
            )
            q_part, k_part, v_part = (q_part, k_part, v_part)
            q_grads[i] = q_grads[i] + q_part
            k_grads[j] = k_grads[j] + k_part
            v_grads[j] = v_grads[j] + v_part
    return (
        jnp.concatenate(q_grads, axis=0),
        jnp.concatenate(k_grads, axis=0),
        jnp.concatenate(v_grads, axis=0),
    )


def on_device(hidden, queries, key_states, out_grad, w_value, q_gain, k_gain, dest_rows, doc_ids):
    tok_rows = hidden.shape[1]
    model_width = hidden.shape[2]
    head_width = q_gain.shape[0]
    ctx_count = lax.axis_size("ctx")
    slab_rows = tok_rows * ctx_count
    bucket = 2 * tok_rows // ctx_count
    kv_count = key_states.shape[2] // head_width
    set_heads = queries.shape[2] // (ctx_count * head_width)
    share_count = ctx_count // kv_count
    tile_rows = max(slab_rows // 8, min(512, slab_rows // 4))
    arriving = hidden[0]
    targets = dest_rows[0]
    owner_dev = targets // tok_rows
    row_in_dest = targets % tok_rows
    peer_index = jnp.arange(ctx_count, dtype=jnp.int32)
    to_owner = (owner_dev[:, None] == peer_index[None, :]).astype(jnp.int32)
    order_in_bucket = jnp.sum((jnp.cumsum(to_owner, axis=0) - 1) * to_owner, axis=1)
    slot_index = owner_dev * bucket + order_in_bucket
    selector = jnp.arange(ctx_count * bucket, dtype=jnp.int32)[:, None] == slot_index[None, :]
    outgoing = jnp.dot(selector.astype(jnp.bfloat16), arriving, preferred_element_type=jnp.float32)
    outgoing = outgoing.astype(jnp.bfloat16).reshape(ctx_count, bucket, model_width)
    rows_sent = jnp.where(
        jnp.any(selector, axis=1), jnp.sum(jnp.where(selector, row_in_dest[None, :], 0), axis=1), -1
    )
    rows_sent = rows_sent.reshape(ctx_count, bucket)
    incoming, rows_got = (
        lax.all_to_all(outgoing, "ctx", split_axis=0, concat_axis=0, tiled=True),
        lax.all_to_all(rows_sent, "ctx", split_axis=0, concat_axis=0, tiled=True),
    )
    placing = jnp.arange(tok_rows, dtype=jnp.int32)[:, None] == rows_got.reshape(-1)[None, :]
    balanced = jnp.dot(
        placing.astype(jnp.bfloat16),
        incoming.reshape(ctx_count * bucket, model_width),
        preferred_element_type=jnp.float32,
    ).astype(jnp.bfloat16)
    value_rows = jnp.dot(balanced, w_value, preferred_element_type=jnp.float32).astype(jnp.bfloat16)
    slab_docs = lax.all_gather(doc_ids[0], "ctx", axis=0, tiled=True)
    cosine, sine_table = rope_tables(doc_positions(slab_docs), head_width)
    q_leaving = queries[0].reshape(tok_rows, ctx_count, set_heads * head_width)
    key_value = jnp.concatenate(
        [
            key_states[0].reshape(tok_rows, kv_count, head_width),
            value_rows.reshape(tok_rows, kv_count, head_width),
        ],
        axis=2,
    )
    key_value = jnp.repeat(key_value, share_count, axis=1)
    g_leaving = out_grad[0].reshape(tok_rows, ctx_count, set_heads * head_width)
    q_arrived, kv_arrived, g_arrived = (
        lax.all_to_all(q_leaving, "ctx", split_axis=1, concat_axis=0, tiled=True),
        lax.all_to_all(key_value, "ctx", split_axis=1, concat_axis=0, tiled=True),
        lax.all_to_all(g_leaving, "ctx", split_axis=1, concat_axis=0, tiled=True),
    )
    q_arrived = q_arrived.reshape(slab_rows, set_heads, head_width)
    g_arrived = g_arrived.reshape(slab_rows, set_heads, head_width)
    k_arrived = kv_arrived[:, :, :head_width]
    v_arrived = kv_arrived[:, 0, head_width:]
    q_normed, q_back = jax.vjp(
        lambda operand: norm_rope(operand, q_gain, cosine, sine_table),
        q_arrived.astype(jnp.float32),
    )
    k_normed, k_back = jax.vjp(
        lambda operand: norm_rope(operand, k_gain, cosine, sine_table),
        k_arrived.astype(jnp.float32),
    )
    q_grad, k_grad, v_grad = attention(
        q_normed.astype(jnp.bfloat16),
        k_normed[:, 0].astype(jnp.bfloat16),
        v_arrived,
        g_arrived,
        slab_docs,
        tile_rows,
    )
    q_sending = q_back(q_grad)[0].astype(jnp.bfloat16).reshape(slab_rows, 1, set_heads * head_width)
    k_pre = k_back(k_grad[:, None, :])[0].astype(jnp.bfloat16)
    kv_sending = jnp.concatenate([k_pre, v_grad.astype(jnp.bfloat16)[:, None, :]], axis=2)
    q_back_rows, kv_back_rows = (
        lax.all_to_all(q_sending, "ctx", split_axis=0, concat_axis=1, tiled=True),
        lax.all_to_all(kv_sending, "ctx", split_axis=0, concat_axis=1, tiled=True),
    )
    query_grad = q_back_rows.reshape(tok_rows, ctx_count * set_heads * head_width)
    summed = kv_back_rows.astype(jnp.float32).reshape(
        tok_rows, kv_count, share_count, 2 * head_width
    )
    summed = jnp.sum(summed, axis=2)
    key_grad = (
        summed[..., :head_width].astype(jnp.bfloat16).reshape(tok_rows, kv_count * head_width)
    )
    value_grad = (
        summed[..., head_width:].astype(jnp.bfloat16).reshape(tok_rows, kv_count * head_width)
    )
    hidden_grad = jnp.einsum(
        "tk,dk->td", value_grad, w_value, preferred_element_type=jnp.float32
    ).astype(jnp.bfloat16)
    dp_count = lax.axis_size("dp")
    device_count = dp_count * ctx_count
    inverse_count = 1.0 / device_count
    share_width = model_width // device_count
    feature_split = balanced.reshape(tok_rows, dp_count, ctx_count, share_width)
    feature_rows = lax.all_to_all(feature_split, "ctx", split_axis=2, concat_axis=0, tiled=True)
    feature_rows = feature_rows.reshape(slab_rows, dp_count * share_width)
    share_sum = (
        jnp.einsum(
            "td,tk->dk",
            feature_rows,
            lax.all_gather(value_grad, "ctx", axis=0, tiled=True),
            preferred_element_type=jnp.float32,
        )
        * inverse_count
    )
    weight_grad = lax.psum_scatter(
        share_sum.astype(jnp.bfloat16), "dp", scatter_dimension=0, tiled=True
    ).astype(jnp.float32)
    return (hidden_grad[None], query_grad[None], key_grad[None], weight_grad)


def solution(mesh):
    return jax.shard_map(
        on_device,
        mesh=mesh,
        in_specs=(
            P("dp", "ctx", None),
            P("dp", "ctx", None),
            P("dp", "ctx", None),
            P("dp", "ctx", None),
            P(),
            P(),
            P(),
            P("dp", "ctx"),
            P("dp", "ctx"),
        ),
        out_specs=(
            P("dp", "ctx", None),
            P("dp", "ctx", None),
            P("dp", "ctx", None),
            P(("dp", "ctx"), None),
        ),
        check_vma=False,
    )
```

profile of v0, /device:TPU:0, one launch (start us, length us, event | category | flops | bytes accessed | tf_op | source)
XLA Modules:
  0.0 239.8 jit_solution(5070866990805751254)
XLA Ops:
  10.0 5.2 %all-to-all-start = ((s32[4,1,64]{2,1,0:T(1,128)}), s32[4,1,64]{2,1,0:T(1,128)S(1)}, u32[]{:S(2)}, u32[]{:S(2)}) async-start(s32[4,1,64]{2,1,0:T(1,128)} %select_n.90), calls=%async_computation | async-start | bytes 4096 | tf_op jit(solution)/shard_map/all_to_all | solution.py:161
  15.1 8.5 %all-gather = s32[1,512]{1,0:T(1,128)S(1)} all-gather(s32[1,128]{1,0:T(1,128)} %param.17), channel_id=2, replica_groups=mesh['dp'=8,'ctx'=4] {'ctx'}, dimensions={1}, use_global_device_ids=true | all-gather | bytes 2560 | tf_op jit(solution)/shard_map/all_gather | solution.py:170
  24.3 1.8 reshape_squeeze.10
  26.2 1.3 copy.548
  27.5 3.5 %all-to-all-start.3 = ((bf16[128,4,1024]{2,0,1:T(8,128)(2,1)}), bf16[128,4,1024]{2,0,1:T(8,128)(2,1)S(1)}, u32[]{:S(2)}, u32[]{:S(2)}) async-start(bf16[128,4,1024]{2,0,1:T(8,128)(2,1)} %copy.548), calls=%async_computation.3 | async-start | bytes 2097152 | tf_op jit(solution)/shard_map/all_to_all | solution.py:183
  31.8 2.3 copy.666
  34.9 2.4 convolution_convert_fusion
  37.3 5.3 %all-to-all-done.3 = bf16[128,4,1024]{2,0,1:T(8,128)(2,1)S(1)} async-done(((bf16[128,4,1024]{2,0,1:T(8,128)(2,1)}), bf16[128,4,1024]{2,0,1:T(8,128)(2,1)S(1)}, u32[]{:S(2)}, u32[]{:S(2)}) %all-to-all-start.3) | async-done | bytes 1048608 | tf_op jit(solution)/shard_map/all_to_all | solution.py:183
  42.6 4.6 %all-to-all-start.1 = ((bf16[4,64,5120]{2,1,0:T(8,128)(2,1)}), bf16[4,64,5120]{2,1,0:T(8,128)(2,1)}, u32[]{:S(2)}, u32[]{:S(2)}) async-start(bf16[4,64,5120]{2,1,0:T(8,128)(2,1)} %bitcast.497), calls=%async_computation.1 | async-start | bytes 5242880 | tf_op jit(solution)/shard_map/all_to_all | solution.py:160
  47.2 1.7 multiply_cosine_fusion
  54.5 1.2 fusion.133
  55.7 21.4 %all-to-all-done.1 = bf16[4,64,5120]{2,1,0:T(8,128)(2,1)} async-done(((bf16[4,64,5120]{2,1,0:T(8,128)(2,1)}), bf16[4,64,5120]{2,1,0:T(8,128)(2,1)}, u32[]{:S(2)}, u32[]{:S(2)}) %all-to-all-start.1) | async-done | bytes 2621472 | tf_op jit(solution)/shard_map/all_to_all | solution.py:160
  77.1 4.3 %all-to-all-start.4 = ((bf16[128,4,1024]{0,2,1:T(8,128)(2,1)}), bf16[128,4,1024]{0,2,1:T(8,128)(2,1)}, u32[]{:S(2)}, u32[]{:S(2)}) async-start(bf16[128,4,1024]{0,2,1:T(8,128)(2,1)} %bitcast.503), calls=%async_computation.4 | async-start | bytes 2097152 | tf_op jit(solution)/shard_map/all_to_all | solution.py:185
  81.4 2.3 convolution_convert_fusion.2
  83.7 1.0 copy-done.6
  84.8 3.4 %convolution_convert_fusion.3 = bf16[128,512]{1,0:T(8,128)(2,1)S(1)} fusion(bf16[128,5120]{1,0:T(8,128)(2,1)S(1)} %convolution_convert_fusion.2, bf16[5120,512]{1,0:T(8,128)(2,1)} %param.13), kind=kOutput, calls=%fused_computation.132 | convolution fusion | flops 671154176 | bytes 6684672 | tf_op jit(solution)/shard_map/dot_general | solution.py:169
  88.9 1.7 pad_maximum_fusion.2
  90.6 1.8 copy.547
  92.4 2.2 all-to-all-done.4
  94.6 4.2 %all-to-all-start.2 = ((bf16[128,4,256]{2,0,1:T(8,128)(2,1)}), bf16[128,4,256]{2,0,1:T(8,128)(2,1)}, u32[]{:S(2)}, u32[]{:S(2)}) async-start(bf16[128,4,256]{2,0,1:T(8,128)(2,1)} %copy.547), calls=%async_computation.2 | async-start | bytes 524288 | tf_op jit(solution)/shard_map/all_to_all | solution.py:184
  98.8 2.2 fusion.185
  101.0 2.5 %copy.610 = bf16[128,5120]{0,1:T(8,128)(2,1)} copy(bf16[128,5120]{1,0:T(8,128)(2,1)} %copy-done.6) | data formatting | bytes 2621440 | tf_op jit(solution)/shard_map/convert_element_type | solution.py:168
  103.4 2.5 %copy.611 = bf16[128,8,4,160]{0,3,1,2:T(8,128)(2,1)} copy(bf16[128,8,4,160]{0,3,2,1:T(8,128)(2,1)} %bitcast.500) | data formatting | bytes 2621440 | tf_op jit(solution)/shard_map/reshape | solution.py:232
  105.9 1.1 fusion.128
  107.1 1.1 fusion.129
  108.2 1.2 fusion.122
  109.5 1.2 fusion.195
  113.0 1.1 fusion.82
  122.0 1.1 fusion.81
  125.0 1.1 fusion.77
  134.4 1.1 fusion.80
  140.6 1.1 convolution_add_fusion.4
  143.9 1.8 fusion.186
  145.6 1.1 fusion.65
  148.4 2.1 fusion.83
  150.5 1.6 fusion.79
  152.9 1.2 fusion.125
  154.2 1.1 fusion.130
  155.3 1.2 fusion.127
  159.6 4.0 %all-to-all-start.5 = ((bf16[4,2,16384]{2,1,0:T(2,128)(2,1)}), bf16[4,2,16384]{2,1,0:T(2,128)(2,1)S(1)}, u32[]{:S(2)}, u32[]{:S(2)}) async-start(bf16[4,2,16384]{2,1,0:T(2,128)(2,1)} %reshape.736), calls=%async_computation.5 | async-start | bytes 524288 | tf_op jit(solution)/shard_map/all_to_all | solution.py:212
  163.6 1.1 fusion.67
  164.7 4.3 %all-to-all-done.5 = bf16[4,2,16384]{2,1,0:T(2,128)(2,1)S(1)} async-done(((bf16[4,2,16384]{2,1,0:T(2,128)(2,1)}), bf16[4,2,16384]{2,1,0:T(2,128)(2,1)S(1)}, u32[]{:S(2)}, u32[]{:S(2)}) %all-to-all-start.5) | async-done | bytes 262176 | tf_op jit(solution)/shard_map/all_to_all | solution.py:212
  169.6 3.8 %all-to-all-start.7 = ((bf16[128,8,4,160]{0,3,1,2:T(8,128)(2,1)}), bf16[128,8,4,160]{0,3,1,2:T(8,128)(2,1)S(1)}, u32[]{:S(2)}, u32[]{:S(2)}) async-start(bf16[128,8,4,160]{0,3,1,2:T(8,128)(2,1)} %copy.611), calls=%async_computation.7 | async-start | bytes 2621440 | tf_op jit(solution)/shard_map/all_to_all | solution.py:233
  173.4 1.3 fusion.199
  174.7 1.2 convolution_add_fusion.2
  176.0 1.1 convolution_add_fusion.1
  177.1 1.9 reshape.737
  178.9 1.1 copy.677
  180.8 1.7 copy.593
  182.4 12.1 %all_gather.7 = bf16[512,512]{0,1:T(8,128)(2,1)} all-gather(bf16[128,512]{0,1:T(8,128)(2,1)} %bitcast.506), channel_id=1, replica_groups=mesh['dp'=8,'ctx'=4] {'ctx'}, dimensions={0}, use_global_device_ids=true | all-gather | bytes 655360 | tf_op jit(solution)/shard_map/all_gather | solution.py:239
  195.6 2.0 fusion.1
  198.6 1.2 fusion.69
  199.8 1.4 pad_maximum_fusion
  202.2 1.3 multiply_reduce_fusion
  203.5 1.9 fusion.2
  206.0 1.5 reduce.11
  208.0 2.0 reshape.738
  210.0 3.5 %all-to-all-start.6 = ((bf16[4,2,65536]{2,1,0:T(2,128)(2,1)}), bf16[4,2,65536]{2,1,0:T(2,128)(2,1)S(1)}, u32[]{:S(2)}, u32[]{:S(2)}) async-start(bf16[4,2,65536]{2,1,0:T(2,128)(2,1)} %reshape.738), calls=%async_computation.6 | async-start | bytes 2097152 | tf_op jit(solution)/shard_map/all_to_all | solution.py:211
  214.5 5.4 %fusion = bf16[1,128,5120]{2,1,0:T(8,128)(2,1)} fusion(bf16[128,512]{0,1:T(8,128)(2,1)S(1)} %bitcast.507, bf16[5120,512]{1,0:T(8,128)(2,1)} %param.13), kind=kOutput, calls=%fused_computation.3 | convolution fusion | flops 671744000 | bytes 6684672 | tf_op jit(solution)/shard_map/tk,dk->td/dot_general | solution.py:225
  219.9 4.3 %all-to-all-done.6 = bf16[4,2,65536]{2,1,0:T(2,128)(2,1)S(1)} async-done(((bf16[4,2,65536]{2,1,0:T(2,128)(2,1)}), bf16[4,2,65536]{2,1,0:T(2,128)(2,1)S(1)}, u32[]{:S(2)}, u32[]{:S(2)}) %all-to-all-start.6) | async-done | bytes 1048608 | tf_op jit(solution)/shard_map/all_to_all | solution.py:211
  225.5 1.3 copy.608
  226.8 2.3 copy.613
  229.1 2.2 reduce-scatter.2.cloned.1.call-done
  231.3 1.7 convert_element_type.220
  (255 shorter events, 51.7 us)
Async XLA Ops:
  7.2 27.7 %copy-start = (bf16[1,128,5120]{2,1,0:T(8,128)(2,1)S(1)}, bf16[1,128,5120]{2,1,0:T(8,128)(2,1)}, u32[]{:S(2)}) copy-start(bf16[1,128,5120]{2,1,0:T(8,128)(2,1)} %param.9) | copy-start | bytes 3932164
  10.0 17.5 %all-to-all-start = ((s32[4,1,64]{2,1,0:T(1,128)}), s32[4,1,64]{2,1,0:T(1,128)S(1)}, u32[]{:S(2)}, u32[]{:S(2)}) async-start(s32[4,1,64]{2,1,0:T(1,128)} %select_n.90), calls=%async_computation | async-start | bytes 4096 | tf_op jit(solution)/shard_map/all_to_all | solution.py:161
  26.2 4.8 %copy-start.43 = (bf16[1,128,512]{2,1,0:T(8,128)(2,1)S(1)}, bf16[1,128,512]{2,1,0:T(8,128)(2,1)}, u32[]{:S(2)}) copy-start(bf16[1,128,512]{2,1,0:T(8,128)(2,1)} %param.11) | copy-start | bytes 393220
  27.5 15.1 %all-to-all-start.3 = ((bf16[128,4,1024]{2,0,1:T(8,128)(2,1)}), bf16[128,4,1024]{2,0,1:T(8,128)(2,1)S(1)}, u32[]{:S(2)}, u32[]{:S(2)}) async-start(bf16[128,4,1024]{2,0,1:T(8,128)(2,1)} %copy.548), calls=%async_computation.3 | async-start | bytes 2097152 | tf_op jit(solution)/shard_map/all_to_all | solution.py:183
  31.0 16.2 %copy-start.62 = (f32[64]{0:T(128)}, f32[64]{0:T(128)S(1)}, u32[]{:S(2)}) copy-start(f32[64]{0:T(128)S(1)} %negate_power_fusion) | copy-start | bytes 772
  42.6 34.6 %all-to-all-start.1 = ((bf16[4,64,5120]{2,1,0:T(8,128)(2,1)}), bf16[4,64,5120]{2,1,0:T(8,128)(2,1)}, u32[]{:S(2)}, u32[]{:S(2)}) async-start(bf16[4,64,5120]{2,1,0:T(8,128)(2,1)} %bitcast.497), calls=%async_computation.1 | async-start | bytes 5242880 | tf_op jit(solution)/shard_map/all_to_all | solution.py:160
  47.2 3.3 %copy-start.53 = (f32[512]{0:T(512)}, f32[512]{0:T(512)S(1)}, u32[]{:S(2)}) copy-start(f32[512]{0:T(512)S(1)} %fusion.176) | copy-start | bytes 6148
  49.0 3.4 %copy-start.8 = (f32[512,64]{1,0:T(8,128)}, f32[512,64]{1,0:T(8,128)S(1)}, u32[]{:S(2)}) copy-start(f32[512,64]{1,0:T(8,128)S(1)} %get-tuple-element.59) | copy-start | bytes 393220
  77.1 17.4 %all-to-all-start.4 = ((bf16[128,4,1024]{0,2,1:T(8,128)(2,1)}), bf16[128,4,1024]{0,2,1:T(8,128)(2,1)}, u32[]{:S(2)}, u32[]{:S(2)}) async-start(bf16[128,4,1024]{0,2,1:T(8,128)(2,1)} %bitcast.503), calls=%async_computation.4 | async-start | bytes 2097152 | tf_op jit(solution)/shard_map/all_to_all | solution.py:185
  94.6 11.3 %all-to-all-start.2 = ((bf16[128,4,256]{2,0,1:T(8,128)(2,1)}), bf16[128,4,256]{2,0,1:T(8,128)(2,1)}, u32[]{:S(2)}, u32[]{:S(2)}) async-start(bf16[128,4,256]{2,0,1:T(8,128)(2,1)} %copy.547), calls=%async_computation.2 | async-start | bytes 524288 | tf_op jit(solution)/shard_map/all_to_all | solution.py:184
  101.0 6.1 %copy-start.65 = (f32[128]{0:T(128)S(1)}, f32[128]{0:T(128)}, u32[]{:S(2)}) copy-start(f32[128]{0:T(128)} %param.15) | copy-start | bytes 1540
  103.4 4.7 %copy-start.54 = (f32[512]{0:T(512)S(1)}, f32[512]{0:T(512)}, u32[]{:S(2)}) copy-start(f32[512]{0:T(512)} %copy-done.53) | copy-start | bytes 6148
  103.4 4.7 %copy-start.63 = (f32[64]{0:T(128)S(1)}, f32[64]{0:T(128)}, u32[]{:S(2)}) copy-start(f32[64]{0:T(128)} %copy-done.62) | copy-start | bytes 772
  105.9 5.9 %copy-start.7 = (bf16[128,8,128]{2,0,1:T(8,128)(2,1)S(1)}, bf16[128,8,128]{2,0,1:T(8,128)(2,1)}, u32[]{:S(2)}) copy-start(bf16[128,8,128]{2,0,1:T(8,128)(2,1)} %get-tuple-element.40) | copy-start | bytes 786436
  105.9 5.9 %copy-start.52 = (pred[128,128]{0,1:T(8,128)(4,1)S(1)}, pred[128,128]{0,1:T(8,128)(4,1)}, u32[]{:S(2)}) copy-start(pred[128,128]{0,1:T(8,128)(4,1)} %get-tuple-element.69) | copy-start | bytes 49156
  107.0 2.4 copy-start.60
  107.0 2.4 copy-start.58
  107.1 5.1 %copy-start.36 = (bf16[1,128,1,1024]{1,3,2,0:T(8,128)(2,1)S(1)}, bf16[1,128,1,1024]{1,3,2,0:T(8,128)(2,1)}, u32[]{:S(2)}) copy-start(bf16[1,128,1,1024]{1,3,2,0:T(8,128)(2,1)} %get-tuple-element.46) | copy-start | bytes 786436
  112.1 2.0 copy-start.26
  112.1 3.0 %copy-start.70 = (f32[8,128]{1,0:T(8,128)}, f32[8,128]{1,0:T(8,128)S(1)}, u32[]{:S(2)}) copy-start(f32[8,128]{1,0:T(8,128)S(1)} %add.196) | copy-start | bytes 12292
  115.1 2.2 copy-start.5
  115.1 2.2 copy-start.51
  115.1 2.5 %copy-start.50 = (pred[128,128]{0,1:T(8,128)(4,1)S(1)}, pred[128,128]{0,1:T(8,128)(4,1)}, u32[]{:S(2)}) copy-start(pred[128,128]{0,1:T(8,128)(4,1)} %get-tuple-element.66) | copy-start | bytes 49156
  116.1 2.7 %copy-start.49 = (pred[128,128]{0,1:T(8,128)(4,1)S(1)}, pred[128,128]{0,1:T(8,128)(4,1)}, u32[]{:S(2)}) copy-start(pred[128,128]{0,1:T(8,128)(4,1)} %get-tuple-element.74) | copy-start | bytes 49156
  117.0 2.2 copy-start.38
  125.0 21.7 %copy-start.20 = (bf16[8,128,128]{1,2,0:T(8,128)(2,1)}, bf16[8,128,128]{1,2,0:T(8,128)(2,1)S(1)}, u32[]{:S(2)}) copy-start(bf16[8,128,128]{1,2,0:T(8,128)(2,1)S(1)} %fusion.72) | copy-start | bytes 786436
  125.0 2.2 copy-start.48
  125.0 2.5 %copy-start.47 = (pred[128,128]{0,1:T(8,128)(4,1)S(1)}, pred[128,128]{0,1:T(8,128)(4,1)}, u32[]{:S(2)}) copy-start(pred[128,128]{0,1:T(8,128)(4,1)} %get-tuple-element.70) | copy-start | bytes 49156
  127.0 2.2 copy-start.45
  127.3 2.2 copy-start.39
  136.4 7.2 %copy-start.24 = (bf16[8,128,128]{1,2,0:T(8,128)(2,1)}, bf16[8,128,128]{1,2,0:T(8,128)(2,1)S(1)}, u32[]{:S(2)}) copy-start(bf16[8,128,128]{1,2,0:T(8,128)(2,1)S(1)} %fusion.73) | copy-start | bytes 786436
  137.4 5.9 %copy-start.22 = (bf16[8,128,128]{1,2,0:T(8,128)(2,1)}, bf16[8,128,128]{1,2,0:T(8,128)(2,1)S(1)}, u32[]{:S(2)}) copy-start(bf16[8,128,128]{1,2,0:T(8,128)(2,1)S(1)} %fusion.71) | copy-start | bytes 786436
  138.5 4.1 %copy-start.19 = (bf16[8,128,128]{1,2,0:T(8,128)(2,1)}, bf16[8,128,128]{1,2,0:T(8,128)(2,1)S(1)}, u32[]{:S(2)}) copy-start(bf16[8,128,128]{1,2,0:T(8,128)(2,1)S(1)} %fusion.70) | copy-start | bytes 786436
  139.5 3.0 %copy-start.17 = (bf16[8,128,128]{1,2,0:T(8,128)(2,1)}, bf16[8,128,128]{1,2,0:T(8,128)(2,1)S(1)}, u32[]{:S(2)}) copy-start(bf16[8,128,128]{1,2,0:T(8,128)(2,1)S(1)} %fusion.76) | copy-start | bytes 786436
  140.3 3.5 %copy-start.3 = (bf16[512,8,64]{2,0,1:T(8,128)(2,1)S(1)}, bf16[512,8,64]{2,0,1:T(8,128)(2,1)}, u32[]{:S(2)}) copy-start(bf16[512,8,64]{2,0,1:T(8,128)(2,1)} %copy-done.2) | copy-start | bytes 1572868
  140.3 3.5 %copy-start.44 = (pred[128,128]{0,1:T(8,128)(4,1)S(1)}, pred[128,128]{0,1:T(8,128)(4,1)}, u32[]{:S(2)}) copy-start(pred[128,128]{0,1:T(8,128)(4,1)} %get-tuple-element.65) | copy-start | bytes 49156
  150.5 2.1 copy-start.33
  150.5 2.1 copy-start.34
  150.5 2.1 copy-start.40
  152.2 2.0 copy-start.15
  152.2 3.1 %copy-start.61 = (f32[512]{0:T(512)S(1)}, f32[512]{0:T(512)}, u32[]{:S(2)}) copy-start(f32[512]{0:T(512)} %copy-done.60) | copy-start | bytes 6148
  152.2 3.1 %copy-start.59 = (f32[512]{0:T(512)S(1)}, f32[512]{0:T(512)}, u32[]{:S(2)}) copy-start(f32[512]{0:T(512)} %copy-done.58) | copy-start | bytes 6148
  152.6 3.9 %copy-start.27 = (f32[8,128,128]{1,2,0:T(8,128)S(1)}, f32[8,128,128]{1,2,0:T(8,128)}, u32[]{:S(2)}) copy-start(f32[8,128,128]{1,2,0:T(8,128)} %copy-done.26) | copy-start | bytes 1572868
  152.6 3.9 %copy-start.37 = (bf16[1,128,1,1024]{1,3,2,0:T(8,128)(2,1)S(1)}, bf16[1,128,1,1024]{1,3,2,0:T(8,128)(2,1)}, u32[]{:S(2)}) copy-start(bf16[1,128,1,1024]{1,3,2,0:T(8,128)(2,1)} %get-tuple-element.46) | copy-start | bytes 786436
  152.6 3.9 %copy-start.71 = (f32[8,128]{1,0:T(8,128)S(1)}, f32[8,128]{1,0:T(8,128)}, u32[]{:S(2)}) copy-start(f32[8,128]{1,0:T(8,128)} %copy-done.70) | copy-start | bytes 12292
  152.6 3.9 %copy-start.75 = (f32[128,128]{1,0:T(8,128)S(1)}, f32[128,128]{1,0:T(8,128)}, u32[]{:S(2)}) copy-start(f32[128,128]{1,0:T(8,128)} %convolution_bitcast_fusion.14) | copy-start | bytes 196612
  152.6 3.9 %copy-start.76 = (f32[128,128]{1,0:T(8,128)S(1)}, f32[128,128]{1,0:T(8,128)}, u32[]{:S(2)}) copy-start(f32[128,128]{1,0:T(8,128)} %convolution_bitcast_fusion.13) | copy-start | bytes 196612
  152.9 4.0 %copy-start.29 = (f32[8,128,128]{1,2,0:T(8,128)S(1)}, f32[8,128,128]{1,2,0:T(8,128)}, u32[]{:S(2)}) copy-start(f32[8,128,128]{1,2,0:T(8,128)} %get-tuple-element.95) | copy-start | bytes 1572868
  152.9 4.0 %copy-start.35 = (bf16[1,128,1,1024]{1,3,2,0:T(8,128)(2,1)S(1)}, bf16[1,128,1,1024]{1,3,2,0:T(8,128)(2,1)}, u32[]{:S(2)}) copy-start(bf16[1,128,1,1024]{1,3,2,0:T(8,128)(2,1)} %get-tuple-element.43) | copy-start | bytes 786436
  152.9 4.0 %copy-start.69 = (f32[8,128]{1,0:T(8,128)S(1)}, f32[8,128]{1,0:T(8,128)}, u32[]{:S(2)}) copy-start(f32[8,128]{1,0:T(8,128)} %get-tuple-element.48) | copy-start | bytes 12292
  152.9 4.0 %copy-start.72 = (f32[128,128]{1,0:T(8,128)S(1)}, f32[128,128]{1,0:T(8,128)}, u32[]{:S(2)}) copy-start(f32[128,128]{1,0:T(8,128)} %convolution_bitcast_fusion.18) | copy-start | bytes 196612
  152.9 4.0 %copy-start.73 = (f32[128,128]{1,0:T(8,128)S(1)}, f32[128,128]{1,0:T(8,128)}, u32[]{:S(2)}) copy-start(f32[128,128]{1,0:T(8,128)} %convolution_bitcast_fusion.17) | copy-start | bytes 196612
  152.9 4.0 %copy-start.74 = (f32[128,128]{1,0:T(8,128)S(1)}, f32[128,128]{1,0:T(8,128)}, u32[]{:S(2)}) copy-start(f32[128,128]{1,0:T(8,128)} %convolution_bitcast_fusion.16) | copy-start | bytes 196612
  156.9 6.7 %copy-start.12 = (f32[128,8,128]{0,2,1:T(8,128)S(1)}, f32[128,8,128]{0,2,1:T(8,128)}, u32[]{:S(2)}) copy-start(f32[128,8,128]{0,2,1:T(8,128)} %convolution_add_fusion.4) | copy-start | bytes 1572868
  156.9 6.7 %copy-start.21 = (bf16[8,128,128]{1,2,0:T(8,128)(2,1)S(1)}, bf16[8,128,128]{1,2,0:T(8,128)(2,1)}, u32[]{:S(2)}) copy-start(bf16[8,128,128]{1,2,0:T(8,128)(2,1)} %copy-done.20) | copy-start | bytes 786436
  159.6 9.3 %all-to-all-start.5 = ((bf16[4,2,16384]{2,1,0:T(2,128)(2,1)}), bf16[4,2,16384]{2,1,0:T(2,128)(2,1)S(1)}, u32[]{:S(2)}, u32[]{:S(2)}) async-start(bf16[4,2,16384]{2,1,0:T(2,128)(2,1)} %reshape.736), calls=%async_computation.5 | async-start | bytes 524288 | tf_op jit(solution)/shard_map/all_to_all | solution.py:212
  169.6 24.9 %all-to-all-start.7 = ((bf16[128,8,4,160]{0,3,1,2:T(8,128)(2,1)}), bf16[128,8,4,160]{0,3,1,2:T(8,128)(2,1)S(1)}, u32[]{:S(2)}, u32[]{:S(2)}) async-start(bf16[128,8,4,160]{0,3,1,2:T(8,128)(2,1)} %copy.611), calls=%async_computation.7 | async-start | bytes 2621440 | tf_op jit(solution)/shard_map/all_to_all | solution.py:233
  173.4 57.9 %reduce-scatter.2.cloned.1.call-start = ((), (), s32[]{:S(2)}) async-start(), calls=%async_computation.9 | async-start | bytes 1474560 | tf_op jit(solution)/shard_map/reduce_scatter | solution.py:244
  173.4 2.5 %copy-start.23 = (bf16[8,128,128]{1,2,0:T(8,128)(2,1)S(1)}, bf16[8,128,128]{1,2,0:T(8,128)(2,1)}, u32[]{:S(2)}) copy-start(bf16[8,128,128]{1,2,0:T(8,128)(2,1)} %copy-done.22) | copy-start | bytes 786436
  195.6 2.0 copy-start.16
  208.0 5.5 %copy-start.28 = (bf16[128,4,128]{2,0,1:T(8,128)(2,1)S(1)}, bf16[128,4,128]{2,0,1:T(8,128)(2,1)}, u32[]{:S(2)}) copy-start(bf16[128,4,128]{2,0,1:T(8,128)(2,1)} %get-tuple-element.53) | copy-start | bytes 393220
  208.0 6.5 %copy-start.14 = (bf16[128,4,128]{0,2,1:T(8,128)(2,1)S(1)}, bf16[128,4,128]{0,2,1:T(8,128)(2,1)}, u32[]{:S(2)}) copy-start(bf16[128,4,128]{0,2,1:T(8,128)(2,1)} %copy.593) | copy-start | bytes 393220
  210.0 14.1 %all-to-all-start.6 = ((bf16[4,2,65536]{2,1,0:T(2,128)(2,1)}), bf16[4,2,65536]{2,1,0:T(2,128)(2,1)S(1)}, u32[]{:S(2)}, u32[]{:S(2)}) async-start(bf16[4,2,65536]{2,1,0:T(2,128)(2,1)} %reshape.738), calls=%async_computation.6 | async-start | bytes 2097152 | tf_op jit(solution)/shard_map/all_to_all | solution.py:211
  225.5 7.5 %copy-start.1 = (bf16[1,128,5120]{2,1,0:T(8,128)(2,1)S(1)}, bf16[1,128,5120]{2,1,0:T(8,128)(2,1)}, u32[]{:S(2)}) copy-start(bf16[1,128,5120]{2,1,0:T(8,128)(2,1)} %param.9) | copy-start | bytes 3932164
  (22 other events, 25.4 us)
Sparse Core Ops, SparseCore 0:
  197.7 33.5 reduce-scatter.1
where the time goes:
time: 243 us; the launch traced here: 240 us
  matrix products  64.3 us (26%)
  waiting for transfers between devices  39.7 us (16%)
  local copies, waits for them, and re-layouts  38.9 us (16%)
  starting transfers between devices  33 us (14%)
  other arithmetic  27.8 us (11%)
  blocking collectives  20.6 us (8%)
  between operations  15.6 us (6%)
    all_to_all x1, waiting for transfers between devices, on_device(): lax.all_to_all(outgoing, 'ctx', split_axis=0, concat_axis=0, tiled=True)  21.4 us
    unnamed x165, local copies, waits for them, and re-layouts  16.3 us
    all_gather x1, blocking collectives, on_device(): lax.all_gather(value_grad, 'ctx', axis=0, tiled=True)  12.1 us
    dot_general x10, matrix products, attention(): jnp.einsum('qhd,kd->hqk', g_tile, tile(v_heads, j), preferred_element_typ...  10.7 us
    dot_general x9, matrix products, attention(): jnp.einsum('hqk,kd->hqd', exponent.astype(jnp.bfloat16), tile(v_heads, j)...  9.31 us
    dot_general x10, matrix products, attention(): jnp.einsum('hqk,kd->qhd', dlogit, tile(k_normed, j), preferred_element_ty...  8.94 us
    all_gather x1, blocking collectives, on_device(): slab_docs = lax.all_gather(doc_ids[0], 'ctx', axis=0, tiled=True)  8.49 us
    dot_general x10, matrix products, attention(): jnp.einsum('hqk,qhd->kd', probability.astype(jnp.bfloat16), g_tile, prefe...  6.76 us
  transfers between devices with their start and end apart: 9, of which 6 were waited for; matrix products, arithmetic and copies ran while one was open for 28% of the time, Pallas kernels for 0%

commit v1 on v0

v1 whole, which is shorter than its diff:
```python
import functools
import math

import jax
import jax.numpy as jnp
import numpy as np
from jax import lax
from jax.experimental import pallas as pl
from jax.experimental.pallas import tpu as pltpu
from jax.sharding import PartitionSpec as P

epsilon = 1e-06
rope_base = 1000000.0
meta_rows = 16
masked = -1e30
VMEM = pltpu.VMEM
f32, bf16 = jnp.float32, jnp.bfloat16
NT = (((1,), (1,)), ((), ()))


def params(mib=48):
    return pltpu.CompilerParams(vmem_limit_bytes=mib << 20)


def cost(flops, bytes_accessed):
    return pl.CostEstimate(flops=int(flops), bytes_accessed=int(bytes_accessed), transcendentals=0)


def rope_constants(rows, blocks, head_width):
    half = head_width // 2
    frequency = rope_base ** (-(np.arange(half) * 2.0 / head_width))
    frequency = np.concatenate([frequency, frequency])
    sign = np.concatenate([-np.ones(half), np.ones(half)])

    def table(positions):
        angles = positions[:, None] * frequency[None, :]
        return np.stack([np.cos(angles), np.sin(angles) * sign]).astype(np.float32)

    return table(np.arange(rows)), table(np.arange(blocks) * rows)


def rotation(rows_ref, base_ref, me):
    cos_b = base_ref[0, pl.ds(me, 1), :]
    sin_b = base_ref[1, pl.ds(me, 1), :]
    cos_r, sin_r = rows_ref[0], rows_ref[1]
    return cos_b * cos_r - sin_b * sin_r, sin_b * cos_r + cos_b * sin_r


def swap_halves(x):
    return pltpu.roll(x, x.shape[-1] // 2, 1)


def norm_rope(u, gain, cosine, sine):
    inverse = lax.rsqrt(jnp.mean(u * u, axis=-1, keepdims=True) + epsilon)
    y = u * inverse * gain
    return y * cosine + swap_halves(y) * sine


def norm_rope_back(u, dz, gain, cosine, sine):
    inverse = lax.rsqrt(jnp.mean(u * u, axis=-1, keepdims=True) + epsilon)
    dn = (dz * cosine + swap_halves(dz * sine)) * gain
    along = jnp.mean(dn * u, axis=-1, keepdims=True) * (inverse * inverse)
    return inverse * (dn - u * along)


def key_message_kernel(k_ref, doc_ref, gain_ref, rows_ref, base_ref, out_ref):
    me = lax.axis_index("ctx")
    rows, width = k_ref.shape
    hd = gain_ref.shape[1]
    cosine, sine = rotation(rows_ref, base_ref, me)
    gain = gain_ref[...]
    marks = jnp.broadcast_to((doc_ref[...] + 1).astype(f32), (meta_rows, rows)).astype(bf16)
    for h in range(width // hd):
        cols = slice(h * hd, (h + 1) * hd)
        u = k_ref[:, cols].astype(f32)
        out_ref[:rows, cols] = norm_rope(u, gain, cosine, sine).astype(bf16)
        out_ref[rows:, cols] = marks


def query_prep_kernel(scale, q_ref, gain_ref, rows_ref, base_ref, out_ref):
    me = lax.axis_index("ctx")
    rows, width = q_ref.shape
    hd = gain_ref.shape[1]
    cosine, sine = rotation(rows_ref, base_ref, me)
    gain = gain_ref[...] * scale
    for h in range(width // hd):
        u = q_ref[:, h * hd : (h + 1) * hd].astype(f32)
        out_ref[0, h * rows : (h + 1) * rows] = norm_rope(u, gain, cosine, sine).astype(bf16)


def value_message_kernel(blocks, h_ref, w_ref, dest_ref, out_ref, acc_ref):
    step = pl.program_id(0)
    rows, width = acc_ref.shape
    part = jnp.dot(h_ref[...], w_ref[...], preferred_element_type=f32)

    @pl.when(step == 0)
    def _():
        acc_ref[...] = part

    @pl.when(step > 0)
    def _():
        acc_ref[...] += part

    @pl.when(step == pl.num_programs(0) - 1)
    def _():
        out_ref[:rows] = acc_ref[...].astype(bf16)
        dest = jnp.broadcast_to(dest_ref[...], (meta_rows, rows))
        block = jnp.zeros_like(dest)
        for j in range(1, blocks):
            block = block + (dest >= j * rows).astype(jnp.int32)
        which = lax.broadcasted_iota(jnp.int32, dest.shape, 0)
        marks = jnp.where(which == 0, block, dest - block * rows).astype(f32).astype(bf16)
        for c in range(width // rows):
            out_ref[rows:, c * rows : (c + 1) * rows] = marks


def share_index(j, half, c, z, core, zs, blocks):
    owner_core = core if half else 1 - core
    return (lax.rem(z + j, zs) * 2 + owner_core) * blocks + c


def feature_kernel(blocks, zs, h_ref, *refs):
    outs, turned = refs[:-1], refs[-1]
    me, dp = lax.axis_index("ctx"), lax.axis_index("dp")
    z, core = dp // 2, dp % 2
    rows, width = h_ref.shape
    share = width // (blocks * zs * 2)
    for c in range(width // 128):
        turned[c * 128 : (c + 1) * 128] = h_ref[:, c * 128 : (c + 1) * 128].T
    for m in range(blocks):
        c = lax.rem(me + m, blocks)
        for half in range(2):
            for j in range(zs):
                start = share_index(j, half, c, z, core, zs, blocks) * share
                start = pl.multiple_of(start, 16)
                at = (half * zs + j) * share
                outs[m][at : at + share] = turned[pl.ds(start, share)]


def mark_rows(ref, rows):
    return ref[rows : rows + meta_rows, :rows].astype(f32)


def attend_kernel(back, qs_ref, g_ref, *refs):
    k_refs = refs[: back + 1]
    p_ref, own_ref = refs[back + 1], refs[back + 2]
    send_refs = refs[back + 3 : 2 * back + 3]
    bias_ref = refs[-1]
    rows = g_ref.shape[0]
    hd = own_ref.shape[1]
    group = g_ref.shape[1] // hd

    @pl.when(pl.program_id(0) == 0)
    def _():
        query_doc = mark_rows(k_refs[0], rows)[:1]
        for b in range(back + 1):
            key_doc = jnp.broadcast_to(mark_rows(k_refs[b], rows)[:1], (rows, rows)).T
            allowed = key_doc == query_doc
            if b == 0:
                key_row = lax.broadcasted_iota(jnp.int32, (rows, rows), 0)
                query_row = lax.broadcasted_iota(jnp.int32, (rows, rows), 1)
                allowed = allowed & (key_row <= query_row)
            bias_ref[b * rows : (b + 1) * rows] = jnp.where(allowed, 0.0, masked)

    keys = jnp.concatenate([r[:rows] for r in k_refs], axis=0)
    logits = lax.dot_general(keys, qs_ref[0], NT, preferred_element_type=f32)
    e = jnp.exp2(logits + jnp.concatenate([bias_ref[...]] * group, axis=1))
    p = (e * (1.0 / jnp.sum(e, axis=0, keepdims=True))).astype(bf16)
    p_ref[0] = p
    g = jnp.concatenate([g_ref[:, j * hd : (j + 1) * hd] for j in range(group)], axis=0)
    gv = jnp.dot(p, g, preferred_element_type=f32)
    own_ref[...] = gv[:rows]
    for b in range(back):
        send_refs[b][...] = gv[(b + 1) * rows : (b + 2) * rows].astype(bf16)


def backward_kernel(back, blocks, factor, p_ref, g_ref, q_ref, qs_ref, gain_ref, rows_ref, base_ref, *refs):
    k_refs, refs = refs[: back + 1], refs[back + 1 :]
    v_refs, refs = refs[:blocks], refs[blocks:]
    gq_ref, own_ref, send_refs, place_ref = refs[0], refs[1], refs[2:-1], refs[-1]
    me = lax.axis_index("ctx")
    rows = g_ref.shape[0]
    hd = own_ref.shape[1]
    group = g_ref.shape[1] // hd
    key_count = (back + 1) * rows

    @pl.when(pl.program_id(0) == 0)
    def _():
        slot = lax.broadcasted_iota(jnp.int32, (key_count, rows), 0).astype(f32)
        for s in range(blocks):
            marks = mark_rows(v_refs[s], rows)
            away = me.astype(f32) - marks[:1]
            away = jnp.where(away < 0, away + blocks, away)
            place_ref[:, s * rows : (s + 1) * rows] = (
                (slot == away * rows + marks[1:2]).astype(f32).astype(bf16)
            )

    arrived = jnp.concatenate([r[:rows] for r in v_refs], axis=0)
    values = jnp.dot(place_ref[...], arrived, preferred_element_type=f32).astype(bf16)
    g = jnp.concatenate([g_ref[:, j * hd : (j + 1) * hd] for j in range(group)], axis=0)
    dp = lax.dot_general(values, g, NT, preferred_element_type=f32)
    p = p_ref[0].astype(f32)
    delta = jnp.sum(p * dp, axis=0, keepdims=True)
    ds = (p * (dp - delta)).astype(bf16)
    gk = jnp.dot(ds, qs_ref[0], preferred_element_type=f32) * math.log(2.0)
    own_ref[...] = gk[:rows]
    for b in range(back):
        send_refs[b][...] = gk[(b + 1) * rows : (b + 2) * rows].astype(bf16)
    keys = jnp.concatenate([r[:rows] for r in k_refs], axis=0)
    gq = jnp.dot(keys.T, ds, preferred_element_type=f32)
    cosine, sine = rotation(rows_ref, base_ref, me)
    gain = gain_ref[...] * factor
    for j in range(group):
        dz = gq[:, j * rows : (j + 1) * rows].T
        u = q_ref[:, j * hd : (j + 1) * hd].astype(f32)
        gq_ref[:, j * hd : (j + 1) * hd] = norm_rope_back(u, dz, gain, cosine, sine).astype(bf16)


def key_back_kernel(k_ref, own_ref, gain_ref, rows_ref, base_ref, *refs):
    got_refs, out_ref = refs[:-1], refs[-1]
    me = lax.axis_index("ctx")
    hd = gain_ref.shape[1]
    cosine, sine = rotation(rows_ref, base_ref, me)
    total = own_ref[...]
    for r in got_refs:
        total = total + r[...].astype(f32)
    for h in range(k_ref.shape[1] // hd):
        cols = slice(h * hd, (h + 1) * hd)
        u = k_ref[:, cols].astype(f32)
        out_ref[:, cols] = norm_rope_back(u, total[:, cols], gain_ref[...], cosine, sine).astype(bf16)


def hidden_grad_kernel(v_ref, w_ref, out_ref):
    out_ref[...] = lax.dot_general(
        v_ref[...], w_ref[...], NT, preferred_element_type=f32
    ).astype(bf16)


def weight_kernel(blocks, *refs):
    h_refs, v_refs, m_refs = refs[:blocks], refs[blocks : 2 * blocks], refs[2 * blocks : 3 * blocks]
    sibling_ref, own_ref = refs[3 * blocks :]
    me = lax.axis_index("ctx")
    rows = h_refs[0].shape[1]
    slab = jnp.concatenate([r[...] for r in v_refs], axis=0)
    slot = lax.broadcasted_iota(jnp.int32, (blocks * rows, rows), 0).astype(f32)
    arrival = []
    for s in range(blocks):
        marks = mark_rows(m_refs[s], rows)
        away = me.astype(f32) - marks[:1]
        away = jnp.where(away < 0, away + blocks, away)
        place = (slot == away * rows + marks[1:2]).astype(f32).T.astype(bf16)
        arrival.append(jnp.dot(place, slab, preferred_element_type=f32).astype(bf16))
    arrival = jnp.concatenate(arrival, axis=0)
    half = sibling_ref.shape[0]
    features = jnp.concatenate([r[...] for r in h_refs], axis=1)
    sibling_ref[...] = jnp.dot(features[:half], arrival, preferred_element_type=f32).astype(bf16)
    own_ref[...] = jnp.dot(features[half:], arrival, preferred_element_type=f32)


def on_device(hidden, queries, key_states, out_grad, w_value, q_gain, k_gain, dest_rows, doc_ids):
    hidden, queries, key_states, out_grad = hidden[0], queries[0], key_states[0], out_grad[0]
    rows, width = hidden.shape
    hd = q_gain.shape[0]
    kv_width = key_states.shape[1]
    q_width = queries.shape[1]
    kv = kv_width // hd
    group = q_width // kv_width
    blocks, dp_count = lax.axis_size("ctx"), lax.axis_size("dp")
    zs = dp_count // 2
    back = blocks // 2
    factor = hd ** (-0.5)
    share = width // (blocks * dp_count)
    spread = group * rows
    key_count = (back + 1) * rows
    message = jax.ShapeDtypeStruct((rows + meta_rows, kv_width), bf16)
    rows_table, base_table = (jnp.asarray(t) for t in rope_constants(rows, blocks, hd))
    q_gain, k_gain = q_gain[None], k_gain[None]

    def ahead(array, m):
        return lax.ppermute(array, "ctx", [(i, i + m) for i in range(blocks - m)])

    def behind(array, m):
        return lax.ppermute(array, "ctx", [(i + m, i) for i in range(blocks - m)])

    def around(array, m):
        return lax.ppermute(array, "ctx", [(i, (i + m) % blocks) for i in range(blocks)])

    def call(kernel, out_shape, name, flops=0, nbytes=0, **kw):
        return pl.pallas_call(
            kernel, out_shape=out_shape, name=name, compiler_params=params(),
            cost_estimate=cost(flops, nbytes), **kw,
        )

    def whole(shape):
        return pl.BlockSpec(shape, lambda h: (0,) * len(shape))

    key_own = call(key_message_kernel, message, "key_message", 0, 1e6)(
        key_states, doc_ids, k_gain, rows_table, base_table
    )
    key_messages = [key_own] + [ahead(key_own, m) for m in range(1, back + 1)]

    head_cols = pl.BlockSpec((rows, group * hd), lambda h: (0, h))
    head_set = pl.BlockSpec((1, spread, hd), lambda h: (h, 0, 0))
    message_cols = pl.BlockSpec((rows + meta_rows, hd), lambda h: (0, h))
    row_cols = pl.BlockSpec((rows, hd), lambda h: (0, h))
    tables = [whole((1, hd)), whole(rows_table.shape), whole(base_table.shape)]

    q_scaled = call(
        functools.partial(query_prep_kernel, factor * math.log2(math.e)),
        jax.ShapeDtypeStruct((kv, spread, hd), bf16),
        "query_prep", 0, 4e6, grid=(kv,), in_specs=[head_cols] + tables, out_specs=head_set,
    )(queries, q_gain, rows_table, base_table)

    depth = width // 4
    value_own = call(
        functools.partial(value_message_kernel, blocks),
        message, "value_message", 2 * rows * width * kv_width, 7e6, grid=(width // depth,),
        in_specs=[
            pl.BlockSpec((rows, depth), lambda i: (0, i)),
            pl.BlockSpec((depth, kv_width), lambda i: (i, 0)),
            whole((1, rows)),
        ],
        out_specs=whole((rows + meta_rows, kv_width)),
        scratch_shapes=[VMEM((rows, kv_width), f32)],
    )(hidden, w_value, dest_rows)
    value_messages = [value_own] + [around(value_own, m) for m in range(1, blocks)]

    if share % 16 == 0:
        features = call(
            functools.partial(feature_kernel, blocks, zs),
            [jax.ShapeDtypeStruct((width // blocks, rows), bf16)] * blocks,
            "features", 0, 6e6, scratch_shapes=[VMEM((width, rows), bf16)],
        )(hidden)
    else:
        me, dp = lax.axis_index("ctx"), lax.axis_index("dp")
        turned = hidden.T.reshape(dp_count * blocks, share, rows)
        features = []
        for m in range(blocks):
            places = [
                share_index(j, half, lax.rem(me + m, blocks), dp // 2, dp % 2, zs, blocks)
                for half in range(2)
                for j in range(zs)
            ]
            pieces = [lax.dynamic_index_in_dim(turned, place, axis=0) for place in places]
            features.append(jnp.concatenate(pieces, axis=0).reshape(width // blocks, rows))
    features = [features[0]] + [around(features[m], m) for m in range(1, blocks)]

    attended = call(
        functools.partial(attend_kernel, back),
        [
            jax.ShapeDtypeStruct((kv, key_count, spread), bf16),
            jax.ShapeDtypeStruct((rows, kv_width), f32),
        ]
        + [jax.ShapeDtypeStruct((rows, kv_width), bf16)] * back,
        "attend", 8 * kv * key_count * spread * hd, 5e6, grid=(kv,),
        in_specs=[head_set, head_cols] + [message_cols] * (back + 1),
        out_specs=[pl.BlockSpec((1, key_count, spread), lambda h: (h, 0, 0))]
        + [row_cols] * (back + 1),
        scratch_shapes=[VMEM((key_count, rows), f32)],
    )(q_scaled, out_grad, *key_messages)
    probabilities, value_total = attended[0], attended[1]
    for m in range(1, back + 1):
        value_total = value_total + behind(attended[1 + m], m).astype(f32)
    value_grad = value_total.astype(bf16)
    value_grads = [value_grad] + [around(value_grad, m) for m in range(1, blocks)]

    backed = call(
        functools.partial(backward_kernel, back, blocks, factor),
        [
            jax.ShapeDtypeStruct((rows, q_width), bf16),
            jax.ShapeDtypeStruct((rows, kv_width), f32),
        ]
        + [jax.ShapeDtypeStruct((rows, kv_width), bf16)] * back,
        "backward", 12 * kv * key_count * spread * hd, 7e6, grid=(kv,),
        in_specs=[
            pl.BlockSpec((1, key_count, spread), lambda h: (h, 0, 0)),
            head_cols, head_cols, head_set,
        ]
        + tables + [message_cols] * (back + 1 + blocks),
        out_specs=[head_cols] + [row_cols] * (back + 1),
        scratch_shapes=[VMEM((key_count, blocks * rows), bf16)],
    )(
        probabilities, out_grad, queries, q_scaled, q_gain, rows_table, base_table,
        *key_messages, *value_messages,
    )
    query_grad = backed[0]
    key_got = [behind(backed[1 + m], m) for m in range(1, back + 1)]
    key_grad = call(
        key_back_kernel, jax.ShapeDtypeStruct((rows, kv_width), bf16), "key_back", 0, 1e6
    )(key_states, backed[1], k_gain, rows_table, base_table, *key_got)

    slice_width = width // 4
    hidden_grad = call(
        hidden_grad_kernel, jax.ShapeDtypeStruct((rows, width), bf16),
        "hidden_grad", 2 * rows * width * kv_width, 7e6, grid=(width // slice_width,),
        in_specs=[whole((rows, kv_width)), pl.BlockSpec((slice_width, kv_width), lambda i: (i, 0))],
        out_specs=pl.BlockSpec((rows, slice_width), lambda i: (0, i)),
    )(value_grad, w_value)

    half = width // blocks // 2
    sibling, own = call(
        functools.partial(weight_kernel, blocks),
        [jax.ShapeDtypeStruct((half, kv_width), bf16), jax.ShapeDtypeStruct((half, kv_width), f32)],
        "weight", 2 * width * rows * kv_width, 4e6,
    )(*features, *value_grads, *value_messages)
    got = lax.ppermute(sibling, "dp", [(d, d ^ 1) for d in range(dp_count)])
    pair = own.reshape(zs, share, kv_width) + got.astype(f32).reshape(zs, share, kv_width)
    total = pair[0]
    for j in range(1, zs):
        route = [(z * 2 + c, (z + j) % zs * 2 + c) for z in range(zs) for c in range(2)]
        total = total + lax.ppermute(pair[j].astype(bf16), "dp", route).astype(f32)
    weight_grad = total * (1.0 / (blocks * dp_count))
    return (hidden_grad[None], query_grad[None], key_grad[None], weight_grad)


def solution(mesh):
    return jax.shard_map(
        on_device,
        mesh=mesh,
        in_specs=(
            P("dp", "ctx", None),
            P("dp", "ctx", None),
            P("dp", "ctx", None),
            P("dp", "ctx", None),
            P(),
            P(),
            P(),
            P("dp", "ctx"),
            P("dp", "ctx"),
        ),
        out_specs=(
            P("dp", "ctx", None),
            P("dp", "ctx", None),
            P("dp", "ctx", None),
            P(("dp", "ctx"), None),
        ),
        check_vma=False,
    )
```

time: 243 us -> 99.8 us (0.41)
  the two profiles are of different devices: /device:TPU:0 before, /device:TPU:20 now
where the time goes in v1:
time: 99.8 us; the launch traced here: 99.4 us
  starting transfers between devices  30.4 us (30%)
  Pallas kernels  30 us (30%)
  waiting for transfers between devices  29.4 us (29%)
  local copies, waits for them, and re-layouts  7.48 us (7%)
  other arithmetic  1.11 us (1%)
    ppermute x9, waiting for transfers between devices, around(): lax.ppermute(array, 'ctx', [(i, (i + m) % blocks) for i in range(blocks)])  18.7 us
    ppermute x4, starting transfers between devices, behind(): return lax.ppermute(array, 'ctx', [(i + m, i) for i in range(blocks - m)])  14.5 us
    pallas_call x1, Pallas kernels, on_device(): call(functools.partial(backward_kernel, back, blocks, factor), [jax.Shape...  12.6 us
    ppermute x3, waiting for transfers between devices, on_device(): total = total + lax.ppermute(pair[j].astype(bf16), 'dp', route).astype(f32)  9.78 us
    unnamed x36, local copies, waits for them, and re-layouts  7.45 us
    ppermute x9, starting transfers between devices, around(): lax.ppermute(array, 'ctx', [(i, (i + m) % blocks) for i in range(blocks)])  7.14 us
    ppermute x2, starting transfers between devices, ahead(): return lax.ppermute(array, 'ctx', [(i, i + m) for i in range(blocks - m)])  4.69 us
    pallas_call x1, Pallas kernels, on_device(): call(functools.partial(value_message_kernel, blocks), message, 'value_mes...  4.04 us
  transfers between devices with their start and end apart: 19, of which 10 were waited for; matrix products, arithmetic and copies ran while one was open for 0% of the time, Pallas kernels for 29%

profile of v1, /device:TPU:20, one launch (start us, length us, event | category | flops | bytes accessed | tf_op | source)
XLA Modules:
  0.0 99.4 jit_solution(4993327859574489389)
XLA Ops:
  0.6 0.0 copy-start.2
  0.6 0.9 copy-done.2
  1.5 0.9 copy-done.5
  2.4 0.7 copy-done.7
  3.1 0.7 copy-done.9
  3.8 0.7 copy-done.11
  4.4 0.3 key_message.1.refs_0_
  4.8 3.4 %collective-permute-start = (bf16[144,512]{1,0:T(8,128)(2,1)S(1)}, bf16[144,512]{1,0:T(8,128)(2,1)S(1)}, u32[]{:S(2)}, u32[]{:S(2)}) collective-permute-start(bf16[144,512]{1,0:T(8,128)(2,1)S(1)} %key_message.1.refs_0_), channel_id=1, source_target_pairs={{0,1},{1,2},{2,3},{4,5},{5,6},{6,7},{8,9},{9,10},{10,11},{12,13},{... | collective-permute-start | bytes 442376 | tf_op jit(solution)/shard_map/ppermute | solution.py:280
  8.2 1.3 %collective-permute-start.1 = (bf16[144,512]{1,0:T(8,128)(2,1)S(1)}, bf16[144,512]{1,0:T(8,128)(2,1)S(1)}, u32[]{:S(2)}, u32[]{:S(2)}) collective-permute-start(bf16[144,512]{1,0:T(8,128)(2,1)S(1)} %key_message.1.refs_0_), channel_id=1, source_target_pairs={{0,2},{1,3},{4,6},{5,7},{8,10},{9,11},{12,14},{13,15},{16,18},{17,... | collective-permute-start | bytes 442376 | tf_op jit(solution)/shard_map/ppermute | solution.py:280
  9.5 0.0 copy-start
  9.5 1.3 %copy-done = bf16[1,128,5120]{2,1,0:T(8,128)(2,1)S(1)} copy-done((bf16[1,128,5120]{2,1,0:T(8,128)(2,1)S(1)}, bf16[1,128,5120]{2,1,0:T(8,128)(2,1)}, u32[]{:S(2)}) %copy-start) | copy-done | bytes 1310744
  10.8 0.7 copy-done.13
  11.5 4.0 %value_message.1.refs_3_.refs_8_ = bf16[144,512]{1,0:T(8,128)(2,1)S(1)} custom-call(bf16[128,5120]{1,0:T(8,128)(2,1)S(1)} %bitcast.11, bf16[5120,512]{1,0:T(8,128)(2,1)} %w_ref.3, s32[1,128]{1,0:T(1,128)S(1)} %copy-done.13), custom_call_target="tpu_custom_call" | custom-call | flops 671088640 | bytes 7000000 | tf_op jit(solution)/shard_map/value_message/pallas_call | solution.py:315
  15.5 0.0 copy-start.14
  15.5 0.1 collective-permute-start.4
  15.6 3.4 %query_prep.1.qs_ref = bf16[4,1024,128]{2,1,0:T(8,128)(2,1)S(1)} custom-call(bf16[128,4096]{1,0:T(8,128)(2,1)S(1)} %bitcast.13, f32[1,128]{1,0:T(1,128)S(1)} %bitcast.19, f32[2,128,128]{2,1,0:T(8,128)S(1)} %copy-done.3, f32[2,4,128]{2,1,0:T(4,128)S(1)} %copy-done.8), custom_call_target="tpu_custom_call" | custom-call | bytes 4000000 | tf_op jit(solution)/shard_map/query_prep/pallas_call | solution.py:308
  19.1 0.0 collective-permute-done.refs_1_
  19.1 0.0 collective-permute-done.1.refs_2_
  19.1 0.0 copy-start.1
  19.1 3.7 %attend.1 = (bf16[4,384,1024]{2,1,0:T(8,128)(2,1)S(1)}, f32[128,512]{1,0:T(8,128)S(1)}, bf16[128,512]{1,0:T(8,128)(2,1)S(1)}, bf16[128,512]{1,0:T(8,128)(2,1)S(1)}) custom-call(bf16[4,1024,128]{2,1,0:T(8,128)(2,1)S(1)} %query_prep.1.qs_ref, bf16[128,4096]{1,0:T(8,128)(2,1)S(1)} %bitcast.21, bf16[144,512]{1,0:T(8,128)(2,1)S(1)} %key_message.1.refs_0_, ...), custom_call_target="tpu_custom_call" | custom-call | flops 1610612736 | bytes 5000000 | tf_op jit(solution)/shard_map/attend/pallas_call | solution.py:348
  22.8 1.6 %copy-done.15 = bf16[4,384,1024]{2,1,0:T(8,128)(2,1)} copy-done((bf16[4,384,1024]{2,1,0:T(8,128)(2,1)}, bf16[4,384,1024]{2,1,0:T(8,128)(2,1)S(1)}, u32[]{:S(2)}) %copy-start.15) | copy-done | bytes 3145752
  24.5 4.5 %collective-permute-start.3 = (bf16[128,512]{1,0:T(8,128)(2,1)S(1)}, bf16[128,512]{1,0:T(8,128)(2,1)S(1)}, u32[]{:S(2)}, u32[]{:S(2)}) collective-permute-start(bf16[128,512]{1,0:T(8,128)(2,1)S(1)} %get-tuple-element.20), channel_id=1, source_target_pairs={{2,0},{3,1},{6,4},{7,5},{10,8},{11,9},{14,12},{15,13},{18,16},{19,... | collective-permute-start | bytes 393224 | tf_op jit(solution)/shard_map/ppermute | solution.py:283
  29.0 1.9 %collective-permute-start.2 = (bf16[128,512]{1,0:T(8,128)(2,1)S(1)}, bf16[128,512]{1,0:T(8,128)(2,1)S(1)}, u32[]{:S(2)}, u32[]{:S(2)}) collective-permute-start(bf16[128,512]{1,0:T(8,128)(2,1)S(1)} %get-tuple-element.19), channel_id=1, source_target_pairs={{1,0},{2,1},{3,2},{5,4},{6,5},{7,6},{9,8},{10,9},{11,10},{13,12},{... | collective-permute-start | bytes 393224 | tf_op jit(solution)/shard_map/ppermute | solution.py:283
  31.0 0.5 features.1
  31.4 2.1 %collective-permute-start.9 = (bf16[1280,128]{1,0:T(8,128)(2,1)S(1)}, bf16[1280,128]{1,0:T(8,128)(2,1)S(1)}, u32[]{:S(2)}, u32[]{:S(2)}) collective-permute-start(bf16[1280,128]{1,0:T(8,128)(2,1)S(1)} %get-tuple-element.27), channel_id=1, source_target_pairs={{0,1},{1,2},{2,3},{3,0},{4,5},{5,6},{6,7},{7,4},{8,9},{9,10},{10,1... | collective-permute-start | bytes 983048 | tf_op jit(solution)/shard_map/ppermute | solution.py:286
  33.5 0.0 collective-permute-start.5
  33.5 0.0 collective-permute-done.4.refs_4_.refs_9_
  33.5 1.5 %collective-permute-start.6 = (bf16[144,512]{1,0:T(8,128)(2,1)S(1)}, bf16[144,512]{1,0:T(8,128)(2,1)S(1)}, u32[]{:S(2)}, u32[]{:S(2)}) collective-permute-start(bf16[144,512]{1,0:T(8,128)(2,1)S(1)} %value_message.1.refs_3_.refs_8_), channel_id=1, source_target_pairs={{0,3},{1,0},{2,1},{3,2},{4,7},{5,4},{6,5},{7,6},{8,11},{9,8},{10,9... | collective-permute-start | bytes 442376 | tf_op jit(solution)/shard_map/ppermute | solution.py:286
  35.1 0.0 collective-permute-done.3
  35.1 1.4 %collective-permute-start.10 = (bf16[1280,128]{1,0:T(8,128)(2,1)S(1)}, bf16[1280,128]{1,0:T(8,128)(2,1)S(1)}, u32[]{:S(2)}, u32[]{:S(2)}) collective-permute-start(bf16[1280,128]{1,0:T(8,128)(2,1)S(1)} %get-tuple-element.28), channel_id=1, source_target_pairs={{0,2},{1,3},{2,0},{3,1},{4,6},{5,7},{6,4},{7,5},{8,10},{9,11},{10,... | collective-permute-start | bytes 983048 | tf_op jit(solution)/shard_map/ppermute | solution.py:286
  36.5 0.9 collective-permute-done.2
  37.3 0.5 collective-permute-start.11
  37.9 7.1 %collective-permute-done.5.refs_5_.refs_10_ = bf16[144,512]{1,0:T(8,128)(2,1)S(1)} collective-permute-done((bf16[144,512]{1,0:T(8,128)(2,1)S(1)}, bf16[144,512]{1,0:T(8,128)(2,1)S(1)}, u32[]{:S(2)}, u32[]{:S(2)}) %collective-permute-start.5) | collective-permute-done | bytes 147488 | tf_op jit(solution)/shard_map/ppermute | solution.py:286
  45.0 0.0 collective-permute-start.12
  45.0 2.5 %collective-permute-done.6.refs_6_.refs_11_ = bf16[144,512]{1,0:T(8,128)(2,1)S(1)} collective-permute-done((bf16[144,512]{1,0:T(8,128)(2,1)S(1)}, bf16[144,512]{1,0:T(8,128)(2,1)S(1)}, u32[]{:S(2)}, u32[]{:S(2)}) %collective-permute-start.6) | collective-permute-done | bytes 147488 | tf_op jit(solution)/shard_map/ppermute | solution.py:286
  47.5 0.0 collective-permute-start.13
  47.5 0.0 collective-permute-done.9.refs_1_
  47.5 1.6 %collective-permute-start.14 = (bf16[128,512]{1,0:T(8,128)(2,1)S(1)}, bf16[128,512]{1,0:T(8,128)(2,1)S(1)}, u32[]{:S(2)}, u32[]{:S(2)}) collective-permute-start(bf16[128,512]{1,0:T(8,128)(2,1)S(1)} %add_convert_fusion.v_ref.refs_4_), channel_id=1, source_target_pairs={{0,3},{1,0},{2,1},{3,2},{4,7},{5,4},{6,5},{7,6},{8,11},{9,8},{10,9... | collective-permute-start | bytes 393224 | tf_op jit(solution)/shard_map/ppermute | solution.py:286
  49.1 4.6 %collective-permute-done.10.refs_2_ = bf16[1280,128]{1,0:T(8,128)(2,1)S(1)} collective-permute-done((bf16[1280,128]{1,0:T(8,128)(2,1)S(1)}, bf16[1280,128]{1,0:T(8,128)(2,1)S(1)}, u32[]{:S(2)}, u32[]{:S(2)}) %collective-permute-start.10) | collective-permute-done | bytes 327712 | tf_op jit(solution)/shard_map/ppermute | solution.py:286
  53.7 0.9 collective-permute-done.11.refs_3_
  54.6 1.5 %collective-permute-done.12.refs_5_ = bf16[128,512]{1,0:T(8,128)(2,1)S(1)} collective-permute-done((bf16[128,512]{1,0:T(8,128)(2,1)S(1)}, bf16[128,512]{1,0:T(8,128)(2,1)S(1)}, u32[]{:S(2)}, u32[]{:S(2)}) %collective-permute-start.12) | collective-permute-done | bytes 131104 | tf_op jit(solution)/shard_map/ppermute | solution.py:286
  56.1 1.0 collective-permute-done.13.refs_6_
  57.1 1.1 %collective-permute-done.14.refs_7_ = bf16[128,512]{1,0:T(8,128)(2,1)S(1)} collective-permute-done((bf16[128,512]{1,0:T(8,128)(2,1)S(1)}, bf16[128,512]{1,0:T(8,128)(2,1)S(1)}, u32[]{:S(2)}, u32[]{:S(2)}) %collective-permute-start.14) | collective-permute-done | bytes 131104 | tf_op jit(solution)/shard_map/ppermute | solution.py:286
  58.1 1.2 %weight.1 = (bf16[640,512]{1,0:T(8,128)(2,1)S(1)}, f32[640,512]{1,0:T(8,128)S(1)}) custom-call(bf16[1280,128]{1,0:T(8,128)(2,1)S(1)} %get-tuple-element.26.refs_0_, bf16[1280,128]{1,0:T(8,128)(2,1)S(1)} %collective-permute-done.9.refs_1_, bf16[1280,128]{1,0:T(8,128)(2,1)S(1)} %collective-permute-done.10.refs_2_, ...), custom_call_target="tpu_custom_call" | custom-call | flops 671088640 | bytes 4000000 | tf_op jit(solution)/shard_map/weight/pallas_call | solution.py:401
  59.3 0.1 collective-permute-start.15
  59.4 0.0 slice-start
  59.4 0.0 slice-start.1
  59.4 12.6 %backward.1 = (bf16[128,4096]{1,0:T(8,128)(2,1)}, f32[128,512]{1,0:T(8,128)S(1)}, bf16[128,512]{1,0:T(8,128)(2,1)S(1)}, bf16[128,512]{1,0:T(8,128)(2,1)S(1)}) custom-call(bf16[4,384,1024]{2,1,0:T(8,128)(2,1)} %copy-done.15, bf16[128,4096]{1,0:T(8,128)(2,1)S(1)} %bitcast.22, bf16[128,4096]{1,0:T(8,128)(2,1)S(1)} %bitcast.14, ...), custom_call_target="tpu_custom_call" | custom-call | flops 2415919104 | bytes 7000000 | tf_op jit(solution)/shard_map/backward/pallas_call | solution.py:367
  72.1 6.8 %collective-permute-start.7 = (bf16[128,512]{1,0:T(8,128)(2,1)S(1)}, bf16[128,512]{1,0:T(8,128)(2,1)S(1)}, u32[]{:S(2)}, u32[]{:S(2)}) collective-permute-start(bf16[128,512]{1,0:T(8,128)(2,1)S(1)} %get-tuple-element.24), channel_id=1, source_target_pairs={{1,0},{2,1},{3,2},{5,4},{6,5},{7,6},{9,8},{10,9},{11,10},{13,12},{... | collective-permute-start | bytes 393224 | tf_op jit(solution)/shard_map/ppermute | solution.py:283
  78.8 1.3 %collective-permute-start.8 = (bf16[128,512]{1,0:T(8,128)(2,1)S(1)}, bf16[128,512]{1,0:T(8,128)(2,1)S(1)}, u32[]{:S(2)}, u32[]{:S(2)}) collective-permute-start(bf16[128,512]{1,0:T(8,128)(2,1)S(1)} %get-tuple-element.25), channel_id=1, source_target_pairs={{2,0},{3,1},{6,4},{7,5},{10,8},{11,9},{14,12},{15,13},{18,16},{19,... | collective-permute-start | bytes 393224 | tf_op jit(solution)/shard_map/ppermute | solution.py:283
  80.1 0.0 collective-permute-done.15
  80.1 0.0 copy-start.6
  80.2 0.0 copy-start.10
  80.2 0.3 fusion.3
  80.5 0.5 collective-permute-start.18
  81.0 3.5 %collective-permute-start.17 = (bf16[160,512]{1,0:T(8,128)(2,1)S(1)}, bf16[160,512]{1,0:T(8,128)(2,1)S(1)}, u32[]{:S(2)}, u32[]{:S(2)}) collective-permute-start(bf16[160,512]{1,0:T(8,128)(2,1)S(1)} %get-tuple-element.36), channel_id=1, source_target_pairs={{0,16},{4,20},{8,24},{12,28},{16,0},{20,4},{24,8},{28,12},{1,17},{... | collective-permute-start | bytes 491528 | tf_op jit(solution)/shard_map/ppermute | solution.py:411
  84.5 0.0 collective-permute-start.16
  84.5 0.0 collective-permute-done.7.refs_0_
  84.5 1.2 %key_back.1 = bf16[128,512]{1,0:T(8,128)(2,1)} custom-call(bf16[128,512]{1,0:T(8,128)(2,1)S(1)} %bitcast.16, f32[128,512]{1,0:T(8,128)S(1)} %get-tuple-element.23.own_ref, f32[1,128]{1,0:T(1,128)S(1)} %bitcast.18, f32[2,128,128]{2,1,0:T(8,128)S(1)} %copy-done.3, f32[2,4,128]{2,1,0:T(4,128)S(1)} %copy-done.8, ...), custom_call_target="tpu_custom_call" | custom-call | bytes 1000000 | tf_op jit(solution)/shard_map/key_back/pallas_call | solution.py:388
  85.7 3.1 %hidden_grad.1 = bf16[128,5120]{1,0:T(8,128)(2,1)} custom-call(bf16[128,512]{1,0:T(8,128)(2,1)S(1)} %add_convert_fusion.v_ref.refs_4_, bf16[5120,512]{1,0:T(8,128)(2,1)S(1)} %bitcast.10), custom_call_target="tpu_custom_call" | custom-call | flops 671088640 | bytes 7000000 | tf_op jit(solution)/shard_map/hidden_grad/pallas_call | solution.py:393
  88.8 0.0 collective-permute-done.18
  88.8 6.5 %collective-permute-done.17 = bf16[160,512]{1,0:T(8,128)(2,1)S(1)} collective-permute-done((bf16[160,512]{1,0:T(8,128)(2,1)S(1)}, bf16[160,512]{1,0:T(8,128)(2,1)S(1)}, u32[]{:S(2)}, u32[]{:S(2)}) %collective-permute-start.17) | collective-permute-done | bytes 163872 | tf_op jit(solution)/shard_map/ppermute | solution.py:411
  95.3 3.2 %collective-permute-done.16 = bf16[160,512]{1,0:T(8,128)(2,1)S(1)} collective-permute-done((bf16[160,512]{1,0:T(8,128)(2,1)S(1)}, bf16[160,512]{1,0:T(8,128)(2,1)S(1)}, u32[]{:S(2)}, u32[]{:S(2)}) %collective-permute-start.16) | collective-permute-done | bytes 163872 | tf_op jit(solution)/shard_map/ppermute | solution.py:411
  98.6 0.8 fusion.2
  (24 shorter events, 0.1 us)
Async XLA Ops:
  0.6 0.9 copy-start.2
  1.5 0.9 copy-start.5
  2.4 0.7 copy-start.7
  3.1 0.7 copy-start.9
  3.8 0.7 copy-start.11
  4.8 14.3 %collective-permute-start = (bf16[144,512]{1,0:T(8,128)(2,1)S(1)}, bf16[144,512]{1,0:T(8,128)(2,1)S(1)}, u32[]{:S(2)}, u32[]{:S(2)}) collective-permute-start(bf16[144,512]{1,0:T(8,128)(2,1)S(1)} %key_message.1.refs_0_), channel_id=1, source_target_pairs={{0,1},{1,2},{2,3},{4,5},{5,6},{6,7},{8,9},{9,10},{10,11},{12,13},{... | collective-permute-start | bytes 442376 | tf_op jit(solution)/shard_map/ppermute | solution.py:280
  8.2 10.9 %collective-permute-start.1 = (bf16[144,512]{1,0:T(8,128)(2,1)S(1)}, bf16[144,512]{1,0:T(8,128)(2,1)S(1)}, u32[]{:S(2)}, u32[]{:S(2)}) collective-permute-start(bf16[144,512]{1,0:T(8,128)(2,1)S(1)} %key_message.1.refs_0_), channel_id=1, source_target_pairs={{0,2},{1,3},{4,6},{5,7},{8,10},{9,11},{12,14},{13,15},{16,18},{17,... | collective-permute-start | bytes 442376 | tf_op jit(solution)/shard_map/ppermute | solution.py:280
  9.5 1.3 %copy-start = (bf16[1,128,5120]{2,1,0:T(8,128)(2,1)S(1)}, bf16[1,128,5120]{2,1,0:T(8,128)(2,1)}, u32[]{:S(2)}) copy-start(bf16[1,128,5120]{2,1,0:T(8,128)(2,1)} %param.11) | copy-start | bytes 3932164
  10.8 0.7 copy-start.13
  11.5 4.1 %copy-start.3 = (f32[2,128,128]{2,1,0:T(8,128)S(1)}, f32[2,128,128]{2,1,0:T(8,128)}, u32[]{:S(2)}) copy-start(f32[2,128,128]{2,1,0:T(8,128)} %constant.6.clone.rows_ref) | copy-start | bytes 393220
  11.5 4.2 %copy-start.4 = (bf16[1,128,4096]{2,1,0:T(8,128)(2,1)S(1)}, bf16[1,128,4096]{2,1,0:T(8,128)(2,1)}, u32[]{:S(2)}) copy-start(bf16[1,128,4096]{2,1,0:T(8,128)(2,1)} %param.12) | copy-start | bytes 3145732
  11.5 4.2 %copy-start.8 = (f32[2,4,128]{2,1,0:T(4,128)S(1)}, f32[2,4,128]{2,1,0:T(4,128)}, u32[]{:S(2)}) copy-start(f32[2,4,128]{2,1,0:T(4,128)} %constant.7.clone.base_ref) | copy-start | bytes 12292
  11.5 4.2 %copy-start.12 = (f32[128]{0:T(128)S(1)}, f32[128]{0:T(128)}, u32[]{:S(2)}) copy-start(f32[128]{0:T(128)} %param.16) | copy-start | bytes 1540
  15.5 3.5 %copy-start.14 = (bf16[1,128,4096]{2,1,0:T(8,128)(2,1)S(1)}, bf16[1,128,4096]{2,1,0:T(8,128)(2,1)}, u32[]{:S(2)}) copy-start(bf16[1,128,4096]{2,1,0:T(8,128)(2,1)} %param.14) | copy-start | bytes 3145732
  15.5 18.0 %collective-permute-start.4 = (bf16[144,512]{1,0:T(8,128)(2,1)S(1)}, bf16[144,512]{1,0:T(8,128)(2,1)S(1)}, u32[]{:S(2)}, u32[]{:S(2)}) collective-permute-start(bf16[144,512]{1,0:T(8,128)(2,1)S(1)} %value_message.1.refs_3_.refs_8_), channel_id=1, source_target_pairs={{0,1},{1,2},{2,3},{3,0},{4,5},{5,6},{6,7},{7,4},{8,9},{9,10},{10,1... | collective-permute-start | bytes 442376 | tf_op jit(solution)/shard_map/ppermute | solution.py:286
  19.1 11.9 %copy-start.1 = (bf16[1,128,5120]{2,1,0:T(8,128)(2,1)S(1)}, bf16[1,128,5120]{2,1,0:T(8,128)(2,1)}, u32[]{:S(2)}) copy-start(bf16[1,128,5120]{2,1,0:T(8,128)(2,1)} %param.11) | copy-start | bytes 3932164
  22.8 1.6 %copy-start.15 = (bf16[4,384,1024]{2,1,0:T(8,128)(2,1)}, bf16[4,384,1024]{2,1,0:T(8,128)(2,1)S(1)}, u32[]{:S(2)}) copy-start(bf16[4,384,1024]{2,1,0:T(8,128)(2,1)S(1)} %get-tuple-element.21.p_ref) | copy-start | bytes 9437188
  24.5 10.6 %collective-permute-start.3 = (bf16[128,512]{1,0:T(8,128)(2,1)S(1)}, bf16[128,512]{1,0:T(8,128)(2,1)S(1)}, u32[]{:S(2)}, u32[]{:S(2)}) collective-permute-start(bf16[128,512]{1,0:T(8,128)(2,1)S(1)} %get-tuple-element.20), channel_id=1, source_target_pairs={{2,0},{3,1},{6,4},{7,5},{10,8},{11,9},{14,12},{15,13},{18,16},{19,... | collective-permute-start | bytes 393224 | tf_op jit(solution)/shard_map/ppermute | solution.py:283
  29.0 8.3 %collective-permute-start.2 = (bf16[128,512]{1,0:T(8,128)(2,1)S(1)}, bf16[128,512]{1,0:T(8,128)(2,1)S(1)}, u32[]{:S(2)}, u32[]{:S(2)}) collective-permute-start(bf16[128,512]{1,0:T(8,128)(2,1)S(1)} %get-tuple-element.19), channel_id=1, source_target_pairs={{1,0},{2,1},{3,2},{5,4},{6,5},{7,6},{9,8},{10,9},{11,10},{13,12},{... | collective-permute-start | bytes 393224 | tf_op jit(solution)/shard_map/ppermute | solution.py:283
  31.4 16.1 %collective-permute-start.9 = (bf16[1280,128]{1,0:T(8,128)(2,1)S(1)}, bf16[1280,128]{1,0:T(8,128)(2,1)S(1)}, u32[]{:S(2)}, u32[]{:S(2)}) collective-permute-start(bf16[1280,128]{1,0:T(8,128)(2,1)S(1)} %get-tuple-element.27), channel_id=1, source_target_pairs={{0,1},{1,2},{2,3},{3,0},{4,5},{5,6},{6,7},{7,4},{8,9},{9,10},{10,1... | collective-permute-start | bytes 983048 | tf_op jit(solution)/shard_map/ppermute | solution.py:286
  33.5 11.5 %collective-permute-start.5 = (bf16[144,512]{1,0:T(8,128)(2,1)S(1)}, bf16[144,512]{1,0:T(8,128)(2,1)S(1)}, u32[]{:S(2)}, u32[]{:S(2)}) collective-permute-start(bf16[144,512]{1,0:T(8,128)(2,1)S(1)} %value_message.1.refs_3_.refs_8_), channel_id=1, source_target_pairs={{0,2},{1,3},{2,0},{3,1},{4,6},{5,7},{6,4},{7,5},{8,10},{9,11},{10,... | collective-permute-start | bytes 442376 | tf_op jit(solution)/shard_map/ppermute | solution.py:286
  33.5 14.0 %collective-permute-start.6 = (bf16[144,512]{1,0:T(8,128)(2,1)S(1)}, bf16[144,512]{1,0:T(8,128)(2,1)S(1)}, u32[]{:S(2)}, u32[]{:S(2)}) collective-permute-start(bf16[144,512]{1,0:T(8,128)(2,1)S(1)} %value_message.1.refs_3_.refs_8_), channel_id=1, source_target_pairs={{0,3},{1,0},{2,1},{3,2},{4,7},{5,4},{6,5},{7,6},{8,11},{9,8},{10,9... | collective-permute-start | bytes 442376 | tf_op jit(solution)/shard_map/ppermute | solution.py:286
  35.1 18.6 %collective-permute-start.10 = (bf16[1280,128]{1,0:T(8,128)(2,1)S(1)}, bf16[1280,128]{1,0:T(8,128)(2,1)S(1)}, u32[]{:S(2)}, u32[]{:S(2)}) collective-permute-start(bf16[1280,128]{1,0:T(8,128)(2,1)S(1)} %get-tuple-element.28), channel_id=1, source_target_pairs={{0,2},{1,3},{2,0},{3,1},{4,6},{5,7},{6,4},{7,5},{8,10},{9,11},{10,... | collective-permute-start | bytes 983048 | tf_op jit(solution)/shard_map/ppermute | solution.py:286
  37.3 17.2 %collective-permute-start.11 = (bf16[1280,128]{1,0:T(8,128)(2,1)S(1)}, bf16[1280,128]{1,0:T(8,128)(2,1)S(1)}, u32[]{:S(2)}, u32[]{:S(2)}) collective-permute-start(bf16[1280,128]{1,0:T(8,128)(2,1)S(1)} %get-tuple-element.29), channel_id=1, source_target_pairs={{0,3},{1,0},{2,1},{3,2},{4,7},{5,4},{6,5},{7,6},{8,11},{9,8},{10,9... | collective-permute-start | bytes 983048 | tf_op jit(solution)/shard_map/ppermute | solution.py:286
  45.0 11.0 %collective-permute-start.12 = (bf16[128,512]{1,0:T(8,128)(2,1)S(1)}, bf16[128,512]{1,0:T(8,128)(2,1)S(1)}, u32[]{:S(2)}, u32[]{:S(2)}) collective-permute-start(bf16[128,512]{1,0:T(8,128)(2,1)S(1)} %add_convert_fusion.v_ref.refs_4_), channel_id=1, source_target_pairs={{0,1},{1,2},{2,3},{3,0},{4,5},{5,6},{6,7},{7,4},{8,9},{9,10},{10,1... | collective-permute-start | bytes 393224 | tf_op jit(solution)/shard_map/ppermute | solution.py:286
  47.5 9.5 %collective-permute-start.13 = (bf16[128,512]{1,0:T(8,128)(2,1)S(1)}, bf16[128,512]{1,0:T(8,128)(2,1)S(1)}, u32[]{:S(2)}, u32[]{:S(2)}) collective-permute-start(bf16[128,512]{1,0:T(8,128)(2,1)S(1)} %add_convert_fusion.v_ref.refs_4_), channel_id=1, source_target_pairs={{0,2},{1,3},{2,0},{3,1},{4,6},{5,7},{6,4},{7,5},{8,10},{9,11},{10,... | collective-permute-start | bytes 393224 | tf_op jit(solution)/shard_map/ppermute | solution.py:286
  47.5 10.6 %collective-permute-start.14 = (bf16[128,512]{1,0:T(8,128)(2,1)S(1)}, bf16[128,512]{1,0:T(8,128)(2,1)S(1)}, u32[]{:S(2)}, u32[]{:S(2)}) collective-permute-start(bf16[128,512]{1,0:T(8,128)(2,1)S(1)} %add_convert_fusion.v_ref.refs_4_), channel_id=1, source_target_pairs={{0,3},{1,0},{2,1},{3,2},{4,7},{5,4},{6,5},{7,6},{8,11},{9,8},{10,9... | collective-permute-start | bytes 393224 | tf_op jit(solution)/shard_map/ppermute | solution.py:286
  59.3 20.8 %collective-permute-start.15 = (bf16[640,512]{1,0:T(8,128)(2,1)S(1)}, bf16[640,512]{1,0:T(8,128)(2,1)S(1)}, u32[]{:S(2)}, u32[]{:S(2)}) collective-permute-start(bf16[640,512]{1,0:T(8,128)(2,1)S(1)} %get-tuple-element.31), channel_id=1, source_target_pairs={{0,4},{4,0},{8,12},{12,8},{16,20},{20,16},{24,28},{28,24},{1,5},{5... | collective-permute-start | bytes 1966088 | tf_op jit(solution)/shard_map/ppermute | solution.py:406
  59.4 26.3 %slice-start = ((s8[5242880]{0:T(1024)(128)(4,1)}), s8[4194304]{0:T(1024)(128)(4,1)S(1)}, s32[]{:S(2)}) async-start(s8[5242880]{0:T(1024)(128)(4,1)} %bitcast.9), calls=%async_computation | async-start | bytes 8388608
  59.4 26.2 %slice-start.1 = ((s8[5242880]{0:T(1024)(128)(4,1)}), s8[1048576]{0:T(1024)(128)(4,1)S(1)}, s32[]{:S(2)}) async-start(s8[5242880]{0:T(1024)(128)(4,1)} %bitcast.9), calls=%async_computation.1 | async-start | bytes 2097152
  72.1 12.4 %collective-permute-start.7 = (bf16[128,512]{1,0:T(8,128)(2,1)S(1)}, bf16[128,512]{1,0:T(8,128)(2,1)S(1)}, u32[]{:S(2)}, u32[]{:S(2)}) collective-permute-start(bf16[128,512]{1,0:T(8,128)(2,1)S(1)} %get-tuple-element.24), channel_id=1, source_target_pairs={{1,0},{2,1},{3,2},{5,4},{6,5},{7,6},{9,8},{10,9},{11,10},{13,12},{... | collective-permute-start | bytes 393224 | tf_op jit(solution)/shard_map/ppermute | solution.py:283
  78.8 5.7 %collective-permute-start.8 = (bf16[128,512]{1,0:T(8,128)(2,1)S(1)}, bf16[128,512]{1,0:T(8,128)(2,1)S(1)}, u32[]{:S(2)}, u32[]{:S(2)}) collective-permute-start(bf16[128,512]{1,0:T(8,128)(2,1)S(1)} %get-tuple-element.25), channel_id=1, source_target_pairs={{2,0},{3,1},{6,4},{7,5},{10,8},{11,9},{14,12},{15,13},{18,16},{19,... | collective-permute-start | bytes 393224 | tf_op jit(solution)/shard_map/ppermute | solution.py:283
  80.1 4.3 %copy-start.6 = (bf16[1,128,512]{2,1,0:T(8,128)(2,1)S(1)}, bf16[1,128,512]{2,1,0:T(8,128)(2,1)}, u32[]{:S(2)}) copy-start(bf16[1,128,512]{2,1,0:T(8,128)(2,1)} %param.13) | copy-start | bytes 393220
  80.2 4.3 %copy-start.10 = (f32[128]{0:T(128)S(1)}, f32[128]{0:T(128)}, u32[]{:S(2)}) copy-start(f32[128]{0:T(128)} %param.17) | copy-start | bytes 1540
  80.5 8.3 %collective-permute-start.18 = (bf16[160,512]{1,0:T(8,128)(2,1)S(1)}, bf16[160,512]{1,0:T(8,128)(2,1)S(1)}, u32[]{:S(2)}, u32[]{:S(2)}) collective-permute-start(bf16[160,512]{1,0:T(8,128)(2,1)S(1)} %get-tuple-element.35), channel_id=1, source_target_pairs={{0,24},{4,28},{8,0},{12,4},{16,8},{20,12},{24,16},{28,20},{1,25},{... | collective-permute-start | bytes 491528 | tf_op jit(solution)/shard_map/ppermute | solution.py:411
  81.0 14.3 %collective-permute-start.17 = (bf16[160,512]{1,0:T(8,128)(2,1)S(1)}, bf16[160,512]{1,0:T(8,128)(2,1)S(1)}, u32[]{:S(2)}, u32[]{:S(2)}) collective-permute-start(bf16[160,512]{1,0:T(8,128)(2,1)S(1)} %get-tuple-element.36), channel_id=1, source_target_pairs={{0,16},{4,20},{8,24},{12,28},{16,0},{20,4},{24,8},{28,12},{1,17},{... | collective-permute-start | bytes 491528 | tf_op jit(solution)/shard_map/ppermute | solution.py:411
  84.5 14.1 %collective-permute-start.16 = (bf16[160,512]{1,0:T(8,128)(2,1)S(1)}, bf16[160,512]{1,0:T(8,128)(2,1)S(1)}, u32[]{:S(2)}, u32[]{:S(2)}) collective-permute-start(bf16[160,512]{1,0:T(8,128)(2,1)S(1)} %get-tuple-element.34), channel_id=1, source_target_pairs={{0,8},{4,12},{8,16},{12,20},{16,24},{20,28},{24,0},{28,4},{1,9},{5... | collective-permute-start | bytes 491528 | tf_op jit(solution)/shard_map/ppermute | solution.py:411

commit v2 on v1

v2 whole, which is shorter than its diff:
```python
import functools
import math

import jax
import jax.numpy as jnp
import numpy as np
from jax import lax
from jax.experimental import pallas as pl
from jax.experimental.pallas import tpu as pltpu
from jax.sharding import PartitionSpec as P

epsilon = 1e-06
rope_base = 1000000.0
meta_rows = 16
masked = -1e30
VMEM = pltpu.VMEM
f32, bf16 = jnp.float32, jnp.bfloat16
NT = (((1,), (1,)), ((), ()))


def params(mib):
    return pltpu.CompilerParams(vmem_limit_bytes=mib << 20)


def ordered(kernel, inputs, after):
    def body(*refs):
        kernel(*refs[:inputs], *refs[inputs + after :])

    return body


def cost(flops, bytes_accessed):
    return pl.CostEstimate(flops=int(flops), bytes_accessed=int(bytes_accessed), transcendentals=0)


def rope_constants(rows, blocks, head_width):
    half = head_width // 2
    frequency = rope_base ** (-(np.arange(half) * 2.0 / head_width))
    frequency = np.concatenate([frequency, frequency])
    sign = np.concatenate([-np.ones(half), np.ones(half)])

    def table(positions):
        angles = positions[:, None] * frequency[None, :]
        return np.stack([np.cos(angles), np.sin(angles) * sign]).astype(np.float32)

    return table(np.arange(rows)), table(np.arange(blocks) * rows)


def rotation(rows_ref, base_ref, me):
    cos_b = base_ref[0, pl.ds(me, 1), :]
    sin_b = base_ref[1, pl.ds(me, 1), :]
    cos_r, sin_r = rows_ref[0], rows_ref[1]
    return cos_b * cos_r - sin_b * sin_r, sin_b * cos_r + cos_b * sin_r


def swap_halves(x):
    return pltpu.roll(x, x.shape[-1] // 2, 1)


def norm_rope(u, gain, cosine, sine):
    inverse = lax.rsqrt(jnp.mean(u * u, axis=-1, keepdims=True) + epsilon)
    y = u * inverse * gain
    return y * cosine + swap_halves(y) * sine


def norm_rope_back(u, dz, gain, cosine, sine):
    inverse = lax.rsqrt(jnp.mean(u * u, axis=-1, keepdims=True) + epsilon)
    dn = (dz * cosine + swap_halves(dz * sine)) * gain
    along = jnp.mean(dn * u, axis=-1, keepdims=True) * (inverse * inverse)
    return inverse * (dn - u * along)


def message_kernel(blocks, *refs):
    sources, (out_ref, far_ref, *held, sems) = refs[:8], refs[8:]
    me = lax.axis_index("ctx")
    w_held, h_held = held[-1], held[-2]
    rows, width = h_held.shape
    parts = 8
    part = width // parts
    copies = [pltpu.make_async_copy(a, b, sems.at[i]) for i, (a, b) in enumerate(zip(sources[:7], held))]
    for i in range(parts):
        piece = pl.ds(i * part, part)
        copies.append(
            pltpu.make_async_copy(sources[7].at[piece], w_held.at[piece], sems.at[7 + i])
        )
    for copy in copies:
        copy.start()
    for copy in copies[:6]:
        copy.wait()
    k_ref, doc_ref, dest_ref, gain_ref, rows_ref, base_ref = held[:6]
    kv_width = k_ref.shape[1]
    hd = gain_ref.shape[1]
    cosine, sine = rotation(rows_ref, base_ref, me)
    dest = jnp.broadcast_to(dest_ref[...], (meta_rows, rows))
    block = jnp.zeros_like(dest)
    for j in range(1, blocks):
        block = block + (dest >= j * rows).astype(jnp.int32)
    which = lax.broadcasted_iota(jnp.int32, dest.shape, 0)
    marks = jnp.where(which == 0, block, dest - block * rows)
    marks = jnp.where(which == 2, doc_ref[...] + 1, marks).astype(f32).astype(bf16)
    for h in range(kv_width // hd):
        cols = slice(h * hd, (h + 1) * hd)
        u = k_ref[:, cols].astype(f32)
        out_ref[rows + meta_rows :, cols] = norm_rope(u, gain_ref[...], cosine, sine).astype(bf16)
        out_ref[rows : rows + meta_rows, cols] = marks
        far_ref[rows:, cols] = marks
    copies[6].wait()
    total = None
    for i in range(parts):
        copies[7 + i].wait()
        piece = slice(i * part, (i + 1) * part)
        product = jnp.dot(h_held[:, piece], w_held[piece], preferred_element_type=f32)
        total = product if total is None else total + product
    out_ref[:rows] = total.astype(bf16)
    far_ref[:rows] = total.astype(bf16)


def upright_tables(gain_ref, rows_ref, base_ref, scale, held):
    rows = rows_ref.shape[1]
    cosine, sine = rotation(rows_ref, base_ref, lax.axis_index("ctx"))
    held[0] = cosine.T
    held[1] = sine.T
    held[2] = jnp.broadcast_to(gain_ref[...] * scale, (rows, gain_ref.shape[1])).T


def swap_rows(x):
    half = x.shape[0] // 2
    return jnp.concatenate([x[half:], x[:half]], axis=0)


def query_prep_kernel(scale, q_ref, gain_ref, rows_ref, base_ref, scaled_ref, turned_ref, held):
    rows, width = q_ref.shape
    hd = gain_ref.shape[1]

    @pl.when(pl.program_id(0) == 0)
    def _():
        upright_tables(gain_ref, rows_ref, base_ref, scale, held)

    for h in range(width // hd):
        turned = q_ref[:, h * hd : (h + 1) * hd].T
        turned_ref[0, :, h * rows : (h + 1) * rows] = turned
        u = turned.astype(f32)
        inverse = lax.rsqrt(jnp.mean(u * u, axis=0, keepdims=True) + epsilon)
        y = u * inverse * held[2]
        z = y * held[0] + swap_rows(y) * held[1]
        scaled_ref[0, :, h * rows : (h + 1) * rows] = z.astype(bf16)


def share_index(j, half, c, z, core, zs, blocks):
    owner_core = core if half else 1 - core
    return ((z ^ j) * 2 + owner_core) * blocks + c


def feature_kernel(blocks, zs, h_hbm, *refs):
    outs, (held, turned, sems) = refs[:blocks], refs[blocks:]
    me, dp = lax.axis_index("ctx"), lax.axis_index("dp")
    z, core = dp // 2, dp % 2
    parts, rows, part = held.shape
    share = turned.shape[0] // (blocks * zs * 2)
    copies = [
        pltpu.make_async_copy(h_hbm.at[:, i * part : (i + 1) * part], held.at[i], sems.at[i])
        for i in range(parts)
    ]
    for copy in copies:
        copy.start()
    for i, copy in enumerate(copies):
        copy.wait()
        for c in range(part // 128):
            at = i * part + c * 128
            turned[at : at + 128] = held[i, :, c * 128 : (c + 1) * 128].T
    for m in range(blocks):
        c = lax.rem(me + m, blocks)
        for half in range(2):
            for j in range(zs):
                start = share_index(j, half, c, z, core, zs, blocks) * share
                start = pl.multiple_of(start, 16)
                at = (half * zs + j) * share
                outs[m][at : at + share] = turned[pl.ds(start, share)]


def mark_rows(ref, rows):
    return ref[rows : rows + meta_rows, :rows].astype(f32)


def attend_kernel(back, qs_ref, g_ref, *refs):
    k_refs = refs[: back + 1]
    p_ref, own_ref = refs[back + 1], refs[back + 2]
    send_refs = refs[back + 3 : 2 * back + 3]
    bias_ref = refs[-1]
    rows = g_ref.shape[0]
    hd = own_ref.shape[1]
    group = g_ref.shape[1] // hd

    @pl.when(pl.program_id(0) == 0)
    def _():
        query_doc = mark_rows(k_refs[0], rows)[2:3]
        for b in range(back + 1):
            key_doc = jnp.broadcast_to(mark_rows(k_refs[b], rows)[2:3], (rows, rows)).T
            allowed = key_doc == query_doc
            if b == 0:
                key_row = lax.broadcasted_iota(jnp.int32, (rows, rows), 0)
                query_row = lax.broadcasted_iota(jnp.int32, (rows, rows), 1)
                allowed = allowed & (key_row <= query_row)
            else:
                allowed = allowed & (lax.axis_index("ctx") >= b)
            bias_ref[b * rows : (b + 1) * rows] = jnp.where(allowed, 0.0, masked)

    keys = jnp.concatenate([r[rows + meta_rows :] for r in k_refs], axis=0)
    logits = jnp.dot(keys, qs_ref[0], preferred_element_type=f32)
    e = jnp.exp2(logits + jnp.concatenate([bias_ref[...]] * group, axis=1))
    p = (e * (1.0 / jnp.sum(e, axis=0, keepdims=True))).astype(bf16)
    p_ref[0] = p
    g = jnp.concatenate([g_ref[:, j * hd : (j + 1) * hd] for j in range(group)], axis=0)
    gv = jnp.dot(p, g, preferred_element_type=f32)
    own_ref[...] = gv[:rows]
    for b in range(back):
        send_refs[b][...] = gv[(b + 1) * rows : (b + 2) * rows].astype(bf16)


def backward_kernel(back, blocks, factor, p_ref, g_ref, u_ref, qs_ref, gain_ref, rows_ref, base_ref, *refs):
    v_refs, refs = refs[:blocks], refs[blocks:]
    k_refs = v_refs[: back + 1]
    gq_ref, own_ref, send_refs, place_ref, held = refs[0], refs[1], refs[2:-2], refs[-2], refs[-1]
    me = lax.axis_index("ctx")
    rows = g_ref.shape[0]
    hd = own_ref.shape[1]
    group = g_ref.shape[1] // hd
    key_count = (back + 1) * rows

    @pl.when(pl.program_id(0) == 0)
    def _():
        upright_tables(gain_ref, rows_ref, base_ref, factor, held)
        slot = lax.broadcasted_iota(jnp.int32, (key_count, rows), 0).astype(f32)
        for s in range(blocks):
            marks = mark_rows(v_refs[s], rows)
            away = me.astype(f32) - marks[:1]
            away = jnp.where(away < 0, away + blocks, away)
            place_ref[:, s * rows : (s + 1) * rows] = (
                (slot == away * rows + marks[1:2]).astype(f32).astype(bf16)
            )

    arrived = jnp.concatenate([r[:rows] for r in v_refs], axis=0)
    values = jnp.dot(place_ref[...], arrived, preferred_element_type=f32).astype(bf16)
    g = jnp.concatenate([g_ref[:, j * hd : (j + 1) * hd] for j in range(group)], axis=0)
    dp = lax.dot_general(values, g, NT, preferred_element_type=f32)
    p = p_ref[0].astype(f32)
    delta = jnp.sum(p * dp, axis=0, keepdims=True)
    ds = (p * (dp - delta)).astype(bf16)
    gk = lax.dot_general(ds, qs_ref[0], NT, preferred_element_type=f32) * math.log(2.0)
    own_ref[...] = gk[:rows]
    for b in range(back):
        send_refs[b][...] = gk[(b + 1) * rows : (b + 2) * rows].astype(bf16)
    keys = jnp.concatenate([r[rows + meta_rows :] for r in k_refs], axis=0)
    gq = jnp.dot(keys.T, ds, preferred_element_type=f32)
    for j in range(group):
        cols = slice(j * rows, (j + 1) * rows)
        dz, u = gq[:, cols], u_ref[0, :, cols].astype(f32)
        inverse = lax.rsqrt(jnp.mean(u * u, axis=0, keepdims=True) + epsilon)
        dn = (dz * held[0] + swap_rows(dz * held[1])) * held[2]
        along = jnp.mean(dn * u, axis=0, keepdims=True) * (inverse * inverse)
        gq_ref[:, j * hd : (j + 1) * hd] = (inverse * (dn - u * along)).astype(bf16).T


def key_back_kernel(k_ref, own_ref, gain_ref, rows_ref, base_ref, *refs):
    got_refs, out_ref = refs[:-1], refs[-1]
    me = lax.axis_index("ctx")
    hd = gain_ref.shape[1]
    cosine, sine = rotation(rows_ref, base_ref, me)
    total = own_ref[...]
    for r in got_refs:
        total = total + r[...].astype(f32)
    for h in range(k_ref.shape[1] // hd):
        cols = slice(h * hd, (h + 1) * hd)
        u = k_ref[:, cols].astype(f32)
        out_ref[:, cols] = norm_rope_back(u, total[:, cols], gain_ref[...], cosine, sine).astype(bf16)


def gate_kernel(*refs):
    pass


def value_sum_kernel(*refs):
    total = refs[0][...]
    for r in refs[1:-1]:
        total = total + r[...].astype(f32)
    refs[-1][...] = total.astype(bf16)


def pair_kernel(own_ref, got_ref, first_ref, *send_refs):
    share = first_ref.shape[0]
    first_ref[...] = own_ref[:share] + got_ref[:share].astype(f32)
    for j, ref in enumerate(send_refs, 1):
        at = slice(j * share, (j + 1) * share)
        ref[...] = (own_ref[at] + got_ref[at].astype(f32)).astype(bf16)


def total_kernel(first_ref, *refs):
    total = first_ref[...]
    for r in refs[:-1]:
        total = total + r[...].astype(f32)
    refs[-1][...] = total * (1.0 / (lax.axis_size("ctx") * lax.axis_size("dp")))


def hidden_grad_kernel(v_ref, w_ref, out_ref):
    out_ref[...] = lax.dot_general(
        v_ref[...], w_ref[...], NT, preferred_element_type=f32
    ).astype(bf16)


def weight_kernel(blocks, *refs):
    h_refs, slab_ref, m_refs = refs[:blocks], refs[blocks], refs[blocks + 1 : 2 * blocks + 1]
    sibling_ref, own_ref = refs[2 * blocks + 1 :]
    rows = h_refs[0].shape[1]
    slot = lax.broadcasted_iota(jnp.int32, (blocks * rows, rows), 0).astype(f32)
    arrival = []
    for s in range(blocks):
        marks = mark_rows(m_refs[s], rows)
        place = (slot == marks[:1] * rows + marks[1:2]).astype(f32).T.astype(bf16)
        arrival.append(jnp.dot(place, slab_ref[...], preferred_element_type=f32).astype(bf16))
    arrival = jnp.concatenate(arrival, axis=0)
    half = sibling_ref.shape[0]
    features = jnp.concatenate([r[...] for r in h_refs], axis=1)
    sibling_ref[...] = jnp.dot(features[:half], arrival, preferred_element_type=f32).astype(bf16)
    own_ref[...] = jnp.dot(features[half:], arrival, preferred_element_type=f32)


def on_device(hidden, queries, key_states, out_grad, w_value, q_gain, k_gain, dest_rows, doc_ids):
    hidden, queries, key_states, out_grad = hidden[0], queries[0], key_states[0], out_grad[0]
    rows, width = hidden.shape
    hd = q_gain.shape[0]
    kv_width = key_states.shape[1]
    q_width = queries.shape[1]
    kv = kv_width // hd
    group = q_width // kv_width
    blocks, dp_count = lax.axis_size("ctx"), lax.axis_size("dp")
    zs = dp_count // 2
    back = blocks // 2
    factor = hd ** (-0.5)
    share = width // (blocks * dp_count)
    spread = group * rows
    key_count = (back + 1) * rows
    message = jax.ShapeDtypeStruct((2 * rows + meta_rows, kv_width), bf16)
    far_message = jax.ShapeDtypeStruct((rows + meta_rows, kv_width), bf16)
    rows_table, base_table = (jnp.asarray(t) for t in rope_constants(rows, blocks, hd))
    q_gain, k_gain = q_gain[None], k_gain[None]

    def behind(array, m):
        return lax.ppermute(array, "ctx", [(i + m, i) for i in range(blocks - m)])

    def around(array, m):
        return lax.ppermute(array, "ctx", [(i, (i + m) % blocks) for i in range(blocks)])

    def call(kernel, out_shape, name, operands, mib, flops=0, nbytes=0, in_specs=None, after=(), **kw):
        if in_specs is None:
            in_specs = [pl.BlockSpec(memory_space=VMEM)] * len(operands)
        return pl.pallas_call(
            ordered(kernel, len(operands), len(after)), out_shape=out_shape, name=name,
            compiler_params=params(mib), cost_estimate=cost(flops, nbytes),
            in_specs=list(in_specs) + [pl.BlockSpec(memory_space=pl.ANY)] * len(after), **kw,
        )(*operands, *after)

    def in_hbm(array):
        return pltpu.with_memory_space_constraint(array, pltpu.HBM)

    def gate(arrays, after, name):
        return pl.pallas_call(
            gate_kernel, name=name, compiler_params=params(1), cost_estimate=cost(0, 0),
            out_shape=[jax.ShapeDtypeStruct(a.shape, a.dtype) for a in arrays],
            in_specs=[pl.BlockSpec(memory_space=pl.ANY)] * (len(arrays) + len(after)),
            out_specs=[pl.BlockSpec(memory_space=pl.ANY)] * len(arrays),
            input_output_aliases={i: i for i in range(len(arrays))},
        )(*arrays, *after)

    def whole(shape):
        return pl.BlockSpec(shape, lambda h: (0,) * len(shape))

    sources = [in_hbm(a) for a in (key_states, doc_ids, dest_rows, k_gain, rows_table, base_table, hidden, w_value)]
    message_own, message_far = call(
        functools.partial(message_kernel, blocks), [message, far_message], "message", sources, 16,
        2 * rows * width * kv_width, 7e6,
        in_specs=[pl.BlockSpec(memory_space=pltpu.HBM)] * 8,
        scratch_shapes=[VMEM(a.shape, a.dtype) for a in sources] + [pltpu.SemaphoreType.DMA((15,))],
    )
    messages = [message_own]
    messages += [around(message_own if m <= back else message_far, m) for m in range(1, blocks)]

    head_cols = pl.BlockSpec((rows, group * hd), lambda h: (0, h))
    head_set = pl.BlockSpec((1, hd, spread), lambda h: (h, 0, 0))
    message_cols = pl.BlockSpec((2 * rows + meta_rows, hd), lambda h: (0, h))
    far_cols = pl.BlockSpec((rows + meta_rows, hd), lambda h: (0, h))
    row_cols = pl.BlockSpec((rows, hd), lambda h: (0, h))
    table_specs = [whole((1, hd)), whole(rows_table.shape), whole(base_table.shape)]
    upright = VMEM((3, hd, rows), f32)

    q_scaled, q_turned = call(
        functools.partial(query_prep_kernel, factor * math.log2(math.e)),
        [jax.ShapeDtypeStruct((kv, hd, spread), bf16)] * 2,
        "query_prep", (queries, q_gain, rows_table, base_table), 8, 0, 4e6, grid=(kv,),
        in_specs=[head_cols] + table_specs, out_specs=[head_set] * 2, scratch_shapes=[upright],
        after=(message_own,),
    )

    if share % 16 == 0:
        features = call(
            functools.partial(feature_kernel, blocks, zs),
            [jax.ShapeDtypeStruct((width // blocks, rows), bf16)] * blocks,
            "features", (in_hbm(hidden),), 8, 0, 6e6,
            in_specs=[pl.BlockSpec(memory_space=pltpu.HBM)], after=(q_scaled,),
            scratch_shapes=[
                VMEM((4, rows, width // 4), bf16),
                VMEM((width, rows), bf16),
                pltpu.SemaphoreType.DMA((4,)),
            ],
        )
    else:
        me, dp = lax.axis_index("ctx"), lax.axis_index("dp")
        turned = hidden.T.reshape(dp_count * blocks, share, rows)
        features = []
        for m in range(blocks):
            places = [
                share_index(j, half, lax.rem(me + m, blocks), dp // 2, dp % 2, zs, blocks)
                for half in range(2)
                for j in range(zs)
            ]
            pieces = [lax.dynamic_index_in_dim(turned, place, axis=0) for place in places]
            features.append(jnp.concatenate(pieces, axis=0).reshape(width // blocks, rows))
    first_features = features[0]
    leaving = gate(features[1:], messages[1 : back + 1], "features_leave")
    features = [first_features] + [around(leaving[m - 1], m) for m in range(1, blocks)]

    attended = call(
        functools.partial(attend_kernel, back),
        [
            jax.ShapeDtypeStruct((kv, key_count, spread), bf16),
            jax.ShapeDtypeStruct((rows, kv_width), f32),
        ]
        + [jax.ShapeDtypeStruct((rows, kv_width), bf16)] * back,
        "attend", (q_scaled, out_grad, *messages[: back + 1]), 16,
        8 * kv * key_count * spread * hd, 5e6, grid=(kv,),
        in_specs=[head_set, head_cols] + [message_cols] * (back + 1),
        out_specs=[pl.BlockSpec((1, key_count, spread), lambda h: (h, 0, 0))]
        + [row_cols] * (back + 1),
        scratch_shapes=[VMEM((key_count, rows), f32)], after=(leaving[0],),
    )
    probabilities, value_total = attended[0], attended[1]
    value_got = [behind(attended[1 + m], m) for m in range(1, back + 1)]

    backed = call(
        functools.partial(backward_kernel, back, blocks, factor),
        [
            jax.ShapeDtypeStruct((rows, q_width), bf16),
            jax.ShapeDtypeStruct((rows, kv_width), f32),
        ]
        + [jax.ShapeDtypeStruct((rows, kv_width), bf16)] * back,
        "backward",
        (
            probabilities, out_grad, q_turned, q_scaled, q_gain, rows_table, base_table,
            *messages,
        ),
        20, 12 * kv * key_count * spread * hd, 7e6, grid=(kv,),
        in_specs=[
            pl.BlockSpec((1, key_count, spread), lambda h: (h, 0, 0)),
            head_cols, head_set, head_set,
        ]
        + table_specs + [message_cols] * (back + 1) + [far_cols] * (blocks - back - 1),
        out_specs=[head_cols] + [row_cols] * (back + 1),
        scratch_shapes=[VMEM((key_count, blocks * rows), bf16), upright],
        after=(value_total,),
    )
    value_grad = call(
        value_sum_kernel, jax.ShapeDtypeStruct((rows, kv_width), bf16), "value_sum",
        (value_total, *value_got), 4, 0, 1e6, after=(backed[1], *features[1:]),
    )
    slab_value_grad = lax.all_gather(value_grad, "ctx", axis=0, tiled=True)

    half = width // blocks // 2
    sibling, own = call(
        functools.partial(weight_kernel, blocks),
        [jax.ShapeDtypeStruct((half, kv_width), bf16), jax.ShapeDtypeStruct((half, kv_width), f32)],
        "weight", (*features, slab_value_grad, *messages), 16, 2 * width * rows * kv_width, 4e6,
    )
    got = lax.ppermute(sibling, "dp", [(d, d ^ 1) for d in range(dp_count)])

    slice_width = width // 4
    hidden_grad = call(
        hidden_grad_kernel, jax.ShapeDtypeStruct((rows, width), bf16),
        "hidden_grad", (value_grad, w_value), 8, 2 * rows * width * kv_width, 7e6,
        grid=(width // slice_width,),
        in_specs=[whole((rows, kv_width)), pl.BlockSpec((slice_width, kv_width), lambda i: (i, 0))],
        out_specs=pl.BlockSpec((rows, slice_width), lambda i: (0, i)),
        after=(),
    )

    pairs = call(
        pair_kernel,
        [jax.ShapeDtypeStruct((share, kv_width), f32)]
        + [jax.ShapeDtypeStruct((share, kv_width), bf16)] * (zs - 1),
        "pair", (own, got), 12, 0, 3e6,
    )
    sums = []
    for j in range(1, zs):
        route = [(z * 2 + c, (z ^ j) * 2 + c) for z in range(zs) for c in range(2)]
        sums.append(lax.ppermute(pairs[j], "dp", route))

    query_grad = backed[0]
    key_leaving = gate(backed[2:], (pairs[0],), "keys_leave")
    key_got = [behind(key_leaving[m - 1], m) for m in range(1, back + 1)]
    weight_grad = call(
        total_kernel, jax.ShapeDtypeStruct((share, kv_width), f32), "total",
        (pairs[0], *sums), 4, 0, 1e6,
    )
    key_grad = call(
        key_back_kernel, jax.ShapeDtypeStruct((rows, kv_width), bf16), "key_back",
        (key_states, backed[1], k_gain, rows_table, base_table, *key_got), 4, 0, 1e6,
    )
    return (hidden_grad[None], query_grad[None], key_grad[None], weight_grad)


def solution(mesh):
    return jax.shard_map(
        on_device,
        mesh=mesh,
        in_specs=(
            P("dp", "ctx", None),
            P("dp", "ctx", None),
            P("dp", "ctx", None),
            P("dp", "ctx", None),
            P(),
            P(),
            P(),
            P("dp", "ctx"),
            P("dp", "ctx"),
        ),
        out_specs=(
            P("dp", "ctx", None),
            P("dp", "ctx", None),
            P("dp", "ctx", None),
            P(("dp", "ctx"), None),
        ),
        check_vma=False,
    )
```

time: 99.8 us -> 70.8 us (0.71)
  the two profiles are of different devices: /device:TPU:20 before, /device:TPU:0 now
where the time goes in v2:
time: 70.8 us; the launch traced here: 69.9 us
  Pallas kernels  23.1 us (33%)
  starting transfers between devices  19.5 us (28%)
  waiting for transfers between devices  17.2 us (24%)
  blocking collectives  9.17 us (13%)
  between operations  0.85 us (1%)
    pallas_call x11, Pallas kernels, call(): pl.pallas_call(ordered(kernel, len(operands), len(after)), out_shape=out_...  23.1 us
    ppermute x6, starting transfers between devices, around(): lax.ppermute(array, 'ctx', [(i, (i + m) % blocks) for i in range(blocks)])  9.72 us
    all_gather x1, blocking collectives, on_device(): slab_value_grad = lax.all_gather(value_grad, 'ctx', axis=0, tiled=True)  9.17 us
    ppermute x4, waiting for transfers between devices, behind(): return lax.ppermute(array, 'ctx', [(i + m, i) for i in range(blocks - m)])  7.38 us
    ppermute x6, waiting for transfers between devices, around(): lax.ppermute(array, 'ctx', [(i, (i + m) % blocks) for i in range(blocks)])  6.59 us
    ppermute x4, starting transfers between devices, behind(): return lax.ppermute(array, 'ctx', [(i + m, i) for i in range(blocks - m)])  5.29 us
    ppermute x3, starting transfers between devices, on_device(): sums.append(lax.ppermute(pairs[j], 'dp', route))  4.45 us
    ppermute x1, waiting for transfers between devices, on_device(): got = lax.ppermute(sibling, 'dp', [(d, d ^ 1) for d in range(dp_count)])  2.08 us
  transfers between devices with their start and end apart: 14, of which 6 were waited for; matrix products, arithmetic and copies ran while one was open for 0% of the time, Pallas kernels for 25%

profile of v2, /device:TPU:0, one launch (start us, length us, event | category | flops | bytes accessed | tf_op | source)
XLA Modules:
  0.0 69.9 jit_solution(10467128115489441257)
XLA Ops:
  0.6 0.0 copy-start
  0.6 0.0 copy-start.1
  0.7 0.0 copy-start.3
  0.7 0.0 copy-start.5
  0.7 3.5 %message.1 = (bf16[272,512]{1,0:T(8,128)(2,1)S(1)}, bf16[144,512]{1,0:T(8,128)(2,1)S(1)}) custom-call(bf16[128,512]{1,0:T(8,128)(2,1)} %bitcast.12, s32[1,128]{1,0:T(1,128)} %refs_1_.2, s32[1,128]{1,0:T(1,128)} %refs_2_.2, f32[1,128]{1,0:T(1,128)} %bitcast.14, f32[2,128,128]{2,1,0:T(8,128)} %constant.4.clone.refs_4_.refs_2_.refs_5_.refs_3_, ...), custom_call_target="tpu_custom_call" | custom-call | flops 671088640 | bytes 7000000 | tf_op jit(solution)/shard_map/message/pallas_call | solution.py:356
  4.2 3.0 %collective-permute-start.1 = (bf16[272,512]{1,0:T(8,128)(2,1)S(1)}, bf16[272,512]{1,0:T(8,128)(2,1)S(1)}, u32[]{:S(2)}, u32[]{:S(2)}) collective-permute-start(bf16[272,512]{1,0:T(8,128)(2,1)S(1)} %get-tuple-element.31.refs_4_.refs_2_.refs_7_.refs_5_), channel_id=1, source_target_pairs={{0,2},{1,3},{2,0},{3,1},{4,6},{5,7},{6,4},{7,5},{8,10},{9,11},{10,... | collective-permute-start | bytes 835592 | tf_op jit(solution)/shard_map/ppermute | solution.py:351
  7.2 1.5 %collective-permute-start = (bf16[272,512]{1,0:T(8,128)(2,1)S(1)}, bf16[272,512]{1,0:T(8,128)(2,1)S(1)}, u32[]{:S(2)}, u32[]{:S(2)}) collective-permute-start(bf16[272,512]{1,0:T(8,128)(2,1)S(1)} %get-tuple-element.31.refs_4_.refs_2_.refs_7_.refs_5_), channel_id=1, source_target_pairs={{0,1},{1,2},{2,3},{3,0},{4,5},{5,6},{6,7},{7,4},{8,9},{9,10},{10,1... | collective-permute-start | bytes 835592 | tf_op jit(solution)/shard_map/ppermute | solution.py:351
  8.7 1.4 %collective-permute-start.4 = (bf16[144,512]{1,0:T(8,128)(2,1)S(1)}, bf16[144,512]{1,0:T(8,128)(2,1)S(1)}, u32[]{:S(2)}, u32[]{:S(2)}) collective-permute-start(bf16[144,512]{1,0:T(8,128)(2,1)S(1)} %get-tuple-element.42), channel_id=1, source_target_pairs={{0,3},{1,0},{2,1},{3,2},{4,7},{5,4},{6,5},{7,6},{8,11},{9,8},{10,9... | collective-permute-start | bytes 442376 | tf_op jit(solution)/shard_map/ppermute | solution.py:351
  10.2 0.0 copy-done
  10.2 0.0 copy-done.1
  10.2 0.0 copy-done.3
  10.2 0.0 copy-done.5
  10.2 1.4 %query_prep.1 = (bf16[4,128,1024]{2,1,0:T(8,128)(2,1)S(1)}, bf16[4,128,1024]{2,1,0:T(8,128)(2,1)S(1)}) custom-call(bf16[128,4096]{1,0:T(8,128)(2,1)S(1)} %bitcast.11, f32[1,128]{1,0:T(1,128)S(1)} %bitcast.16, f32[2,128,128]{2,1,0:T(8,128)S(1)} %copy-done, f32[2,4,128]{2,1,0:T(4,128)S(1)} %copy-done.3, ...), custom_call_target="tpu_custom_call" | custom-call | bytes 4000000 | tf_op jit(solution)/shard_map/query_prep/pallas_call | solution.py:356
  11.6 1.7 %features.1 = (bf16[1280,128]{1,0:T(8,128)(2,1)S(1)}, bf16[1280,128]{1,0:T(8,128)(2,1)S(1)}, bf16[1280,128]{1,0:T(8,128)(2,1)S(1)}, bf16[1280,128]{1,0:T(8,128)(2,1)S(1)}) custom-call(bf16[128,5120]{1,0:T(8,128)(2,1)} %bitcast.21, bf16[4,128,1024]{2,1,0:T(8,128)(2,1)S(1)} %get-tuple-element.32.refs_1_.refs_0_.refs_3_), custom_call_target="tpu_custom_call" | custom-call | bytes 6000000 | tf_op jit(solution)/shard_map/features/pallas_call | solution.py:356
  13.3 0.0 copy-start.6
  13.3 6.6 %collective-permute-done.1.refs_4_.refs_9_.refs_7_ = bf16[272,512]{1,0:T(8,128)(2,1)S(1)} collective-permute-done((bf16[272,512]{1,0:T(8,128)(2,1)S(1)}, bf16[272,512]{1,0:T(8,128)(2,1)S(1)}, u32[]{:S(2)}, u32[]{:S(2)}) %collective-permute-start.1) | collective-permute-done | bytes 278560 | tf_op jit(solution)/shard_map/ppermute | solution.py:351
  19.9 0.0 collective-permute-done.refs_3_.refs_8_.refs_6_
  19.9 1.7 %collective-permute-start.6 = (bf16[1280,128]{1,0:T(8,128)(2,1)S(1)}, bf16[1280,128]{1,0:T(8,128)(2,1)S(1)}, u32[]{:S(2)}, u32[]{:S(2)}) collective-permute-start(bf16[1280,128]{1,0:T(8,128)(2,1)S(1)} %get-tuple-element.44), channel_id=1, source_target_pairs={{0,2},{1,3},{2,0},{3,1},{4,6},{5,7},{6,4},{7,5},{8,10},{9,11},{10,... | collective-permute-start | bytes 983048 | tf_op jit(solution)/shard_map/ppermute | solution.py:351
  21.6 0.0 collective-permute-start.7
  21.6 2.0 %collective-permute-start.5 = (bf16[1280,128]{1,0:T(8,128)(2,1)S(1)}, bf16[1280,128]{1,0:T(8,128)(2,1)S(1)}, u32[]{:S(2)}, u32[]{:S(2)}) collective-permute-start(bf16[1280,128]{1,0:T(8,128)(2,1)S(1)} %get-tuple-element.36.refs_5_), channel_id=1, source_target_pairs={{0,1},{1,2},{2,3},{3,0},{4,5},{5,6},{6,7},{7,4},{8,9},{9,10},{10,1... | collective-permute-start | bytes 983048 | tf_op jit(solution)/shard_map/ppermute | solution.py:351
  23.6 0.0 copy-done.6
  23.6 3.8 %attend.1 = (bf16[4,384,1024]{2,1,0:T(8,128)(2,1)S(1)}, f32[128,512]{1,0:T(8,128)S(1)}, bf16[128,512]{1,0:T(8,128)(2,1)S(1)}, bf16[128,512]{1,0:T(8,128)(2,1)S(1)}) custom-call(bf16[4,128,1024]{2,1,0:T(8,128)(2,1)S(1)} %get-tuple-element.32.refs_1_.refs_0_.refs_3_, bf16[128,4096]{1,0:T(8,128)(2,1)S(1)} %bitcast.18, ...), custom_call_target="tpu_custom_call" | custom-call | flops 1610612736 | bytes 5000000 | tf_op jit(solution)/shard_map/attend/pallas_call | solution.py:356
  27.5 1.3 %collective-permute-start.2 = (bf16[128,512]{1,0:T(8,128)(2,1)S(1)}, bf16[128,512]{1,0:T(8,128)(2,1)S(1)}, u32[]{:S(2)}, u32[]{:S(2)}) collective-permute-start(bf16[128,512]{1,0:T(8,128)(2,1)S(1)} %get-tuple-element.38), channel_id=1, source_target_pairs={{1,0},{2,1},{3,2},{5,4},{6,5},{7,6},{9,8},{10,9},{11,10},{13,12},{... | collective-permute-start | bytes 393224 | tf_op jit(solution)/shard_map/ppermute | solution.py:348
  28.8 0.0 collective-permute-done.4.refs_10_.refs_8_
  28.8 1.3 %collective-permute-start.3 = (bf16[128,512]{1,0:T(8,128)(2,1)S(1)}, bf16[128,512]{1,0:T(8,128)(2,1)S(1)}, u32[]{:S(2)}, u32[]{:S(2)}) collective-permute-start(bf16[128,512]{1,0:T(8,128)(2,1)S(1)} %get-tuple-element.39), channel_id=1, source_target_pairs={{2,0},{3,1},{6,4},{7,5},{10,8},{11,9},{14,12},{15,13},{18,16},{19,... | collective-permute-start | bytes 393224 | tf_op jit(solution)/shard_map/ppermute | solution.py:348
  30.1 0.0 slice-start
  30.1 0.0 slice-start.1
  30.1 6.2 %backward.1 = (bf16[128,4096]{1,0:T(8,128)(2,1)}, f32[128,512]{1,0:T(8,128)S(1)}, bf16[128,512]{1,0:T(8,128)(2,1)S(1)}, bf16[128,512]{1,0:T(8,128)(2,1)S(1)}) custom-call(bf16[4,384,1024]{2,1,0:T(8,128)(2,1)S(1)} %get-tuple-element.40.refs_0_, bf16[128,4096]{1,0:T(8,128)(2,1)S(1)} %bitcast.19, bf16[4,128,1024]{2,1,0:T(8,128)(2,1)S(1)} %get-tuple-element.41.refs_2_, ...), custom_call_target="tpu_custom_call" | custom-call | flops 2415919104 | bytes 7000000 | tf_op jit(solution)/shard_map/backward/pallas_call | solution.py:356
  36.3 3.5 %collective-permute-done.2.refs_1_ = bf16[128,512]{1,0:T(8,128)(2,1)S(1)} collective-permute-done((bf16[128,512]{1,0:T(8,128)(2,1)S(1)}, bf16[128,512]{1,0:T(8,128)(2,1)S(1)}, u32[]{:S(2)}, u32[]{:S(2)}) %collective-permute-start.2) | collective-permute-done | bytes 131104 | tf_op jit(solution)/shard_map/ppermute | solution.py:348
  39.8 0.0 collective-permute-done.3.refs_2_
  39.8 0.0 collective-permute-done.6.refs_5_.refs_2_
  39.8 0.0 collective-permute-done.7.refs_6_.refs_3_
  39.8 0.0 collective-permute-done.5.refs_4_.refs_1_
  39.8 0.1 value_sum.1.refs_0_
  39.9 9.2 %all_gather.3.refs_4_ = bf16[512,512]{1,0:T(8,128)(2,1)S(1)} all-gather(bf16[128,512]{1,0:T(8,128)(2,1)S(1)} %value_sum.1.refs_0_), channel_id=1, replica_groups=mesh['dp'=8,'ctx'=4] {'ctx'}, dimensions={0}, use_global_device_ids=true | all-gather | bytes 655360 | tf_op jit(solution)/shard_map/all_gather | solution.py:474
  49.1 1.2 %weight.1 = (bf16[640,512]{1,0:T(8,128)(2,1)S(1)}, f32[640,512]{1,0:T(8,128)S(1)}) custom-call(bf16[1280,128]{1,0:T(8,128)(2,1)S(1)} %get-tuple-element.49.refs_0_, bf16[1280,128]{1,0:T(8,128)(2,1)S(1)} %collective-permute-done.5.refs_4_.refs_1_, bf16[1280,128]{1,0:T(8,128)(2,1)S(1)} %collective-permute-done.6.refs_5_.refs_2_, ...), custom_call_target="tpu_custom_call" | custom-call | flops 671088640 | bytes 4000000 | tf_op jit(solution)/shard_map/weight/pallas_call | solution.py:356
  50.2 0.1 collective-permute-start.8
  50.3 2.1 %collective-permute-done.8.refs_1_ = bf16[640,512]{1,0:T(8,128)(2,1)S(1)} collective-permute-done((bf16[640,512]{1,0:T(8,128)(2,1)S(1)}, bf16[640,512]{1,0:T(8,128)(2,1)S(1)}, u32[]{:S(2)}, u32[]{:S(2)}) %collective-permute-start.8) | collective-permute-done | bytes 655392 | tf_op jit(solution)/shard_map/ppermute | solution.py:482
  52.4 0.1 pair.1
  52.6 1.5 %collective-permute-start.11 = (bf16[160,512]{1,0:T(8,128)(2,1)S(1)}, bf16[160,512]{1,0:T(8,128)(2,1)S(1)}, u32[]{:S(2)}, u32[]{:S(2)}) collective-permute-start(bf16[160,512]{1,0:T(8,128)(2,1)S(1)} %get-tuple-element.55), channel_id=1, source_target_pairs={{0,8},{4,12},{8,0},{12,4},{16,24},{20,28},{24,16},{28,20},{1,9},{5... | collective-permute-start | bytes 491528 | tf_op jit(solution)/shard_map/ppermute | solution.py:503
  54.0 2.6 %collective-permute-start.12 = (bf16[160,512]{1,0:T(8,128)(2,1)S(1)}, bf16[160,512]{1,0:T(8,128)(2,1)S(1)}, u32[]{:S(2)}, u32[]{:S(2)}) collective-permute-start(bf16[160,512]{1,0:T(8,128)(2,1)S(1)} %get-tuple-element.56), channel_id=1, source_target_pairs={{0,16},{4,20},{8,24},{12,28},{16,0},{20,4},{24,8},{28,12},{1,17},{... | collective-permute-start | bytes 491528 | tf_op jit(solution)/shard_map/ppermute | solution.py:503
  56.6 0.4 collective-permute-start.13
  57.0 1.3 %collective-permute-start.9 = (bf16[128,512]{1,0:T(8,128)(2,1)S(1)}, bf16[128,512]{1,0:T(8,128)(2,1)S(1)}, u32[]{:S(2)}, u32[]{:S(2)}) collective-permute-start(bf16[128,512]{1,0:T(8,128)(2,1)S(1)} %get-tuple-element.53), channel_id=1, source_target_pairs={{1,0},{2,1},{3,2},{5,4},{6,5},{7,6},{9,8},{10,9},{11,10},{13,12},{... | collective-permute-start | bytes 393224 | tf_op jit(solution)/shard_map/ppermute | solution.py:348
  58.3 0.0 copy-start.2
  58.3 0.0 copy-start.4
  58.3 1.4 %collective-permute-start.10 = (bf16[128,512]{1,0:T(8,128)(2,1)S(1)}, bf16[128,512]{1,0:T(8,128)(2,1)S(1)}, u32[]{:S(2)}, u32[]{:S(2)}) collective-permute-start(bf16[128,512]{1,0:T(8,128)(2,1)S(1)} %get-tuple-element.54), channel_id=1, source_target_pairs={{2,0},{3,1},{6,4},{7,5},{10,8},{11,9},{14,12},{15,13},{18,16},{19,... | collective-permute-start | bytes 393224 | tf_op jit(solution)/shard_map/ppermute | solution.py:348
  59.8 0.0 slice-done
  59.8 0.0 slice-done.1
  59.8 3.1 %hidden_grad.1 = bf16[128,5120]{1,0:T(8,128)(2,1)} custom-call(bf16[128,512]{1,0:T(8,128)(2,1)S(1)} %value_sum.1.refs_0_, bf16[5120,512]{1,0:T(8,128)(2,1)S(1)} %bitcast.10), custom_call_target="tpu_custom_call" | custom-call | flops 671088640 | bytes 7000000 | tf_op jit(solution)/shard_map/hidden_grad/pallas_call | solution.py:356
  62.9 1.0 %collective-permute-done.9.refs_5_ = bf16[128,512]{1,0:T(8,128)(2,1)S(1)} collective-permute-done((bf16[128,512]{1,0:T(8,128)(2,1)S(1)}, bf16[128,512]{1,0:T(8,128)(2,1)S(1)}, u32[]{:S(2)}, u32[]{:S(2)}) %collective-permute-start.9) | collective-permute-done | bytes 131104 | tf_op jit(solution)/shard_map/ppermute | solution.py:348
  63.9 2.8 %collective-permute-done.10.refs_6_ = bf16[128,512]{1,0:T(8,128)(2,1)S(1)} collective-permute-done((bf16[128,512]{1,0:T(8,128)(2,1)S(1)}, bf16[128,512]{1,0:T(8,128)(2,1)S(1)}, u32[]{:S(2)}, u32[]{:S(2)}) %collective-permute-start.10) | collective-permute-done | bytes 131104 | tf_op jit(solution)/shard_map/ppermute | solution.py:348
  66.8 0.0 copy-done.2
  66.8 0.0 copy-done.4
  66.8 1.2 %key_back.1 = bf16[128,512]{1,0:T(8,128)(2,1)} custom-call(bf16[128,512]{1,0:T(8,128)(2,1)S(1)} %bitcast.13, f32[128,512]{1,0:T(8,128)S(1)} %get-tuple-element.43.refs_3_.refs_1_, f32[1,128]{1,0:T(1,128)S(1)} %bitcast.15, f32[2,128,128]{2,1,0:T(8,128)S(1)} %copy-done, f32[2,4,128]{2,1,0:T(4,128)S(1)} %copy-done.3, ...), custom_call_target="tpu_custom_call" | custom-call | bytes 1000000 | tf_op jit(solution)/shard_map/key_back/pallas_call | solution.py:356
  67.9 0.0 collective-permute-done.11.refs_1_
  67.9 1.1 %collective-permute-done.12.refs_2_ = bf16[160,512]{1,0:T(8,128)(2,1)S(1)} collective-permute-done((bf16[160,512]{1,0:T(8,128)(2,1)S(1)}, bf16[160,512]{1,0:T(8,128)(2,1)S(1)}, u32[]{:S(2)}, u32[]{:S(2)}) %collective-permute-start.12) | collective-permute-done | bytes 163872 | tf_op jit(solution)/shard_map/ppermute | solution.py:503
  69.0 0.0 collective-permute-done.13.refs_3_
  69.0 0.8 %total.1 = f32[160,512]{1,0:T(8,128)} custom-call(f32[160,512]{1,0:T(8,128)S(1)} %get-tuple-element.52.refs_2_.refs_0_, bf16[160,512]{1,0:T(8,128)(2,1)S(1)} %collective-permute-done.11.refs_1_, bf16[160,512]{1,0:T(8,128)(2,1)S(1)} %collective-permute-done.12.refs_2_, bf16[160,512]{1,0:T(8,128)(2,1)S(1)} %collective-permute-done.13.refs_3_), custom_call_target="tpu_custom_call" | custom-call | bytes 1000000 | tf_op jit(solution)/shard_map/total/pallas_call | solution.py:356
  (3 shorter events, 0.0 us)
Async XLA Ops:
  0.6 9.5 %copy-start = (f32[2,128,128]{2,1,0:T(8,128)S(1)}, f32[2,128,128]{2,1,0:T(8,128)}, u32[]{:S(2)}) copy-start(f32[2,128,128]{2,1,0:T(8,128)} %constant.4.clone.refs_4_.refs_2_.refs_5_.refs_3_) | copy-start | bytes 393220
  0.6 9.5 %copy-start.1 = (bf16[1,128,4096]{2,1,0:T(8,128)(2,1)S(1)}, bf16[1,128,4096]{2,1,0:T(8,128)(2,1)}, u32[]{:S(2)}) copy-start(bf16[1,128,4096]{2,1,0:T(8,128)(2,1)} %param.12) | copy-start | bytes 3145732
  0.7 9.5 %copy-start.3 = (f32[2,4,128]{2,1,0:T(4,128)S(1)}, f32[2,4,128]{2,1,0:T(4,128)}, u32[]{:S(2)}) copy-start(f32[2,4,128]{2,1,0:T(4,128)} %constant.5.clone.refs_5_.refs_3_.refs_6_.refs_4_) | copy-start | bytes 12292
  0.7 9.5 %copy-start.5 = (f32[128]{0:T(128)S(1)}, f32[128]{0:T(128)}, u32[]{:S(2)}) copy-start(f32[128]{0:T(128)} %param.16) | copy-start | bytes 1540
  4.2 15.7 %collective-permute-start.1 = (bf16[272,512]{1,0:T(8,128)(2,1)S(1)}, bf16[272,512]{1,0:T(8,128)(2,1)S(1)}, u32[]{:S(2)}, u32[]{:S(2)}) collective-permute-start(bf16[272,512]{1,0:T(8,128)(2,1)S(1)} %get-tuple-element.31.refs_4_.refs_2_.refs_7_.refs_5_), channel_id=1, source_target_pairs={{0,2},{1,3},{2,0},{3,1},{4,6},{5,7},{6,4},{7,5},{8,10},{9,11},{10,... | collective-permute-start | bytes 835592 | tf_op jit(solution)/shard_map/ppermute | solution.py:351
  7.2 12.6 %collective-permute-start = (bf16[272,512]{1,0:T(8,128)(2,1)S(1)}, bf16[272,512]{1,0:T(8,128)(2,1)S(1)}, u32[]{:S(2)}, u32[]{:S(2)}) collective-permute-start(bf16[272,512]{1,0:T(8,128)(2,1)S(1)} %get-tuple-element.31.refs_4_.refs_2_.refs_7_.refs_5_), channel_id=1, source_target_pairs={{0,1},{1,2},{2,3},{3,0},{4,5},{5,6},{6,7},{7,4},{8,9},{9,10},{10,1... | collective-permute-start | bytes 835592 | tf_op jit(solution)/shard_map/ppermute | solution.py:351
  8.7 20.1 %collective-permute-start.4 = (bf16[144,512]{1,0:T(8,128)(2,1)S(1)}, bf16[144,512]{1,0:T(8,128)(2,1)S(1)}, u32[]{:S(2)}, u32[]{:S(2)}) collective-permute-start(bf16[144,512]{1,0:T(8,128)(2,1)S(1)} %get-tuple-element.42), channel_id=1, source_target_pairs={{0,3},{1,0},{2,1},{3,2},{4,7},{5,4},{6,5},{7,6},{8,11},{9,8},{10,9... | collective-permute-start | bytes 442376 | tf_op jit(solution)/shard_map/ppermute | solution.py:351
  13.3 10.4 %copy-start.6 = (bf16[1,128,4096]{2,1,0:T(8,128)(2,1)S(1)}, bf16[1,128,4096]{2,1,0:T(8,128)(2,1)}, u32[]{:S(2)}) copy-start(bf16[1,128,4096]{2,1,0:T(8,128)(2,1)} %param.14) | copy-start | bytes 3145732
  19.9 19.9 %collective-permute-start.6 = (bf16[1280,128]{1,0:T(8,128)(2,1)S(1)}, bf16[1280,128]{1,0:T(8,128)(2,1)S(1)}, u32[]{:S(2)}, u32[]{:S(2)}) collective-permute-start(bf16[1280,128]{1,0:T(8,128)(2,1)S(1)} %get-tuple-element.44), channel_id=1, source_target_pairs={{0,2},{1,3},{2,0},{3,1},{4,6},{5,7},{6,4},{7,5},{8,10},{9,11},{10,... | collective-permute-start | bytes 983048 | tf_op jit(solution)/shard_map/ppermute | solution.py:351
  21.6 18.2 %collective-permute-start.7 = (bf16[1280,128]{1,0:T(8,128)(2,1)S(1)}, bf16[1280,128]{1,0:T(8,128)(2,1)S(1)}, u32[]{:S(2)}, u32[]{:S(2)}) collective-permute-start(bf16[1280,128]{1,0:T(8,128)(2,1)S(1)} %get-tuple-element.45), channel_id=1, source_target_pairs={{0,3},{1,0},{2,1},{3,2},{4,7},{5,4},{6,5},{7,6},{8,11},{9,8},{10,9... | collective-permute-start | bytes 983048 | tf_op jit(solution)/shard_map/ppermute | solution.py:351
  21.6 18.2 %collective-permute-start.5 = (bf16[1280,128]{1,0:T(8,128)(2,1)S(1)}, bf16[1280,128]{1,0:T(8,128)(2,1)S(1)}, u32[]{:S(2)}, u32[]{:S(2)}) collective-permute-start(bf16[1280,128]{1,0:T(8,128)(2,1)S(1)} %get-tuple-element.36.refs_5_), channel_id=1, source_target_pairs={{0,1},{1,2},{2,3},{3,0},{4,5},{5,6},{6,7},{7,4},{8,9},{9,10},{10,1... | collective-permute-start | bytes 983048 | tf_op jit(solution)/shard_map/ppermute | solution.py:351
  27.5 12.3 %collective-permute-start.2 = (bf16[128,512]{1,0:T(8,128)(2,1)S(1)}, bf16[128,512]{1,0:T(8,128)(2,1)S(1)}, u32[]{:S(2)}, u32[]{:S(2)}) collective-permute-start(bf16[128,512]{1,0:T(8,128)(2,1)S(1)} %get-tuple-element.38), channel_id=1, source_target_pairs={{1,0},{2,1},{3,2},{5,4},{6,5},{7,6},{9,8},{10,9},{11,10},{13,12},{... | collective-permute-start | bytes 393224 | tf_op jit(solution)/shard_map/ppermute | solution.py:348
  28.8 11.0 %collective-permute-start.3 = (bf16[128,512]{1,0:T(8,128)(2,1)S(1)}, bf16[128,512]{1,0:T(8,128)(2,1)S(1)}, u32[]{:S(2)}, u32[]{:S(2)}) collective-permute-start(bf16[128,512]{1,0:T(8,128)(2,1)S(1)} %get-tuple-element.39), channel_id=1, source_target_pairs={{2,0},{3,1},{6,4},{7,5},{10,8},{11,9},{14,12},{15,13},{18,16},{19,... | collective-permute-start | bytes 393224 | tf_op jit(solution)/shard_map/ppermute | solution.py:348
  30.1 29.7 %slice-start = ((s8[5242880]{0:T(1024)(128)(4,1)}), s8[4194304]{0:T(1024)(128)(4,1)S(1)}, s32[]{:S(2)}) async-start(s8[5242880]{0:T(1024)(128)(4,1)} %bitcast.9), calls=%async_computation | async-start | bytes 8388608
  30.1 29.7 %slice-start.1 = ((s8[5242880]{0:T(1024)(128)(4,1)}), s8[1048576]{0:T(1024)(128)(4,1)S(1)}, s32[]{:S(2)}) async-start(s8[5242880]{0:T(1024)(128)(4,1)} %bitcast.9), calls=%async_computation.1 | async-start | bytes 2097152
  50.2 2.2 %collective-permute-start.8 = (bf16[640,512]{1,0:T(8,128)(2,1)S(1)}, bf16[640,512]{1,0:T(8,128)(2,1)S(1)}, u32[]{:S(2)}, u32[]{:S(2)}) collective-permute-start(bf16[640,512]{1,0:T(8,128)(2,1)S(1)} %get-tuple-element.51), channel_id=1, source_target_pairs={{0,4},{4,0},{8,12},{12,8},{16,20},{20,16},{24,28},{28,24},{1,5},{5... | collective-permute-start | bytes 1966088 | tf_op jit(solution)/shard_map/ppermute | solution.py:482
  52.6 15.4 %collective-permute-start.11 = (bf16[160,512]{1,0:T(8,128)(2,1)S(1)}, bf16[160,512]{1,0:T(8,128)(2,1)S(1)}, u32[]{:S(2)}, u32[]{:S(2)}) collective-permute-start(bf16[160,512]{1,0:T(8,128)(2,1)S(1)} %get-tuple-element.55), channel_id=1, source_target_pairs={{0,8},{4,12},{8,0},{12,4},{16,24},{20,28},{24,16},{28,20},{1,9},{5... | collective-permute-start | bytes 491528 | tf_op jit(solution)/shard_map/ppermute | solution.py:503
  54.0 15.0 %collective-permute-start.12 = (bf16[160,512]{1,0:T(8,128)(2,1)S(1)}, bf16[160,512]{1,0:T(8,128)(2,1)S(1)}, u32[]{:S(2)}, u32[]{:S(2)}) collective-permute-start(bf16[160,512]{1,0:T(8,128)(2,1)S(1)} %get-tuple-element.56), channel_id=1, source_target_pairs={{0,16},{4,20},{8,24},{12,28},{16,0},{20,4},{24,8},{28,12},{1,17},{... | collective-permute-start | bytes 491528 | tf_op jit(solution)/shard_map/ppermute | solution.py:503
  56.6 12.4 %collective-permute-start.13 = (bf16[160,512]{1,0:T(8,128)(2,1)S(1)}, bf16[160,512]{1,0:T(8,128)(2,1)S(1)}, u32[]{:S(2)}, u32[]{:S(2)}) collective-permute-start(bf16[160,512]{1,0:T(8,128)(2,1)S(1)} %get-tuple-element.57), channel_id=1, source_target_pairs={{0,24},{4,28},{8,16},{12,20},{16,8},{20,12},{24,0},{28,4},{1,25},{... | collective-permute-start | bytes 491528 | tf_op jit(solution)/shard_map/ppermute | solution.py:503
  57.0 6.9 %collective-permute-start.9 = (bf16[128,512]{1,0:T(8,128)(2,1)S(1)}, bf16[128,512]{1,0:T(8,128)(2,1)S(1)}, u32[]{:S(2)}, u32[]{:S(2)}) collective-permute-start(bf16[128,512]{1,0:T(8,128)(2,1)S(1)} %get-tuple-element.53), channel_id=1, source_target_pairs={{1,0},{2,1},{3,2},{5,4},{6,5},{7,6},{9,8},{10,9},{11,10},{13,12},{... | collective-permute-start | bytes 393224 | tf_op jit(solution)/shard_map/ppermute | solution.py:348
  58.3 8.5 %copy-start.2 = (bf16[1,128,512]{2,1,0:T(8,128)(2,1)S(1)}, bf16[1,128,512]{2,1,0:T(8,128)(2,1)}, u32[]{:S(2)}) copy-start(bf16[1,128,512]{2,1,0:T(8,128)(2,1)} %param.13) | copy-start | bytes 393220
  58.3 8.4 %copy-start.4 = (f32[128]{0:T(128)S(1)}, f32[128]{0:T(128)}, u32[]{:S(2)}) copy-start(f32[128]{0:T(128)} %param.17) | copy-start | bytes 1540
  58.3 8.4 %collective-permute-start.10 = (bf16[128,512]{1,0:T(8,128)(2,1)S(1)}, bf16[128,512]{1,0:T(8,128)(2,1)S(1)}, u32[]{:S(2)}, u32[]{:S(2)}) collective-permute-start(bf16[128,512]{1,0:T(8,128)(2,1)S(1)} %get-tuple-element.54), channel_id=1, source_target_pairs={{2,0},{3,1},{6,4},{7,5},{10,8},{11,9},{14,12},{15,13},{18,16},{19,... | collective-permute-start | bytes 393224 | tf_op jit(solution)/shard_map/ppermute | solution.py:348

commit v3 on v2

--- a/solution.py
+++ b/solution.py
@@ -70,49 +70,64 @@
     return inverse * (dn - u * along)
 
 
-def message_kernel(blocks, *refs):
-    sources, (out_ref, far_ref, *held, sems) = refs[:8], refs[8:]
+def key_message_kernel(*refs):
+    sources, (out_ref, *held, sems) = refs[:5], refs[5:]
     me = lax.axis_index("ctx")
-    w_held, h_held = held[-1], held[-2]
-    rows, width = h_held.shape
-    parts = 8
-    part = width // parts
-    copies = [pltpu.make_async_copy(a, b, sems.at[i]) for i, (a, b) in enumerate(zip(sources[:7], held))]
-    for i in range(parts):
-        piece = pl.ds(i * part, part)
-        copies.append(
-            pltpu.make_async_copy(sources[7].at[piece], w_held.at[piece], sems.at[7 + i])
-        )
+    copies = [pltpu.make_async_copy(a, b, sems.at[i]) for i, (a, b) in enumerate(zip(sources, held))]
     for copy in copies:
         copy.start()
-    for copy in copies[:6]:
+    for copy in copies:
         copy.wait()
-    k_ref, doc_ref, dest_ref, gain_ref, rows_ref, base_ref = held[:6]
-    kv_width = k_ref.shape[1]
+    k_ref, doc_ref, gain_ref, rows_ref, base_ref = held
+    rows, kv_width = k_ref.shape
     hd = gain_ref.shape[1]
     cosine, sine = rotation(rows_ref, base_ref, me)
+    marks = jnp.broadcast_to((doc_ref[...] + 1).astype(f32), (meta_rows, rows)).astype(bf16)
+    for h in range(kv_width // hd):
+        cols = slice(h * hd, (h + 1) * hd)
+        u = k_ref[:, cols].astype(f32)
+        out_ref[:rows, cols] = norm_rope(u, gain_ref[...], cosine, sine).astype(bf16)
+        out_ref[rows:, cols] = marks
+
+
+def place_marks(dest_ref, blocks):
+    rows = dest_ref.shape[1]
     dest = jnp.broadcast_to(dest_ref[...], (meta_rows, rows))
     block = jnp.zeros_like(dest)
     for j in range(1, blocks):
         block = block + (dest >= j * rows).astype(jnp.int32)
     which = lax.broadcasted_iota(jnp.int32, dest.shape, 0)
-    marks = jnp.where(which == 0, block, dest - block * rows)
-    marks = jnp.where(which == 2, doc_ref[...] + 1, marks).astype(f32).astype(bf16)
-    for h in range(kv_width // hd):
-        cols = slice(h * hd, (h + 1) * hd)
-        u = k_ref[:, cols].astype(f32)
-        out_ref[rows + meta_rows :, cols] = norm_rope(u, gain_ref[...], cosine, sine).astype(bf16)
-        out_ref[rows : rows + meta_rows, cols] = marks
-        far_ref[rows:, cols] = marks
-    copies[6].wait()
+    return jnp.where(which == 0, block, dest - block * rows).astype(f32).astype(bf16)
+
+
+def marks_kernel(blocks):
+    def body(dest_ref, out_ref):
+        out_ref[...] = place_marks(dest_ref, blocks)
+
+    return body
+
+
+def value_kernel(*refs):
+    sources, (out_ref, h_held, w_held, sems) = refs[:2], refs[2:]
+    rows, width = h_held.shape
+    parts = 8
+    part = width // parts
+    copies = [pltpu.make_async_copy(sources[0], h_held, sems.at[0])]
+    for i in range(parts):
+        piece = pl.ds(i * part, part)
+        copies.append(
+            pltpu.make_async_copy(sources[1].at[piece], w_held.at[piece], sems.at[1 + i])
+        )
+    for copy in copies:
+        copy.start()
+    copies[0].wait()
     total = None
     for i in range(parts):
-        copies[7 + i].wait()
+        copies[1 + i].wait()
         piece = slice(i * part, (i + 1) * part)
         product = jnp.dot(h_held[:, piece], w_held[piece], preferred_element_type=f32)
         total = product if total is None else total + product
-    out_ref[:rows] = total.astype(bf16)
-    far_ref[:rows] = total.astype(bf16)
+    out_ref[...] = total.astype(bf16)
 
 
 def upright_tables(gain_ref, rows_ref, base_ref, scale, held):
@@ -151,35 +166,67 @@
     return ((z ^ j) * 2 + owner_core) * blocks + c
 
 
-def feature_kernel(blocks, zs, h_hbm, *refs):
-    outs, (held, turned, sems) = refs[:blocks], refs[blocks:]
+def arrival_kernel(blocks, zs, dest_hbm, h_hbm, w_hbm, *refs):
+    outs, late_outs = refs[:blocks], refs[blocks : 2 * blocks]
+    dest_held, h_held, w_held, turned, sems = refs[2 * blocks :]
     me, dp = lax.axis_index("ctx"), lax.axis_index("dp")
     z, core = dp // 2, dp % 2
-    parts, rows, part = held.shape
+    parts, rows, part = h_held.shape
     share = turned.shape[0] // (blocks * zs * 2)
-    copies = [
-        pltpu.make_async_copy(h_hbm.at[:, i * part : (i + 1) * part], held.at[i], sems.at[i])
-        for i in range(parts)
-    ]
+    kv_width = w_held.shape[1]
+    copies = [pltpu.make_async_copy(dest_hbm, dest_held, sems.at[0])]
+    for i in range(parts):
+        piece = pl.ds(i * part, part)
+        copies.append(pltpu.make_async_copy(h_hbm.at[:, piece], h_held.at[i], sems.at[1 + i]))
+    for i in range(parts):
+        piece = pl.ds(i * part, part)
+        copies.append(
+            pltpu.make_async_copy(w_hbm.at[piece], w_held.at[piece], sems.at[1 + parts + i])
+        )
     for copy in copies:
         copy.start()
-    for i, copy in enumerate(copies):
-        copy.wait()
+    copies[0].wait()
+    marks = place_marks(dest_held, blocks)
+    for i in range(parts):
+        copies[1 + i].wait()
         for c in range(part // 128):
             at = i * part + c * 128
-            turned[at : at + 128] = held[i, :, c * 128 : (c + 1) * 128].T
+            turned[at : at + 128] = h_held[i, :, c * 128 : (c + 1) * 128].T
+    first = kv_width // 128 * rows + meta_rows
     for m in range(blocks):
+        outs[m][first - meta_rows : first] = marks
         c = lax.rem(me + m, blocks)
         for half in range(2):
             for j in range(zs):
                 start = share_index(j, half, c, z, core, zs, blocks) * share
                 start = pl.multiple_of(start, 16)
-                at = (half * zs + j) * share
-                outs[m][at : at + share] = turned[pl.ds(start, share)]
+                piece = turned[pl.ds(start, share)]
+                if half:
+                    late_outs[m][j * share : (j + 1) * share] = piece
+                else:
+                    outs[m][first + j * share : first + (j + 1) * share] = piece
+    total = None
+    for i in range(parts):
+        copies[1 + parts + i].wait()
+        product = jnp.dot(
+            h_held[i], w_held[i * part : (i + 1) * part], preferred_element_type=f32
+        )
+        total = product if total is None else total + product
+    total = total.astype(bf16)
+    for m in range(blocks):
+        for h in range(kv_width // 128):
+            outs[m][h * rows : (h + 1) * rows] = total[:, h * 128 : (h + 1) * 128]
 
 
 def mark_rows(ref, rows):
     return ref[rows : rows + meta_rows, :rows].astype(f32)
+
+
+def arrival_slots(marks, me, blocks, rows):
+    marks = marks.astype(f32)
+    away = me.astype(f32) - marks[:1]
+    away = jnp.where(away < 0, away + blocks, away)
+    return away * rows + marks[1:2]
 
 
 def attend_kernel(back, qs_ref, g_ref, *refs):
@@ -193,9 +240,9 @@
 
     @pl.when(pl.program_id(0) == 0)
     def _():
-        query_doc = mark_rows(k_refs[0], rows)[2:3]
+        query_doc = mark_rows(k_refs[0], rows)[:1]
         for b in range(back + 1):
-            key_doc = jnp.broadcast_to(mark_rows(k_refs[b], rows)[2:3], (rows, rows)).T
+            key_doc = jnp.broadcast_to(mark_rows(k_refs[b], rows)[:1], (rows, rows)).T
             allowed = key_doc == query_doc
             if b == 0:
                 key_row = lax.broadcasted_iota(jnp.int32, (rows, rows), 0)
@@ -205,7 +252,7 @@
                 allowed = allowed & (lax.axis_index("ctx") >= b)
             bias_ref[b * rows : (b + 1) * rows] = jnp.where(allowed, 0.0, masked)
 
-    keys = jnp.concatenate([r[rows + meta_rows :] for r in k_refs], axis=0)
+    keys = jnp.concatenate([r[:rows] for r in k_refs], axis=0)
     logits = jnp.dot(keys, qs_ref[0], preferred_element_type=f32)
     e = jnp.exp2(logits + jnp.concatenate([bias_ref[...]] * group, axis=1))
     p = (e * (1.0 / jnp.sum(e, axis=0, keepdims=True))).astype(bf16)
@@ -217,32 +264,36 @@
         send_refs[b][...] = gv[(b + 1) * rows : (b + 2) * rows].astype(bf16)
 
 
-def backward_kernel(back, blocks, factor, p_ref, g_ref, u_ref, qs_ref, gain_ref, rows_ref, base_ref, *refs):
-    v_refs, refs = refs[:blocks], refs[blocks:]
-    k_refs = v_refs[: back + 1]
-    gq_ref, own_ref, send_refs, place_ref, held = refs[0], refs[1], refs[2:-2], refs[-2], refs[-1]
+def slab_values_kernel(blocks, kv, *refs):
+    a_refs, out_ref = refs[:-1], refs[-1]
     me = lax.axis_index("ctx")
+    key_count, width = out_ref.shape
+    rows = a_refs[0].shape[1]
+    first = kv * rows
+    slot = lax.broadcasted_iota(jnp.int32, (key_count, rows), 0).astype(f32)
+    place, arrived = [], []
+    for r in a_refs:
+        at = arrival_slots(r[first : first + meta_rows], me, blocks, rows)
+        place.append((slot == at).astype(f32).astype(bf16))
+        arrived.append(jnp.concatenate([r[h * rows : (h + 1) * rows] for h in range(kv)], axis=1))
+    out_ref[...] = jnp.dot(
+        jnp.concatenate(place, axis=1), jnp.concatenate(arrived, axis=0), preferred_element_type=f32
+    ).astype(bf16)
+
+
+def backward_kernel(back, factor, p_ref, values_ref, g_ref, u_ref, qs_ref, gain_ref, rows_ref, base_ref, *refs):
+    k_refs, refs = refs[: back + 1], refs[back + 1 :]
+    gq_ref, own_ref, send_refs, held = refs[0], refs[1], refs[2:-1], refs[-1]
     rows = g_ref.shape[0]
     hd = own_ref.shape[1]
     group = g_ref.shape[1] // hd
-    key_count = (back + 1) * rows
 
     @pl.when(pl.program_id(0) == 0)
     def _():
         upright_tables(gain_ref, rows_ref, base_ref, factor, held)
-        slot = lax.broadcasted_iota(jnp.int32, (key_count, rows), 0).astype(f32)
-        for s in range(blocks):
-            marks = mark_rows(v_refs[s], rows)
-            away = me.astype(f32) - marks[:1]
-            away = jnp.where(away < 0, away + blocks, away)
-            place_ref[:, s * rows : (s + 1) * rows] = (
-                (slot == away * rows + marks[1:2]).astype(f32).astype(bf16)
-            )
-
-    arrived = jnp.concatenate([r[:rows] for r in v_refs], axis=0)
-    values = jnp.dot(place_ref[...], arrived, preferred_element_type=f32).astype(bf16)
+
     g = jnp.concatenate([g_ref[:, j * hd : (j + 1) * hd] for j in range(group)], axis=0)
-    dp = lax.dot_general(values, g, NT, preferred_element_type=f32)
+    dp = lax.dot_general(values_ref[...], g, NT, preferred_element_type=f32)
     p = p_ref[0].astype(f32)
     delta = jnp.sum(p * dp, axis=0, keepdims=True)
     ds = (p * (dp - delta)).astype(bf16)
@@ -250,7 +301,7 @@
     own_ref[...] = gk[:rows]
     for b in range(back):
         send_refs[b][...] = gk[(b + 1) * rows : (b + 2) * rows].astype(bf16)
-    keys = jnp.concatenate([r[rows + meta_rows :] for r in k_refs], axis=0)
+    keys = jnp.concatenate([r[:rows] for r in k_refs], axis=0)
     gq = jnp.dot(keys.T, ds, preferred_element_type=f32)
     for j in range(group):
         cols = slice(j * rows, (j + 1) * rows)
@@ -307,21 +358,27 @@
     ).astype(bf16)
 
 
-def weight_kernel(blocks, *refs):
-    h_refs, slab_ref, m_refs = refs[:blocks], refs[blocks], refs[blocks + 1 : 2 * blocks + 1]
-    sibling_ref, own_ref = refs[2 * blocks + 1 :]
+def sibling_weight_kernel(blocks, *refs):
+    h_refs, v_refs = refs[:blocks], refs[blocks : 2 * blocks]
+    sibling_ref, arrival_ref = refs[2 * blocks :]
+    me = lax.axis_index("ctx")
     rows = h_refs[0].shape[1]
+    first = h_refs[0].shape[0] - sibling_ref.shape[0]
+    slab = jnp.concatenate([r[...] for r in v_refs], axis=0)
     slot = lax.broadcasted_iota(jnp.int32, (blocks * rows, rows), 0).astype(f32)
-    arrival = []
     for s in range(blocks):
-        marks = mark_rows(m_refs[s], rows)
-        place = (slot == marks[:1] * rows + marks[1:2]).astype(f32).T.astype(bf16)
-        arrival.append(jnp.dot(place, slab_ref[...], preferred_element_type=f32).astype(bf16))
-    arrival = jnp.concatenate(arrival, axis=0)
-    half = sibling_ref.shape[0]
+        at = arrival_slots(h_refs[s][first - meta_rows : first], me, blocks, rows)
+        place = (slot == at).astype(f32).T.astype(bf16)
+        arrived = jnp.dot(place, slab, preferred_element_type=f32).astype(bf16)
+        arrival_ref[s * rows : (s + 1) * rows] = arrived
+    features = jnp.concatenate([r[first:] for r in h_refs], axis=1)
+    sibling_ref[...] = jnp.dot(features, arrival_ref[...], preferred_element_type=f32).astype(bf16)
+
+
+def own_weight_kernel(*refs):
+    h_refs, arrival_ref, own_ref = refs[:-2], refs[-2], refs[-1]
     features = jnp.concatenate([r[...] for r in h_refs], axis=1)
-    sibling_ref[...] = jnp.dot(features[:half], arrival, preferred_element_type=f32).astype(bf16)
-    own_ref[...] = jnp.dot(features[half:], arrival, preferred_element_type=f32)
+    own_ref[...] = jnp.dot(features, arrival_ref[...], preferred_element_type=f32)
 
 
 def on_device(hidden, queries, key_states, out_grad, w_value, q_gain, k_gain, dest_rows, doc_ids):
@@ -339,13 +396,9 @@
     share = width // (blocks * dp_count)
     spread = group * rows
     key_count = (back + 1) * rows
-    message = jax.ShapeDtypeStruct((2 * rows + meta_rows, kv_width), bf16)
-    far_message = jax.ShapeDtypeStruct((rows + meta_rows, kv_width), bf16)
+    message = jax.ShapeDtypeStruct((rows + meta_rows, kv_width), bf16)
     rows_table, base_table = (jnp.asarray(t) for t in rope_constants(rows, blocks, hd))
     q_gain, k_gain = q_gain[None], k_gain[None]
-
-    def behind(array, m):
-        return lax.ppermute(array, "ctx", [(i + m, i) for i in range(blocks - m)])
 
     def around(array, m):
         return lax.ppermute(array, "ctx", [(i, (i + m) % blocks) for i in range(blocks)])
@@ -374,59 +427,77 @@
     def whole(shape):
         return pl.BlockSpec(shape, lambda h: (0,) * len(shape))
 
-    sources = [in_hbm(a) for a in (key_states, doc_ids, dest_rows, k_gain, rows_table, base_table, hidden, w_value)]
-    message_own, message_far = call(
-        functools.partial(message_kernel, blocks), [message, far_message], "message", sources, 16,
-        2 * rows * width * kv_width, 7e6,
-        in_specs=[pl.BlockSpec(memory_space=pltpu.HBM)] * 8,
-        scratch_shapes=[VMEM(a.shape, a.dtype) for a in sources] + [pltpu.SemaphoreType.DMA((15,))],
-    )
-    messages = [message_own]
-    messages += [around(message_own if m <= back else message_far, m) for m in range(1, blocks)]
+    sources = [in_hbm(a) for a in (key_states, doc_ids, k_gain, rows_table, base_table)]
+    key_own = call(
+        key_message_kernel, message, "key_message", sources, 4, 0, 1e6,
+        in_specs=[pl.BlockSpec(memory_space=pltpu.HBM)] * 5,
+        scratch_shapes=[VMEM(a.shape, a.dtype) for a in sources] + [pltpu.SemaphoreType.DMA((5,))],
+    )
+    key_messages = [key_own] + [around(key_own, m) for m in range(1, back + 1)]
 
     head_cols = pl.BlockSpec((rows, group * hd), lambda h: (0, h))
     head_set = pl.BlockSpec((1, hd, spread), lambda h: (h, 0, 0))
-    message_cols = pl.BlockSpec((2 * rows + meta_rows, hd), lambda h: (0, h))
-    far_cols = pl.BlockSpec((rows + meta_rows, hd), lambda h: (0, h))
+    message_cols = pl.BlockSpec((rows + meta_rows, hd), lambda h: (0, h))
     row_cols = pl.BlockSpec((rows, hd), lambda h: (0, h))
     table_specs = [whole((1, hd)), whole(rows_table.shape), whole(base_table.shape)]
     upright = VMEM((3, hd, rows), f32)
 
+    half = width // blocks // 2
+    length = kv * rows + meta_rows + half
+    sources = [in_hbm(a) for a in (dest_rows, hidden, w_value)]
+    if share % 16 == 0:
+        arrivals = call(
+            functools.partial(arrival_kernel, blocks, zs),
+            [jax.ShapeDtypeStruct((length, hd), bf16)] * blocks
+            + [jax.ShapeDtypeStruct((half, hd), bf16)] * blocks,
+            "arrivals", sources, 24, 2 * rows * width * kv_width, 9e6,
+            in_specs=[pl.BlockSpec(memory_space=pltpu.HBM)] * 3, after=(key_own,),
+            scratch_shapes=[
+                VMEM((1, rows), jnp.int32),
+                VMEM((8, rows, width // 8), bf16),
+                VMEM((width, kv_width), bf16),
+                VMEM((width, rows), bf16),
+                pltpu.SemaphoreType.DMA((17,)),
+            ],
+        )
+    else:
+        me, dp = lax.axis_index("ctx"), lax.axis_index("dp")
+        turned = hidden.T.reshape(dp_count * blocks, share, rows)
+        value_own = call(
+            value_kernel, jax.ShapeDtypeStruct((rows, kv_width), bf16), "value", sources[1:], 16,
+            2 * rows * width * kv_width, 7e6,
+            in_specs=[pl.BlockSpec(memory_space=pltpu.HBM)] * 2,
+            scratch_shapes=[VMEM(a.shape, a.dtype) for a in sources[1:]]
+            + [pltpu.SemaphoreType.DMA((9,))],
+        )
+        marks = call(
+            marks_kernel(blocks), jax.ShapeDtypeStruct((meta_rows, rows), bf16), "marks", (dest_rows,), 1
+        )
+        head_values = [value_own[:, h * hd : (h + 1) * hd] for h in range(kv)]
+        arrivals, late = [], []
+        for m in range(blocks):
+            at = [
+                share_index(j, half, lax.rem(me + m, blocks), dp // 2, dp % 2, zs, blocks)
+                for half in range(2)
+                for j in range(zs)
+            ]
+            pieces = [lax.dynamic_index_in_dim(turned, place, axis=0) for place in at]
+            pieces = jnp.concatenate(pieces, axis=0).reshape(width // blocks, rows)
+            arrivals.append(jnp.concatenate([*head_values, marks, pieces[:half]], axis=0))
+            late.append(pieces[half:])
+        arrivals = arrivals + late
+    arrivals, late = arrivals[:blocks], arrivals[blocks:]
+    first_arrival = arrivals[0]
     q_scaled, q_turned = call(
         functools.partial(query_prep_kernel, factor * math.log2(math.e)),
         [jax.ShapeDtypeStruct((kv, hd, spread), bf16)] * 2,
         "query_prep", (queries, q_gain, rows_table, base_table), 8, 0, 4e6, grid=(kv,),
         in_specs=[head_cols] + table_specs, out_specs=[head_set] * 2, scratch_shapes=[upright],
-        after=(message_own,),
-    )
-
-    if share % 16 == 0:
-        features = call(
-            functools.partial(feature_kernel, blocks, zs),
-            [jax.ShapeDtypeStruct((width // blocks, rows), bf16)] * blocks,
-            "features", (in_hbm(hidden),), 8, 0, 6e6,
-            in_specs=[pl.BlockSpec(memory_space=pltpu.HBM)], after=(q_scaled,),
-            scratch_shapes=[
-                VMEM((4, rows, width // 4), bf16),
-                VMEM((width, rows), bf16),
-                pltpu.SemaphoreType.DMA((4,)),
-            ],
-        )
-    else:
-        me, dp = lax.axis_index("ctx"), lax.axis_index("dp")
-        turned = hidden.T.reshape(dp_count * blocks, share, rows)
-        features = []
-        for m in range(blocks):
-            places = [
-                share_index(j, half, lax.rem(me + m, blocks), dp // 2, dp % 2, zs, blocks)
-                for half in range(2)
-                for j in range(zs)
-            ]
-            pieces = [lax.dynamic_index_in_dim(turned, place, axis=0) for place in places]
-            features.append(jnp.concatenate(pieces, axis=0).reshape(width // blocks, rows))
-    first_features = features[0]
-    leaving = gate(features[1:], messages[1 : back + 1], "features_leave")
-    features = [first_features] + [around(leaving[m - 1], m) for m in range(1, blocks)]
+        after=(first_arrival,),
+    )
+
+    leaving = gate(arrivals[1:], tuple(key_messages[1:]), "arrivals_leave")
+    arrivals = [first_arrival] + [around(leaving[m - 1], m) for m in range(1, blocks)]
 
     attended = call(
         functools.partial(attend_kernel, back),
@@ -435,7 +506,7 @@
             jax.ShapeDtypeStruct((rows, kv_width), f32),
         ]
         + [jax.ShapeDtypeStruct((rows, kv_width), bf16)] * back,
-        "attend", (q_scaled, out_grad, *messages[: back + 1]), 16,
+        "attend", (q_scaled, out_grad, *key_messages), 16,
         8 * kv * key_count * spread * hd, 5e6, grid=(kv,),
         in_specs=[head_set, head_cols] + [message_cols] * (back + 1),
         out_specs=[pl.BlockSpec((1, key_count, spread), lambda h: (h, 0, 0))]
@@ -443,10 +514,23 @@
         scratch_shapes=[VMEM((key_count, rows), f32)], after=(leaving[0],),
     )
     probabilities, value_total = attended[0], attended[1]
-    value_got = [behind(attended[1 + m], m) for m in range(1, back + 1)]
+    value_got = [around(attended[1 + m], blocks - m) for m in range(1, back + 1)]
+
+    slab_values = call(
+        functools.partial(slab_values_kernel, blocks, kv),
+        jax.ShapeDtypeStruct((key_count, kv_width), bf16), "slab_values", arrivals, 16,
+        2 * key_count * blocks * rows * kv_width, 2e6, after=(value_total,),
+    )
+    value_grad = call(
+        value_sum_kernel, jax.ShapeDtypeStruct((rows, kv_width), bf16), "value_sum",
+        (value_total, *value_got), 4, 0, 1e6, after=(slab_values,),
+    )
+    late_leaving = gate(late[1:], (value_grad,), "late_leave")
+    late = [late[0]] + [around(late_leaving[m - 1], m) for m in range(1, blocks)]
+    value_grads = [value_grad] + [around(value_grad, m) for m in range(1, blocks)]
 
     backed = call(
-        functools.partial(backward_kernel, back, blocks, factor),
+        functools.partial(backward_kernel, back, factor),
         [
             jax.ShapeDtypeStruct((rows, q_width), bf16),
             jax.ShapeDtypeStruct((rows, kv_width), f32),
@@ -454,30 +538,32 @@
         + [jax.ShapeDtypeStruct((rows, kv_width), bf16)] * back,
         "backward",
         (
-            probabilities, out_grad, q_turned, q_scaled, q_gain, rows_table, base_table,
-            *messages,
+            probabilities, slab_values, out_grad, q_turned, q_scaled, q_gain, rows_table, base_table,
+            *key_messages,
         ),
         20, 12 * kv * key_count * spread * hd, 7e6, grid=(kv,),
         in_specs=[
             pl.BlockSpec((1, key_count, spread), lambda h: (h, 0, 0)),
+            pl.BlockSpec((key_count, hd), lambda h: (0, h)),
             head_cols, head_set, head_set,
         ]
-        + table_specs + [message_cols] * (back + 1) + [far_cols] * (blocks - back - 1),
+        + table_specs + [message_cols] * (back + 1),
         out_specs=[head_cols] + [row_cols] * (back + 1),
-        scratch_shapes=[VMEM((key_count, blocks * rows), bf16), upright],
-        after=(value_total,),
-    )
-    value_grad = call(
-        value_sum_kernel, jax.ShapeDtypeStruct((rows, kv_width), bf16), "value_sum",
-        (value_total, *value_got), 4, 0, 1e6, after=(backed[1], *features[1:]),
-    )
-    slab_value_grad = lax.all_gather(value_grad, "ctx", axis=0, tiled=True)
-
-    half = width // blocks // 2
-    sibling, own = call(
-        functools.partial(weight_kernel, blocks),
-        [jax.ShapeDtypeStruct((half, kv_width), bf16), jax.ShapeDtypeStruct((half, kv_width), f32)],
-        "weight", (*features, slab_value_grad, *messages), 16, 2 * width * rows * kv_width, 4e6,
+        scratch_shapes=[upright],
+        after=(value_grad,),
+    )
+    sibling, arrival = call(
+        functools.partial(sibling_weight_kernel, blocks),
+        [
+            jax.ShapeDtypeStruct((half, kv_width), bf16),
+            jax.ShapeDtypeStruct((blocks * rows, kv_width), bf16),
+        ],
+        "sibling_weight", (*arrivals, *value_grads), 16, width * rows * kv_width, 4e6,
+        after=(backed[1], *late[1:]),
+    )
+    own = call(
+        own_weight_kernel, jax.ShapeDtypeStruct((half, kv_width), f32), "own_weight",
+        (*late, arrival), 16, width * rows * kv_width, 3e6,
     )
     got = lax.ppermute(sibling, "dp", [(d, d ^ 1) for d in range(dp_count)])
 
@@ -504,7 +590,7 @@
 
     query_grad = backed[0]
     key_leaving = gate(backed[2:], (pairs[0],), "keys_leave")
-    key_got = [behind(key_leaving[m - 1], m) for m in range(1, back + 1)]
+    key_got = [around(key_leaving[m - 1], blocks - m) for m in range(1, back + 1)]
     weight_grad = call(
         total_kernel, jax.ShapeDtypeStruct((share, kv_width), f32), "total",
         (pairs[0], *sums), 4, 0, 1e6,

time: 70.8 us -> 65.6 us (0.927); the launches traced: 69.9 us -> 65.4 us
  blocking collectives: 9.17 us -> 0 us
  starting transfers between devices: 19.5 us -> 24.9 us
  Pallas kernels: 23.1 us -> 22.3 us
    ppermute x6 -> x15, starting transfers between devices: 9.72 us -> 20.4 us  [around(): lax.ppermute(array, 'ctx', [(i, (i + m) % blocks) for i in range(blocks)])]
    all_gather x1 -> x0, blocking collectives: 9.17 us -> none  [on_device(): slab_value_grad = lax.all_gather(value_grad, 'ctx', axis=0, tiled=True)]
    ppermute x4 -> x0, waiting for transfers between devices: 7.38 us -> none  [behind(): return lax.ppermute(array, 'ctx', [(i + m, i) for i in range(blocks - m)])]
    ppermute x4 -> x0, starting transfers between devices: 5.29 us -> none  [behind(): return lax.ppermute(array, 'ctx', [(i + m, i) for i in range(blocks - m)])]
    ppermute x6 -> x15, waiting for transfers between devices: 6.59 us -> 11.3 us  [around(): lax.ppermute(array, 'ctx', [(i, (i + m) % blocks) for i in range(blocks)])]
    ppermute x3, waiting for transfers between devices: 1.13 us -> 4.5 us  [on_device(): sums.append(lax.ppermute(pairs[j], 'dp', route))]
    pallas_call x11 -> x13, Pallas kernels: 23.1 us -> 22.3 us  [call(): pl.pallas_call(ordered(kernel, len(operands), len(after)), out_shape=out_...]
  transfers between devices with their start and end apart: 14 -> 19, of which waited for: 6 -> 9; matrix products, arithmetic and copies ran while one was open for 0% -> 0% of each run, Pallas kernels for 25% -> 29%
where the time goes in v3:
time: 65.6 us; the launch traced here: 65.4 us
  starting transfers between devices  24.9 us (38%)
  Pallas kernels  22.3 us (34%)
  waiting for transfers between devices  17.4 us (27%)
  between operations  0.75 us (1%)
    pallas_call x13, Pallas kernels, call(): pl.pallas_call(ordered(kernel, len(operands), len(after)), out_shape=out_...  22.3 us
    ppermute x15, starting transfers between devices, around(): lax.ppermute(array, 'ctx', [(i, (i + m) % blocks) for i in range(blocks)])  20.4 us
    ppermute x15, waiting for transfers between devices, around(): lax.ppermute(array, 'ctx', [(i, (i + m) % blocks) for i in range(blocks)])  11.3 us
    ppermute x3, waiting for transfers between devices, on_device(): sums.append(lax.ppermute(pairs[j], 'dp', route))  4.5 us
    ppermute x3, starting transfers between devices, on_device(): sums.append(lax.ppermute(pairs[j], 'dp', route))  4.45 us
    ppermute x1, waiting for transfers between devices, on_device(): got = lax.ppermute(sibling, 'dp', [(d, d ^ 1) for d in range(dp_count)])  1.58 us
  transfers between devices with their start and end apart: 19, of which 9 were waited for; matrix products, arithmetic and copies ran while one was open for 0% of the time, Pallas kernels for 29%

profile of v3, /device:TPU:0, one launch (start us, length us, event | category | flops | bytes accessed | tf_op | source)
XLA Modules:
  0.0 65.4 jit_solution(12566037299109381918)
XLA Ops:
  0.6 1.4 %key_message.1.refs_3_.refs_2_.refs_8_ = bf16[144,512]{1,0:T(8,128)(2,1)S(1)} custom-call(bf16[128,512]{1,0:T(8,128)(2,1)} %bitcast.12, s32[1,128]{1,0:T(1,128)} %refs_1_.2, f32[1,128]{1,0:T(1,128)} %bitcast.14, f32[2,128,128]{2,1,0:T(8,128)} %constant.4.clone.refs_3_.refs_2_.refs_6_, f32[2,4,128]{2,1,0:T(4,128)} %constant.5.clone.refs_4_.refs_3_.refs_7_), custom_call_target="tpu_custom_call" | custom-call | bytes 1000000 | tf_op jit(solution)/shard_map/key_message/pallas_call | solution.py:409
  2.0 3.0 %collective-permute-start.1 = (bf16[144,512]{1,0:T(8,128)(2,1)S(1)}, bf16[144,512]{1,0:T(8,128)(2,1)S(1)}, u32[]{:S(2)}, u32[]{:S(2)}) collective-permute-start(bf16[144,512]{1,0:T(8,128)(2,1)S(1)} %key_message.1.refs_3_.refs_2_.refs_8_), channel_id=1, source_target_pairs={{0,2},{1,3},{2,0},{3,1},{4,6},{5,7},{6,4},{7,5},{8,10},{9,11},{10,... | collective-permute-start | bytes 442376 | tf_op jit(solution)/shard_map/ppermute | solution.py:404
  5.1 1.5 %collective-permute-start = (bf16[144,512]{1,0:T(8,128)(2,1)S(1)}, bf16[144,512]{1,0:T(8,128)(2,1)S(1)}, u32[]{:S(2)}, u32[]{:S(2)}) collective-permute-start(bf16[144,512]{1,0:T(8,128)(2,1)S(1)} %key_message.1.refs_3_.refs_2_.refs_8_), channel_id=1, source_target_pairs={{0,1},{1,2},{2,3},{3,0},{4,5},{5,6},{6,7},{7,4},{8,9},{9,10},{10,1... | collective-permute-start | bytes 442376 | tf_op jit(solution)/shard_map/ppermute | solution.py:404
  6.5 0.0 copy-start
  6.5 0.0 copy-start.3
  6.5 0.0 copy-start.5
  6.6 3.5 %arrivals.1 = (bf16[1168,128]{1,0:T(8,128)(2,1)S(1)}, bf16[1168,128]{1,0:T(8,128)(2,1)S(1)}, bf16[1168,128]{1,0:T(8,128)(2,1)S(1)}, bf16[1168,128]{1,0:T(8,128)(...) custom-call(s32[1,128]{1,0:T(1,128)} %refs_0_.1, ...), custom_call_target="tpu_custom_call" | custom-call | flops 671088640 | bytes 9000000 | tf_op jit(solution)/shard_map/arrivals/pallas_call | solution.py:409
  10.0 0.0 copy-start.1
  10.0 2.0 %collective-permute-done.1.refs_4_.refs_10_ = bf16[144,512]{1,0:T(8,128)(2,1)S(1)} collective-permute-done((bf16[144,512]{1,0:T(8,128)(2,1)S(1)}, bf16[144,512]{1,0:T(8,128)(2,1)S(1)}, u32[]{:S(2)}, u32[]{:S(2)}) %collective-permute-start.1) | collective-permute-done | bytes 147488 | tf_op jit(solution)/shard_map/ppermute | solution.py:404
  12.1 0.0 collective-permute-done.refs_3_.refs_9_
  12.1 0.0 copy-start.6
  12.1 1.7 %collective-permute-start.5 = (bf16[1168,128]{1,0:T(8,128)(2,1)S(1)}, bf16[1168,128]{1,0:T(8,128)(2,1)S(1)}, u32[]{:S(2)}, u32[]{:S(2)}) collective-permute-start(bf16[1168,128]{1,0:T(8,128)(2,1)S(1)} %get-tuple-element.45), channel_id=1, source_target_pairs={{0,2},{1,3},{2,0},{3,1},{4,6},{5,7},{6,4},{7,5},{8,10},{9,11},{10,... | collective-permute-start | bytes 897032 | tf_op jit(solution)/shard_map/ppermute | solution.py:404
  13.8 0.0 collective-permute-start.6
  13.8 2.0 %collective-permute-start.4 = (bf16[1168,128]{1,0:T(8,128)(2,1)S(1)}, bf16[1168,128]{1,0:T(8,128)(2,1)S(1)}, u32[]{:S(2)}, u32[]{:S(2)}) collective-permute-start(bf16[1168,128]{1,0:T(8,128)(2,1)S(1)} %get-tuple-element.41.refs_5_), channel_id=1, source_target_pairs={{0,1},{1,2},{2,3},{3,0},{4,5},{5,6},{6,7},{7,4},{8,9},{9,10},{10,1... | collective-permute-start | bytes 897032 | tf_op jit(solution)/shard_map/ppermute | solution.py:404
  15.8 0.0 copy-done
  15.8 0.0 copy-done.3
  15.8 0.0 copy-done.5
  15.8 0.0 copy-done.1
  15.8 1.4 %query_prep.1 = (bf16[4,128,1024]{2,1,0:T(8,128)(2,1)S(1)}, bf16[4,128,1024]{2,1,0:T(8,128)(2,1)S(1)}) custom-call(bf16[128,4096]{1,0:T(8,128)(2,1)S(1)} %bitcast.11, f32[1,128]{1,0:T(1,128)S(1)} %bitcast.16, f32[2,128,128]{2,1,0:T(8,128)S(1)} %copy-done, f32[2,4,128]{2,1,0:T(4,128)S(1)} %copy-done.3, bf16[1168,128]{1,0:T(8,128)(2,1)S(1)} %get-tuple-element.36.refs_4_.refs_0_), custom_call_target="tpu_custom_call" | custom-call | bytes 4000000 | tf_op jit(solution)/shard_map/query_prep/pallas_call | solution.py:409
  17.3 0.0 copy-done.6
  17.3 3.8 %attend.1 = (bf16[4,384,1024]{2,1,0:T(8,128)(2,1)S(1)}, f32[128,512]{1,0:T(8,128)S(1)}, bf16[128,512]{1,0:T(8,128)(2,1)S(1)}, bf16[128,512]{1,0:T(8,128)(2,1)S(1)}) custom-call(bf16[4,128,1024]{2,1,0:T(8,128)(2,1)S(1)} %get-tuple-element.37.refs_0_.refs_4_, bf16[128,4096]{1,0:T(8,128)(2,1)S(1)} %bitcast.18, ...), custom_call_target="tpu_custom_call" | custom-call | flops 1610612736 | bytes 5000000 | tf_op jit(solution)/shard_map/attend/pallas_call | solution.py:409
  21.1 1.0 %collective-permute-start.2 = (bf16[128,512]{1,0:T(8,128)(2,1)S(1)}, bf16[128,512]{1,0:T(8,128)(2,1)S(1)}, u32[]{:S(2)}, u32[]{:S(2)}) collective-permute-start(bf16[128,512]{1,0:T(8,128)(2,1)S(1)} %get-tuple-element.43), channel_id=1, source_target_pairs={{0,3},{1,0},{2,1},{3,2},{4,7},{5,4},{6,5},{7,6},{8,11},{9,8},{10,9... | collective-permute-start | bytes 393224 | tf_op jit(solution)/shard_map/ppermute | solution.py:404
  22.1 0.6 collective-permute-start.3
  22.6 0.0 collective-permute-done.5.refs_2_
  22.6 1.2 %collective-permute-done.6.refs_3_ = bf16[1168,128]{1,0:T(8,128)(2,1)S(1)} collective-permute-done((bf16[1168,128]{1,0:T(8,128)(2,1)S(1)}, bf16[1168,128]{1,0:T(8,128)(2,1)S(1)}, u32[]{:S(2)}, u32[]{:S(2)}) %collective-permute-start.6) | collective-permute-done | bytes 299040 | tf_op jit(solution)/shard_map/ppermute | solution.py:404
  23.8 5.4 %collective-permute-done.4.refs_1_ = bf16[1168,128]{1,0:T(8,128)(2,1)S(1)} collective-permute-done((bf16[1168,128]{1,0:T(8,128)(2,1)S(1)}, bf16[1168,128]{1,0:T(8,128)(2,1)S(1)}, u32[]{:S(2)}, u32[]{:S(2)}) %collective-permute-start.4) | collective-permute-done | bytes 299040 | tf_op jit(solution)/shard_map/ppermute | solution.py:404
  29.3 0.4 slab_values.1.refs_3_.refs_1_
  29.6 1.2 %collective-permute-done.2.refs_1_ = bf16[128,512]{1,0:T(8,128)(2,1)S(1)} collective-permute-done((bf16[128,512]{1,0:T(8,128)(2,1)S(1)}, bf16[128,512]{1,0:T(8,128)(2,1)S(1)}, u32[]{:S(2)}, u32[]{:S(2)}) %collective-permute-start.2) | collective-permute-done | bytes 131104 | tf_op jit(solution)/shard_map/ppermute | solution.py:404
  30.8 0.0 collective-permute-done.3.refs_2_
  30.9 1.2 %collective-permute-start.12 = (bf16[128,512]{1,0:T(8,128)(2,1)S(1)}, bf16[128,512]{1,0:T(8,128)(2,1)S(1)}, u32[]{:S(2)}, u32[]{:S(2)}) collective-permute-start(bf16[128,512]{1,0:T(8,128)(2,1)S(1)} %value_sum.1.refs_0_.refs_11_.refs_3_.refs_4_), channel_id=1, source_target_pairs={{0,3},{1,0},{2,1},{3,2},{4,7},{5,4},{6,5},{7,6},{8,11},{9,8},{10,9... | collective-permute-start | bytes 393224 | tf_op jit(solution)/shard_map/ppermute | solution.py:404
  32.1 1.0 %collective-permute-start.11 = (bf16[128,512]{1,0:T(8,128)(2,1)S(1)}, bf16[128,512]{1,0:T(8,128)(2,1)S(1)}, u32[]{:S(2)}, u32[]{:S(2)}) collective-permute-start(bf16[128,512]{1,0:T(8,128)(2,1)S(1)} %value_sum.1.refs_0_.refs_11_.refs_3_.refs_4_), channel_id=1, source_target_pairs={{0,2},{1,3},{2,0},{3,1},{4,6},{5,7},{6,4},{7,5},{8,10},{9,11},{10,... | collective-permute-start | bytes 393224 | tf_op jit(solution)/shard_map/ppermute | solution.py:404
  33.1 0.4 collective-permute-start.10
  33.5 2.1 %collective-permute-start.7 = (bf16[640,128]{1,0:T(8,128)(2,1)S(1)}, bf16[640,128]{1,0:T(8,128)(2,1)S(1)}, u32[]{:S(2)}, u32[]{:S(2)}) collective-permute-start(bf16[640,128]{1,0:T(8,128)(2,1)S(1)} %get-tuple-element.57), channel_id=1, source_target_pairs={{0,1},{1,2},{2,3},{3,0},{4,5},{5,6},{6,7},{7,4},{8,9},{9,10},{10,1... | collective-permute-start | bytes 491528 | tf_op jit(solution)/shard_map/ppermute | solution.py:404
  35.6 1.0 %collective-permute-start.8 = (bf16[640,128]{1,0:T(8,128)(2,1)S(1)}, bf16[640,128]{1,0:T(8,128)(2,1)S(1)}, u32[]{:S(2)}, u32[]{:S(2)}) collective-permute-start(bf16[640,128]{1,0:T(8,128)(2,1)S(1)} %get-tuple-element.58), channel_id=1, source_target_pairs={{0,2},{1,3},{2,0},{3,1},{4,6},{5,7},{6,4},{7,5},{8,10},{9,11},{10,... | collective-permute-start | bytes 491528 | tf_op jit(solution)/shard_map/ppermute | solution.py:404
  36.6 0.8 %collective-permute-done.12.refs_7_ = bf16[128,512]{1,0:T(8,128)(2,1)S(1)} collective-permute-done((bf16[128,512]{1,0:T(8,128)(2,1)S(1)}, bf16[128,512]{1,0:T(8,128)(2,1)S(1)}, u32[]{:S(2)}, u32[]{:S(2)}) %collective-permute-start.12) | collective-permute-done | bytes 131104 | tf_op jit(solution)/shard_map/ppermute | solution.py:404
  37.4 2.1 %collective-permute-start.9 = (bf16[640,128]{1,0:T(8,128)(2,1)S(1)}, bf16[640,128]{1,0:T(8,128)(2,1)S(1)}, u32[]{:S(2)}, u32[]{:S(2)}) collective-permute-start(bf16[640,128]{1,0:T(8,128)(2,1)S(1)} %get-tuple-element.59), channel_id=1, source_target_pairs={{0,3},{1,0},{2,1},{3,2},{4,7},{5,4},{6,5},{7,6},{8,11},{9,8},{10,9... | collective-permute-start | bytes 491528 | tf_op jit(solution)/shard_map/ppermute | solution.py:404
  39.5 5.3 %backward.1 = (bf16[128,4096]{1,0:T(8,128)(2,1)}, f32[128,512]{1,0:T(8,128)S(1)}, bf16[128,512]{1,0:T(8,128)(2,1)S(1)}, bf16[128,512]{1,0:T(8,128)(2,1)S(1)}) custom-call(bf16[4,384,1024]{2,1,0:T(8,128)(2,1)S(1)} %get-tuple-element.47.refs_0_, bf16[384,512]{1,0:T(8,128)(2,1)S(1)} %slab_values.1.refs_3_.refs_1_, bf16[128,4096]{1,0:T(8,128)(2,1)S(1)} %bitcast.19, ...), custom_call_target="tpu_custom_call" | custom-call | flops 2415919104 | bytes 7000000 | tf_op jit(solution)/shard_map/backward/pallas_call | solution.py:409
  44.7 0.0 collective-permute-done.11.refs_6_
  44.7 0.0 collective-permute-done.10.refs_5_
  44.7 0.0 collective-permute-done.7.refs_9_.refs_1_
  44.7 0.6 collective-permute-done.8.refs_10_.refs_2_
  45.3 0.0 collective-permute-done.9.refs_11_.refs_3_
  45.3 0.9 %sibling_weight.1 = (bf16[640,512]{1,0:T(8,128)(2,1)S(1)}, bf16[512,512]{1,0:T(8,128)(2,1)S(1)}) custom-call(bf16[1168,128]{1,0:T(8,128)(2,1)S(1)} %get-tuple-element.36.refs_4_.refs_0_, bf16[1168,128]{1,0:T(8,128)(2,1)S(1)} %collective-permute-done.4.refs_1_, bf16[1168,128]{1,0:T(8,128)(2,1)S(1)} %collective-permute-done.5.refs_2_, ...), custom_call_target="tpu_custom_call" | custom-call | flops 335544320 | bytes 4000000 | tf_op jit(solution)/shard_map/sibling_weight/pallas_call | solution.py:409
  46.2 0.1 collective-permute-start.13
  46.2 0.5 own_weight.1.refs_0_
  46.7 1.6 %collective-permute-done.13.refs_1_ = bf16[640,512]{1,0:T(8,128)(2,1)S(1)} collective-permute-done((bf16[640,512]{1,0:T(8,128)(2,1)S(1)}, bf16[640,512]{1,0:T(8,128)(2,1)S(1)}, u32[]{:S(2)}, u32[]{:S(2)}) %collective-permute-start.13) | collective-permute-done | bytes 655392 | tf_op jit(solution)/shard_map/ppermute | solution.py:568
  48.3 0.1 pair.1
  48.5 1.1 %collective-permute-start.16 = (bf16[160,512]{1,0:T(8,128)(2,1)S(1)}, bf16[160,512]{1,0:T(8,128)(2,1)S(1)}, u32[]{:S(2)}, u32[]{:S(2)}) collective-permute-start(bf16[160,512]{1,0:T(8,128)(2,1)S(1)} %get-tuple-element.65), channel_id=1, source_target_pairs={{0,8},{4,12},{8,0},{12,4},{16,24},{20,28},{24,16},{28,20},{1,9},{5... | collective-permute-start | bytes 491528 | tf_op jit(solution)/shard_map/ppermute | solution.py:589
  49.6 2.6 %collective-permute-start.17 = (bf16[160,512]{1,0:T(8,128)(2,1)S(1)}, bf16[160,512]{1,0:T(8,128)(2,1)S(1)}, u32[]{:S(2)}, u32[]{:S(2)}) collective-permute-start(bf16[160,512]{1,0:T(8,128)(2,1)S(1)} %get-tuple-element.66), channel_id=1, source_target_pairs={{0,16},{4,20},{8,24},{12,28},{16,0},{20,4},{24,8},{28,12},{1,17},{... | collective-permute-start | bytes 491528 | tf_op jit(solution)/shard_map/ppermute | solution.py:589
  52.2 0.7 %collective-permute-start.18 = (bf16[160,512]{1,0:T(8,128)(2,1)S(1)}, bf16[160,512]{1,0:T(8,128)(2,1)S(1)}, u32[]{:S(2)}, u32[]{:S(2)}) collective-permute-start(bf16[160,512]{1,0:T(8,128)(2,1)S(1)} %get-tuple-element.67), channel_id=1, source_target_pairs={{0,24},{4,28},{8,16},{12,20},{16,8},{20,12},{24,0},{28,4},{1,25},{... | collective-permute-start | bytes 491528 | tf_op jit(solution)/shard_map/ppermute | solution.py:589
  52.9 1.1 %collective-permute-start.14 = (bf16[128,512]{1,0:T(8,128)(2,1)S(1)}, bf16[128,512]{1,0:T(8,128)(2,1)S(1)}, u32[]{:S(2)}, u32[]{:S(2)}) collective-permute-start(bf16[128,512]{1,0:T(8,128)(2,1)S(1)} %get-tuple-element.63), channel_id=1, source_target_pairs={{0,3},{1,0},{2,1},{3,2},{4,7},{5,4},{6,5},{7,6},{8,11},{9,8},{10,9... | collective-permute-start | bytes 393224 | tf_op jit(solution)/shard_map/ppermute | solution.py:404
  54.0 1.8 %collective-permute-start.15 = (bf16[128,512]{1,0:T(8,128)(2,1)S(1)}, bf16[128,512]{1,0:T(8,128)(2,1)S(1)}, u32[]{:S(2)}, u32[]{:S(2)}) collective-permute-start(bf16[128,512]{1,0:T(8,128)(2,1)S(1)} %get-tuple-element.64), channel_id=1, source_target_pairs={{0,2},{1,3},{2,0},{3,1},{4,6},{5,7},{6,4},{7,5},{8,10},{9,11},{10,... | collective-permute-start | bytes 393224 | tf_op jit(solution)/shard_map/ppermute | solution.py:404
  55.7 0.0 slice-done
  55.7 0.0 slice-done.1
  55.7 3.1 %hidden_grad.1 = bf16[128,5120]{1,0:T(8,128)(2,1)} custom-call(bf16[128,512]{1,0:T(8,128)(2,1)S(1)} %value_sum.1.refs_0_.refs_11_.refs_3_.refs_4_, bf16[5120,512]{1,0:T(8,128)(2,1)S(1)} %bitcast.10), custom_call_target="tpu_custom_call" | custom-call | flops 671088640 | bytes 7000000 | tf_op jit(solution)/shard_map/hidden_grad/pallas_call | solution.py:409
  58.8 0.0 collective-permute-done.14.refs_5_
  58.9 0.1 collective-permute-done.15.refs_6_
  58.9 0.0 copy-done.2
  58.9 0.0 copy-done.4
  58.9 1.2 %key_back.1 = bf16[128,512]{1,0:T(8,128)(2,1)} custom-call(bf16[128,512]{1,0:T(8,128)(2,1)S(1)} %bitcast.13, f32[128,512]{1,0:T(8,128)S(1)} %get-tuple-element.50.refs_8_.refs_1_, f32[1,128]{1,0:T(1,128)S(1)} %bitcast.15, f32[2,128,128]{2,1,0:T(8,128)S(1)} %copy-done, f32[2,4,128]{2,1,0:T(4,128)S(1)} %copy-done.3, ...), custom_call_target="tpu_custom_call" | custom-call | bytes 1000000 | tf_op jit(solution)/shard_map/key_back/pallas_call | solution.py:409
  60.1 0.0 collective-permute-done.16.refs_1_
  60.1 4.5 %collective-permute-done.17.refs_2_ = bf16[160,512]{1,0:T(8,128)(2,1)S(1)} collective-permute-done((bf16[160,512]{1,0:T(8,128)(2,1)S(1)}, bf16[160,512]{1,0:T(8,128)(2,1)S(1)}, u32[]{:S(2)}, u32[]{:S(2)}) %collective-permute-start.17) | collective-permute-done | bytes 163872 | tf_op jit(solution)/shard_map/ppermute | solution.py:589
  64.6 0.0 collective-permute-done.18.refs_3_
  64.6 0.8 %total.1 = f32[160,512]{1,0:T(8,128)} custom-call(f32[160,512]{1,0:T(8,128)S(1)} %get-tuple-element.62.refs_2_.refs_0_, bf16[160,512]{1,0:T(8,128)(2,1)S(1)} %collective-permute-done.16.refs_1_, bf16[160,512]{1,0:T(8,128)(2,1)S(1)} %collective-permute-done.17.refs_2_, bf16[160,512]{1,0:T(8,128)(2,1)S(1)} %collective-permute-done.18.refs_3_), custom_call_target="tpu_custom_call" | custom-call | bytes 1000000 | tf_op jit(solution)/shard_map/total/pallas_call | solution.py:409
  (9 shorter events, 0.1 us)
Async XLA Ops:
  2.0 10.0 %collective-permute-start.1 = (bf16[144,512]{1,0:T(8,128)(2,1)S(1)}, bf16[144,512]{1,0:T(8,128)(2,1)S(1)}, u32[]{:S(2)}, u32[]{:S(2)}) collective-permute-start(bf16[144,512]{1,0:T(8,128)(2,1)S(1)} %key_message.1.refs_3_.refs_2_.refs_8_), channel_id=1, source_target_pairs={{0,2},{1,3},{2,0},{3,1},{4,6},{5,7},{6,4},{7,5},{8,10},{9,11},{10,... | collective-permute-start | bytes 442376 | tf_op jit(solution)/shard_map/ppermute | solution.py:404
  5.1 7.0 %collective-permute-start = (bf16[144,512]{1,0:T(8,128)(2,1)S(1)}, bf16[144,512]{1,0:T(8,128)(2,1)S(1)}, u32[]{:S(2)}, u32[]{:S(2)}) collective-permute-start(bf16[144,512]{1,0:T(8,128)(2,1)S(1)} %key_message.1.refs_3_.refs_2_.refs_8_), channel_id=1, source_target_pairs={{0,1},{1,2},{2,3},{3,0},{4,5},{5,6},{6,7},{7,4},{8,9},{9,10},{10,1... | collective-permute-start | bytes 442376 | tf_op jit(solution)/shard_map/ppermute | solution.py:404
  6.5 9.3 %copy-start = (f32[2,128,128]{2,1,0:T(8,128)S(1)}, f32[2,128,128]{2,1,0:T(8,128)}, u32[]{:S(2)}) copy-start(f32[2,128,128]{2,1,0:T(8,128)} %constant.4.clone.refs_3_.refs_2_.refs_6_) | copy-start | bytes 393220
  6.5 9.3 %copy-start.3 = (f32[2,4,128]{2,1,0:T(4,128)S(1)}, f32[2,4,128]{2,1,0:T(4,128)}, u32[]{:S(2)}) copy-start(f32[2,4,128]{2,1,0:T(4,128)} %constant.5.clone.refs_4_.refs_3_.refs_7_) | copy-start | bytes 12292
  6.5 9.3 %copy-start.5 = (f32[128]{0:T(128)S(1)}, f32[128]{0:T(128)}, u32[]{:S(2)}) copy-start(f32[128]{0:T(128)} %param.16) | copy-start | bytes 1540
  10.0 5.8 %copy-start.1 = (bf16[1,128,4096]{2,1,0:T(8,128)(2,1)S(1)}, bf16[1,128,4096]{2,1,0:T(8,128)(2,1)}, u32[]{:S(2)}) copy-start(bf16[1,128,4096]{2,1,0:T(8,128)(2,1)} %param.12) | copy-start | bytes 3145732
  12.1 5.2 %copy-start.6 = (bf16[1,128,4096]{2,1,0:T(8,128)(2,1)S(1)}, bf16[1,128,4096]{2,1,0:T(8,128)(2,1)}, u32[]{:S(2)}) copy-start(bf16[1,128,4096]{2,1,0:T(8,128)(2,1)} %param.14) | copy-start | bytes 3145732
  12.1 10.6 %collective-permute-start.5 = (bf16[1168,128]{1,0:T(8,128)(2,1)S(1)}, bf16[1168,128]{1,0:T(8,128)(2,1)S(1)}, u32[]{:S(2)}, u32[]{:S(2)}) collective-permute-start(bf16[1168,128]{1,0:T(8,128)(2,1)S(1)} %get-tuple-element.45), channel_id=1, source_target_pairs={{0,2},{1,3},{2,0},{3,1},{4,6},{5,7},{6,4},{7,5},{8,10},{9,11},{10,... | collective-permute-start | bytes 897032 | tf_op jit(solution)/shard_map/ppermute | solution.py:404
  13.8 10.0 %collective-permute-start.6 = (bf16[1168,128]{1,0:T(8,128)(2,1)S(1)}, bf16[1168,128]{1,0:T(8,128)(2,1)S(1)}, u32[]{:S(2)}, u32[]{:S(2)}) collective-permute-start(bf16[1168,128]{1,0:T(8,128)(2,1)S(1)} %get-tuple-element.46), channel_id=1, source_target_pairs={{0,3},{1,0},{2,1},{3,2},{4,7},{5,4},{6,5},{7,6},{8,11},{9,8},{10,9... | collective-permute-start | bytes 897032 | tf_op jit(solution)/shard_map/ppermute | solution.py:404
  13.8 15.4 %collective-permute-start.4 = (bf16[1168,128]{1,0:T(8,128)(2,1)S(1)}, bf16[1168,128]{1,0:T(8,128)(2,1)S(1)}, u32[]{:S(2)}, u32[]{:S(2)}) collective-permute-start(bf16[1168,128]{1,0:T(8,128)(2,1)S(1)} %get-tuple-element.41.refs_5_), channel_id=1, source_target_pairs={{0,1},{1,2},{2,3},{3,0},{4,5},{5,6},{6,7},{7,4},{8,9},{9,10},{10,1... | collective-permute-start | bytes 897032 | tf_op jit(solution)/shard_map/ppermute | solution.py:404
  21.1 9.7 %collective-permute-start.2 = (bf16[128,512]{1,0:T(8,128)(2,1)S(1)}, bf16[128,512]{1,0:T(8,128)(2,1)S(1)}, u32[]{:S(2)}, u32[]{:S(2)}) collective-permute-start(bf16[128,512]{1,0:T(8,128)(2,1)S(1)} %get-tuple-element.43), channel_id=1, source_target_pairs={{0,3},{1,0},{2,1},{3,2},{4,7},{5,4},{6,5},{7,6},{8,11},{9,8},{10,9... | collective-permute-start | bytes 393224 | tf_op jit(solution)/shard_map/ppermute | solution.py:404
  22.1 8.8 %collective-permute-start.3 = (bf16[128,512]{1,0:T(8,128)(2,1)S(1)}, bf16[128,512]{1,0:T(8,128)(2,1)S(1)}, u32[]{:S(2)}, u32[]{:S(2)}) collective-permute-start(bf16[128,512]{1,0:T(8,128)(2,1)S(1)} %get-tuple-element.44), channel_id=1, source_target_pairs={{0,2},{1,3},{2,0},{3,1},{4,6},{5,7},{6,4},{7,5},{8,10},{9,11},{10,... | collective-permute-start | bytes 393224 | tf_op jit(solution)/shard_map/ppermute | solution.py:404
  30.9 6.5 %collective-permute-start.12 = (bf16[128,512]{1,0:T(8,128)(2,1)S(1)}, bf16[128,512]{1,0:T(8,128)(2,1)S(1)}, u32[]{:S(2)}, u32[]{:S(2)}) collective-permute-start(bf16[128,512]{1,0:T(8,128)(2,1)S(1)} %value_sum.1.refs_0_.refs_11_.refs_3_.refs_4_), channel_id=1, source_target_pairs={{0,3},{1,0},{2,1},{3,2},{4,7},{5,4},{6,5},{7,6},{8,11},{9,8},{10,9... | collective-permute-start | bytes 393224 | tf_op jit(solution)/shard_map/ppermute | solution.py:404
  32.1 12.6 %collective-permute-start.11 = (bf16[128,512]{1,0:T(8,128)(2,1)S(1)}, bf16[128,512]{1,0:T(8,128)(2,1)S(1)}, u32[]{:S(2)}, u32[]{:S(2)}) collective-permute-start(bf16[128,512]{1,0:T(8,128)(2,1)S(1)} %value_sum.1.refs_0_.refs_11_.refs_3_.refs_4_), channel_id=1, source_target_pairs={{0,2},{1,3},{2,0},{3,1},{4,6},{5,7},{6,4},{7,5},{8,10},{9,11},{10,... | collective-permute-start | bytes 393224 | tf_op jit(solution)/shard_map/ppermute | solution.py:404
  33.1 11.6 %collective-permute-start.10 = (bf16[128,512]{1,0:T(8,128)(2,1)S(1)}, bf16[128,512]{1,0:T(8,128)(2,1)S(1)}, u32[]{:S(2)}, u32[]{:S(2)}) collective-permute-start(bf16[128,512]{1,0:T(8,128)(2,1)S(1)} %value_sum.1.refs_0_.refs_11_.refs_3_.refs_4_), channel_id=1, source_target_pairs={{0,1},{1,2},{2,3},{3,0},{4,5},{5,6},{6,7},{7,4},{8,9},{9,10},{10,1... | collective-permute-start | bytes 393224 | tf_op jit(solution)/shard_map/ppermute | solution.py:404
  33.5 11.2 %collective-permute-start.7 = (bf16[640,128]{1,0:T(8,128)(2,1)S(1)}, bf16[640,128]{1,0:T(8,128)(2,1)S(1)}, u32[]{:S(2)}, u32[]{:S(2)}) collective-permute-start(bf16[640,128]{1,0:T(8,128)(2,1)S(1)} %get-tuple-element.57), channel_id=1, source_target_pairs={{0,1},{1,2},{2,3},{3,0},{4,5},{5,6},{6,7},{7,4},{8,9},{9,10},{10,1... | collective-permute-start | bytes 491528 | tf_op jit(solution)/shard_map/ppermute | solution.py:404
  35.6 9.7 %collective-permute-start.8 = (bf16[640,128]{1,0:T(8,128)(2,1)S(1)}, bf16[640,128]{1,0:T(8,128)(2,1)S(1)}, u32[]{:S(2)}, u32[]{:S(2)}) collective-permute-start(bf16[640,128]{1,0:T(8,128)(2,1)S(1)} %get-tuple-element.58), channel_id=1, source_target_pairs={{0,2},{1,3},{2,0},{3,1},{4,6},{5,7},{6,4},{7,5},{8,10},{9,11},{10,... | collective-permute-start | bytes 491528 | tf_op jit(solution)/shard_map/ppermute | solution.py:404
  37.4 7.9 %collective-permute-start.9 = (bf16[640,128]{1,0:T(8,128)(2,1)S(1)}, bf16[640,128]{1,0:T(8,128)(2,1)S(1)}, u32[]{:S(2)}, u32[]{:S(2)}) collective-permute-start(bf16[640,128]{1,0:T(8,128)(2,1)S(1)} %get-tuple-element.59), channel_id=1, source_target_pairs={{0,3},{1,0},{2,1},{3,2},{4,7},{5,4},{6,5},{7,6},{8,11},{9,8},{10,9... | collective-permute-start | bytes 491528 | tf_op jit(solution)/shard_map/ppermute | solution.py:404
  39.4 16.3 %slice-start = ((s8[5242880]{0:T(1024)(128)(4,1)}), s8[4194304]{0:T(1024)(128)(4,1)S(1)}, s32[]{:S(2)}) async-start(s8[5242880]{0:T(1024)(128)(4,1)} %bitcast.9), calls=%async_computation | async-start | bytes 8388608
  39.4 16.3 %slice-start.1 = ((s8[5242880]{0:T(1024)(128)(4,1)}), s8[1048576]{0:T(1024)(128)(4,1)S(1)}, s32[]{:S(2)}) async-start(s8[5242880]{0:T(1024)(128)(4,1)} %bitcast.9), calls=%async_computation.1 | async-start | bytes 2097152
  46.2 2.2 %collective-permute-start.13 = (bf16[640,512]{1,0:T(8,128)(2,1)S(1)}, bf16[640,512]{1,0:T(8,128)(2,1)S(1)}, u32[]{:S(2)}, u32[]{:S(2)}) collective-permute-start(bf16[640,512]{1,0:T(8,128)(2,1)S(1)} %get-tuple-element.61), channel_id=1, source_target_pairs={{0,4},{4,0},{8,12},{12,8},{16,20},{20,16},{24,28},{28,24},{1,5},{5... | collective-permute-start | bytes 1966088 | tf_op jit(solution)/shard_map/ppermute | solution.py:568
  48.5 11.7 %collective-permute-start.16 = (bf16[160,512]{1,0:T(8,128)(2,1)S(1)}, bf16[160,512]{1,0:T(8,128)(2,1)S(1)}, u32[]{:S(2)}, u32[]{:S(2)}) collective-permute-start(bf16[160,512]{1,0:T(8,128)(2,1)S(1)} %get-tuple-element.65), channel_id=1, source_target_pairs={{0,8},{4,12},{8,0},{12,4},{16,24},{20,28},{24,16},{28,20},{1,9},{5... | collective-permute-start | bytes 491528 | tf_op jit(solution)/shard_map/ppermute | solution.py:589
  49.6 15.0 %collective-permute-start.17 = (bf16[160,512]{1,0:T(8,128)(2,1)S(1)}, bf16[160,512]{1,0:T(8,128)(2,1)S(1)}, u32[]{:S(2)}, u32[]{:S(2)}) collective-permute-start(bf16[160,512]{1,0:T(8,128)(2,1)S(1)} %get-tuple-element.66), channel_id=1, source_target_pairs={{0,16},{4,20},{8,24},{12,28},{16,0},{20,4},{24,8},{28,12},{1,17},{... | collective-permute-start | bytes 491528 | tf_op jit(solution)/shard_map/ppermute | solution.py:589
  52.2 12.4 %collective-permute-start.18 = (bf16[160,512]{1,0:T(8,128)(2,1)S(1)}, bf16[160,512]{1,0:T(8,128)(2,1)S(1)}, u32[]{:S(2)}, u32[]{:S(2)}) collective-permute-start(bf16[160,512]{1,0:T(8,128)(2,1)S(1)} %get-tuple-element.67), channel_id=1, source_target_pairs={{0,24},{4,28},{8,16},{12,20},{16,8},{20,12},{24,0},{28,4},{1,25},{... | collective-permute-start | bytes 491528 | tf_op jit(solution)/shard_map/ppermute | solution.py:589
  52.9 5.9 %collective-permute-start.14 = (bf16[128,512]{1,0:T(8,128)(2,1)S(1)}, bf16[128,512]{1,0:T(8,128)(2,1)S(1)}, u32[]{:S(2)}, u32[]{:S(2)}) collective-permute-start(bf16[128,512]{1,0:T(8,128)(2,1)S(1)} %get-tuple-element.63), channel_id=1, source_target_pairs={{0,3},{1,0},{2,1},{3,2},{4,7},{5,4},{6,5},{7,6},{8,11},{9,8},{10,9... | collective-permute-start | bytes 393224 | tf_op jit(solution)/shard_map/ppermute | solution.py:404
  54.0 5.0 %copy-start.2 = (bf16[1,128,512]{2,1,0:T(8,128)(2,1)S(1)}, bf16[1,128,512]{2,1,0:T(8,128)(2,1)}, u32[]{:S(2)}) copy-start(bf16[1,128,512]{2,1,0:T(8,128)(2,1)} %param.13) | copy-start | bytes 393220
  54.0 5.0 %copy-start.4 = (f32[128]{0:T(128)S(1)}, f32[128]{0:T(128)}, u32[]{:S(2)}) copy-start(f32[128]{0:T(128)} %param.17) | copy-start | bytes 1540
  54.0 5.0 %collective-permute-start.15 = (bf16[128,512]{1,0:T(8,128)(2,1)S(1)}, bf16[128,512]{1,0:T(8,128)(2,1)S(1)}, u32[]{:S(2)}, u32[]{:S(2)}) collective-permute-start(bf16[128,512]{1,0:T(8,128)(2,1)S(1)} %get-tuple-element.64), channel_id=1, source_target_pairs={{0,2},{1,3},{2,0},{3,1},{4,6},{5,7},{6,4},{7,5},{8,10},{9,11},{10,... | collective-permute-start | bytes 393224 | tf_op jit(solution)/shard_map/ppermute | solution.py:404

commit v4 on v3

--- a/solution.py
+++ b/solution.py
@@ -330,11 +330,20 @@
     pass
 
 
-def value_sum_kernel(*refs):
-    total = refs[0][...]
-    for r in refs[1:-1]:
+def value_sum_kernel(back, total_ref, *refs):
+    got_refs, refs = refs[:back], refs[back:]
+    count = len(refs) // 2
+    late_refs, grad_ref, send_refs = refs[:count], refs[count], refs[count + 1 :]
+    total = total_ref[...]
+    for r in got_refs:
         total = total + r[...].astype(f32)
-    refs[-1][...] = total.astype(bf16)
+    grad = total.astype(bf16)
+    grad_ref[...] = grad
+    rows, width = grad.shape
+    for late_ref, send_ref in zip(late_refs, send_refs):
+        for h in range(width // 128):
+            send_ref[h * rows : (h + 1) * rows] = grad[:, h * 128 : (h + 1) * 128]
+        send_ref[width // 128 * rows :] = late_ref[...]
 
 
 def pair_kernel(own_ref, got_ref, first_ref, *send_refs):
@@ -361,10 +370,14 @@
 def sibling_weight_kernel(blocks, *refs):
     h_refs, v_refs = refs[:blocks], refs[blocks : 2 * blocks]
     sibling_ref, arrival_ref = refs[2 * blocks :]
+    heads = v_refs[0].shape[1] // 128
     me = lax.axis_index("ctx")
     rows = h_refs[0].shape[1]
     first = h_refs[0].shape[0] - sibling_ref.shape[0]
-    slab = jnp.concatenate([r[...] for r in v_refs], axis=0)
+    slab = [v_refs[0][...]]
+    for r in v_refs[1:]:
+        slab.append(jnp.concatenate([r[h * rows : (h + 1) * rows] for h in range(heads)], axis=1))
+    slab = jnp.concatenate(slab, axis=0)
     slot = lax.broadcasted_iota(jnp.int32, (blocks * rows, rows), 0).astype(f32)
     for s in range(blocks):
         at = arrival_slots(h_refs[s][first - meta_rows : first], me, blocks, rows)
@@ -377,7 +390,8 @@
 
 def own_weight_kernel(*refs):
     h_refs, arrival_ref, own_ref = refs[:-2], refs[-2], refs[-1]
-    features = jnp.concatenate([r[...] for r in h_refs], axis=1)
+    half = own_ref.shape[0]
+    features = jnp.concatenate([r[r.shape[0] - half :] for r in h_refs], axis=1)
     own_ref[...] = jnp.dot(features, arrival_ref[...], preferred_element_type=f32)
 
 
@@ -521,13 +535,13 @@
         jax.ShapeDtypeStruct((key_count, kv_width), bf16), "slab_values", arrivals, 16,
         2 * key_count * blocks * rows * kv_width, 2e6, after=(value_total,),
     )
-    value_grad = call(
-        value_sum_kernel, jax.ShapeDtypeStruct((rows, kv_width), bf16), "value_sum",
-        (value_total, *value_got), 4, 0, 1e6, after=(slab_values,),
-    )
-    late_leaving = gate(late[1:], (value_grad,), "late_leave")
-    late = [late[0]] + [around(late_leaving[m - 1], m) for m in range(1, blocks)]
-    value_grads = [value_grad] + [around(value_grad, m) for m in range(1, blocks)]
+    value_grad, *followed = call(
+        functools.partial(value_sum_kernel, back),
+        [jax.ShapeDtypeStruct((rows, kv_width), bf16)]
+        + [jax.ShapeDtypeStruct((kv * rows + half, hd), bf16)] * (blocks - 1),
+        "value_sum", (value_total, *value_got, *late[1:]), 8, 0, 3e6, after=(slab_values,),
+    )
+    followed = [around(followed[m - 1], m) for m in range(1, blocks)]
 
     backed = call(
         functools.partial(backward_kernel, back, factor),
@@ -558,12 +572,12 @@
             jax.ShapeDtypeStruct((half, kv_width), bf16),
             jax.ShapeDtypeStruct((blocks * rows, kv_width), bf16),
         ],
-        "sibling_weight", (*arrivals, *value_grads), 16, width * rows * kv_width, 4e6,
-        after=(backed[1], *late[1:]),
+        "sibling_weight", (*arrivals, value_grad, *followed), 16, width * rows * kv_width, 4e6,
+        after=(backed[1],),
     )
     own = call(
         own_weight_kernel, jax.ShapeDtypeStruct((half, kv_width), f32), "own_weight",
-        (*late, arrival), 16, width * rows * kv_width, 3e6,
+        (late[0], *followed, arrival), 16, width * rows * kv_width, 3e6,
     )
     got = lax.ppermute(sibling, "dp", [(d, d ^ 1) for d in range(dp_count)])
 

time: 65.6 us -> 64.9 us (0.989)
  starting transfers between devices: 24.9 us -> 20.7 us
  waiting for transfers between devices: 17.4 us -> 20.8 us
    ppermute x15 -> x12, waiting for transfers between devices: 11.3 us -> 17 us  [around(): lax.ppermute(array, 'ctx', [(i, (i + m) % blocks) for i in range(blocks)])]
    ppermute x15 -> x12, starting transfers between devices: 20.4 us -> 16.2 us  [around(): lax.ppermute(array, 'ctx', [(i, (i + m) % blocks) for i in range(blocks)])]
    ppermute x3, waiting for transfers between devices: 4.5 us -> 2.24 us  [on_device(): sums.append(lax.ppermute(pairs[j], 'dp', route))]
  transfers between devices with their start and end apart: 19 -> 16, of which waited for: 9 -> 9; matrix products, arithmetic and copies ran while one was open for 0% -> 0% of each run, Pallas kernels for 29% -> 30%
where the time goes in v4:
time: 64.9 us; the launch traced here: 64.6 us
  Pallas kernels  22.3 us (34%)
  waiting for transfers between devices  20.8 us (32%)
  starting transfers between devices  20.7 us (32%)
  between operations  0.74 us (1%)
    pallas_call x13, Pallas kernels, call(): pl.pallas_call(ordered(kernel, len(operands), len(after)), out_shape=out_...  22.3 us
    ppermute x12, waiting for transfers between devices, around(): lax.ppermute(array, 'ctx', [(i, (i + m) % blocks) for i in range(blocks)])  17 us
    ppermute x12, starting transfers between devices, around(): lax.ppermute(array, 'ctx', [(i, (i + m) % blocks) for i in range(blocks)])  16.2 us
    ppermute x3, starting transfers between devices, on_device(): sums.append(lax.ppermute(pairs[j], 'dp', route))  4.45 us
    ppermute x3, waiting for transfers between devices, on_device(): sums.append(lax.ppermute(pairs[j], 'dp', route))  2.24 us
    ppermute x1, waiting for transfers between devices, on_device(): got = lax.ppermute(sibling, 'dp', [(d, d ^ 1) for d in range(dp_count)])  1.58 us
  transfers between devices with their start and end apart: 16, of which 9 were waited for; matrix products, arithmetic and copies ran while one was open for 0% of the time, Pallas kernels for 30%

profile of v4, /device:TPU:0, one launch (start us, length us, event | category | flops | bytes accessed | tf_op | source)
XLA Modules:
  0.0 64.6 jit_solution(9496701775679157965)
XLA Ops:
  0.6 1.4 %key_message.1.refs_3_.refs_2_.refs_8_ = bf16[144,512]{1,0:T(8,128)(2,1)S(1)} custom-call(bf16[128,512]{1,0:T(8,128)(2,1)} %bitcast.12, s32[1,128]{1,0:T(1,128)} %refs_1_.2, f32[1,128]{1,0:T(1,128)} %bitcast.14, f32[2,128,128]{2,1,0:T(8,128)} %constant.4.clone.refs_3_.refs_2_.refs_6_, f32[2,4,128]{2,1,0:T(4,128)} %constant.5.clone.refs_4_.refs_3_.refs_7_), custom_call_target="tpu_custom_call" | custom-call | bytes 1000000 | tf_op jit(solution)/shard_map/key_message/pallas_call | solution.py:423
  2.0 3.0 %collective-permute-start.1 = (bf16[144,512]{1,0:T(8,128)(2,1)S(1)}, bf16[144,512]{1,0:T(8,128)(2,1)S(1)}, u32[]{:S(2)}, u32[]{:S(2)}) collective-permute-start(bf16[144,512]{1,0:T(8,128)(2,1)S(1)} %key_message.1.refs_3_.refs_2_.refs_8_), channel_id=1, source_target_pairs={{0,2},{1,3},{2,0},{3,1},{4,6},{5,7},{6,4},{7,5},{8,10},{9,11},{10,... | collective-permute-start | bytes 442376 | tf_op jit(solution)/shard_map/ppermute | solution.py:418
  5.1 1.5 %collective-permute-start = (bf16[144,512]{1,0:T(8,128)(2,1)S(1)}, bf16[144,512]{1,0:T(8,128)(2,1)S(1)}, u32[]{:S(2)}, u32[]{:S(2)}) collective-permute-start(bf16[144,512]{1,0:T(8,128)(2,1)S(1)} %key_message.1.refs_3_.refs_2_.refs_8_), channel_id=1, source_target_pairs={{0,1},{1,2},{2,3},{3,0},{4,5},{5,6},{6,7},{7,4},{8,9},{9,10},{10,1... | collective-permute-start | bytes 442376 | tf_op jit(solution)/shard_map/ppermute | solution.py:418
  6.5 0.0 copy-start
  6.5 0.0 copy-start.3
  6.5 0.0 copy-start.5
  6.6 3.5 %arrivals.1 = (bf16[1168,128]{1,0:T(8,128)(2,1)S(1)}, bf16[1168,128]{1,0:T(8,128)(2,1)S(1)}, bf16[1168,128]{1,0:T(8,128)(2,1)S(1)}, bf16[1168,128]{1,0:T(8,128)(...) custom-call(s32[1,128]{1,0:T(1,128)} %refs_0_.1, ...), custom_call_target="tpu_custom_call" | custom-call | flops 671088640 | bytes 9000000 | tf_op jit(solution)/shard_map/arrivals/pallas_call | solution.py:423
  10.0 0.0 copy-start.1
  10.0 2.0 %collective-permute-done.1.refs_4_.refs_10_ = bf16[144,512]{1,0:T(8,128)(2,1)S(1)} collective-permute-done((bf16[144,512]{1,0:T(8,128)(2,1)S(1)}, bf16[144,512]{1,0:T(8,128)(2,1)S(1)}, u32[]{:S(2)}, u32[]{:S(2)}) %collective-permute-start.1) | collective-permute-done | bytes 147488 | tf_op jit(solution)/shard_map/ppermute | solution.py:418
  12.1 0.0 collective-permute-done.refs_3_.refs_9_
  12.1 0.0 copy-start.6
  12.1 1.7 %collective-permute-start.5 = (bf16[1168,128]{1,0:T(8,128)(2,1)S(1)}, bf16[1168,128]{1,0:T(8,128)(2,1)S(1)}, u32[]{:S(2)}, u32[]{:S(2)}) collective-permute-start(bf16[1168,128]{1,0:T(8,128)(2,1)S(1)} %get-tuple-element.49), channel_id=1, source_target_pairs={{0,2},{1,3},{2,0},{3,1},{4,6},{5,7},{6,4},{7,5},{8,10},{9,11},{10,... | collective-permute-start | bytes 897032 | tf_op jit(solution)/shard_map/ppermute | solution.py:418
  13.8 0.0 collective-permute-start.6
  13.8 2.0 %collective-permute-start.4 = (bf16[1168,128]{1,0:T(8,128)(2,1)S(1)}, bf16[1168,128]{1,0:T(8,128)(2,1)S(1)}, u32[]{:S(2)}, u32[]{:S(2)}) collective-permute-start(bf16[1168,128]{1,0:T(8,128)(2,1)S(1)} %get-tuple-element.42.refs_5_), channel_id=1, source_target_pairs={{0,1},{1,2},{2,3},{3,0},{4,5},{5,6},{6,7},{7,4},{8,9},{9,10},{10,1... | collective-permute-start | bytes 897032 | tf_op jit(solution)/shard_map/ppermute | solution.py:418
  15.8 0.0 copy-done
  15.8 0.0 copy-done.3
  15.8 0.0 copy-done.5
  15.8 0.0 copy-done.1
  15.8 1.4 %query_prep.1 = (bf16[4,128,1024]{2,1,0:T(8,128)(2,1)S(1)}, bf16[4,128,1024]{2,1,0:T(8,128)(2,1)S(1)}) custom-call(bf16[128,4096]{1,0:T(8,128)(2,1)S(1)} %bitcast.11, f32[1,128]{1,0:T(1,128)S(1)} %bitcast.16, f32[2,128,128]{2,1,0:T(8,128)S(1)} %copy-done, f32[2,4,128]{2,1,0:T(4,128)S(1)} %copy-done.3, bf16[1168,128]{1,0:T(8,128)(2,1)S(1)} %get-tuple-element.37.refs_4_.refs_0_), custom_call_target="tpu_custom_call" | custom-call | bytes 4000000 | tf_op jit(solution)/shard_map/query_prep/pallas_call | solution.py:423
  17.3 0.0 copy-done.6
  17.3 3.8 %attend.1 = (bf16[4,384,1024]{2,1,0:T(8,128)(2,1)S(1)}, f32[128,512]{1,0:T(8,128)S(1)}, bf16[128,512]{1,0:T(8,128)(2,1)S(1)}, bf16[128,512]{1,0:T(8,128)(2,1)S(1)}) custom-call(bf16[4,128,1024]{2,1,0:T(8,128)(2,1)S(1)} %get-tuple-element.38.refs_0_.refs_4_, bf16[128,4096]{1,0:T(8,128)(2,1)S(1)} %bitcast.18, ...), custom_call_target="tpu_custom_call" | custom-call | flops 1610612736 | bytes 5000000 | tf_op jit(solution)/shard_map/attend/pallas_call | solution.py:423
  21.1 1.0 %collective-permute-start.2 = (bf16[128,512]{1,0:T(8,128)(2,1)S(1)}, bf16[128,512]{1,0:T(8,128)(2,1)S(1)}, u32[]{:S(2)}, u32[]{:S(2)}) collective-permute-start(bf16[128,512]{1,0:T(8,128)(2,1)S(1)} %get-tuple-element.44), channel_id=1, source_target_pairs={{0,3},{1,0},{2,1},{3,2},{4,7},{5,4},{6,5},{7,6},{8,11},{9,8},{10,9... | collective-permute-start | bytes 393224 | tf_op jit(solution)/shard_map/ppermute | solution.py:418
  22.1 0.6 collective-permute-start.3
  22.6 0.0 collective-permute-done.5.refs_2_
  22.6 1.2 %collective-permute-done.6.refs_3_ = bf16[1168,128]{1,0:T(8,128)(2,1)S(1)} collective-permute-done((bf16[1168,128]{1,0:T(8,128)(2,1)S(1)}, bf16[1168,128]{1,0:T(8,128)(2,1)S(1)}, u32[]{:S(2)}, u32[]{:S(2)}) %collective-permute-start.6) | collective-permute-done | bytes 299040 | tf_op jit(solution)/shard_map/ppermute | solution.py:418
  23.8 5.4 %collective-permute-done.4.refs_1_ = bf16[1168,128]{1,0:T(8,128)(2,1)S(1)} collective-permute-done((bf16[1168,128]{1,0:T(8,128)(2,1)S(1)}, bf16[1168,128]{1,0:T(8,128)(2,1)S(1)}, u32[]{:S(2)}, u32[]{:S(2)}) %collective-permute-start.4) | collective-permute-done | bytes 299040 | tf_op jit(solution)/shard_map/ppermute | solution.py:418
  29.3 0.4 slab_values.1.refs_6_.refs_1_
  29.6 1.2 %collective-permute-done.2.refs_1_ = bf16[128,512]{1,0:T(8,128)(2,1)S(1)} collective-permute-done((bf16[128,512]{1,0:T(8,128)(2,1)S(1)}, bf16[128,512]{1,0:T(8,128)(2,1)S(1)}, u32[]{:S(2)}, u32[]{:S(2)}) %collective-permute-start.2) | collective-permute-done | bytes 131104 | tf_op jit(solution)/shard_map/ppermute | solution.py:418
  30.8 0.0 collective-permute-done.3.refs_2_
  30.8 0.1 value_sum.1
  30.9 0.8 %collective-permute-start.7 = (bf16[1152,128]{1,0:T(8,128)(2,1)S(1)}, bf16[1152,128]{1,0:T(8,128)(2,1)S(1)}, u32[]{:S(2)}, u32[]{:S(2)}) collective-permute-start(bf16[1152,128]{1,0:T(8,128)(2,1)S(1)} %get-tuple-element.59), channel_id=1, source_target_pairs={{0,1},{1,2},{2,3},{3,0},{4,5},{5,6},{6,7},{7,4},{8,9},{9,10},{10,1... | collective-permute-start | bytes 884744 | tf_op jit(solution)/shard_map/ppermute | solution.py:418
  31.7 1.1 %collective-permute-start.8 = (bf16[1152,128]{1,0:T(8,128)(2,1)S(1)}, bf16[1152,128]{1,0:T(8,128)(2,1)S(1)}, u32[]{:S(2)}, u32[]{:S(2)}) collective-permute-start(bf16[1152,128]{1,0:T(8,128)(2,1)S(1)} %get-tuple-element.60), channel_id=1, source_target_pairs={{0,2},{1,3},{2,0},{3,1},{4,6},{5,7},{6,4},{7,5},{8,10},{9,11},{10,... | collective-permute-start | bytes 884744 | tf_op jit(solution)/shard_map/ppermute | solution.py:418
  32.7 1.7 %collective-permute-start.9 = (bf16[1152,128]{1,0:T(8,128)(2,1)S(1)}, bf16[1152,128]{1,0:T(8,128)(2,1)S(1)}, u32[]{:S(2)}, u32[]{:S(2)}) collective-permute-start(bf16[1152,128]{1,0:T(8,128)(2,1)S(1)} %get-tuple-element.61), channel_id=1, source_target_pairs={{0,3},{1,0},{2,1},{3,2},{4,7},{5,4},{6,5},{7,6},{8,11},{9,8},{10,9... | collective-permute-start | bytes 884744 | tf_op jit(solution)/shard_map/ppermute | solution.py:418
  34.4 0.0 slice-start
  34.4 0.0 slice-start.1
  34.4 5.3 %backward.1 = (bf16[128,4096]{1,0:T(8,128)(2,1)}, f32[128,512]{1,0:T(8,128)S(1)}, bf16[128,512]{1,0:T(8,128)(2,1)S(1)}, bf16[128,512]{1,0:T(8,128)(2,1)S(1)}) custom-call(bf16[4,384,1024]{2,1,0:T(8,128)(2,1)S(1)} %get-tuple-element.52.refs_0_, bf16[384,512]{1,0:T(8,128)(2,1)S(1)} %slab_values.1.refs_6_.refs_1_, bf16[128,4096]{1,0:T(8,128)(2,1)S(1)} %bitcast.19, ...), custom_call_target="tpu_custom_call" | custom-call | flops 2415919104 | bytes 7000000 | tf_op jit(solution)/shard_map/backward/pallas_call | solution.py:423
  39.7 2.1 %collective-permute-done.7.refs_5_.refs_1_ = bf16[1152,128]{1,0:T(8,128)(2,1)S(1)} collective-permute-done((bf16[1152,128]{1,0:T(8,128)(2,1)S(1)}, bf16[1152,128]{1,0:T(8,128)(2,1)S(1)}, u32[]{:S(2)}, u32[]{:S(2)}) %collective-permute-start.7) | collective-permute-done | bytes 294944 | tf_op jit(solution)/shard_map/ppermute | solution.py:418
  41.8 3.4 %collective-permute-done.8.refs_6_.refs_2_ = bf16[1152,128]{1,0:T(8,128)(2,1)S(1)} collective-permute-done((bf16[1152,128]{1,0:T(8,128)(2,1)S(1)}, bf16[1152,128]{1,0:T(8,128)(2,1)S(1)}, u32[]{:S(2)}, u32[]{:S(2)}) %collective-permute-start.8) | collective-permute-done | bytes 294944 | tf_op jit(solution)/shard_map/ppermute | solution.py:418
  45.2 0.0 collective-permute-done.9.refs_7_.refs_3_
  45.2 0.9 %sibling_weight.1 = (bf16[640,512]{1,0:T(8,128)(2,1)S(1)}, bf16[512,512]{1,0:T(8,128)(2,1)S(1)}) custom-call(bf16[1168,128]{1,0:T(8,128)(2,1)S(1)} %get-tuple-element.37.refs_4_.refs_0_, bf16[1168,128]{1,0:T(8,128)(2,1)S(1)} %collective-permute-done.4.refs_1_, bf16[1168,128]{1,0:T(8,128)(2,1)S(1)} %collective-permute-done.5.refs_2_, ...), custom_call_target="tpu_custom_call" | custom-call | flops 335544320 | bytes 4000000 | tf_op jit(solution)/shard_map/sibling_weight/pallas_call | solution.py:423
  46.1 0.1 collective-permute-start.10
  46.2 0.5 own_weight.1.refs_0_
  46.7 1.6 %collective-permute-done.10.refs_1_ = bf16[640,512]{1,0:T(8,128)(2,1)S(1)} collective-permute-done((bf16[640,512]{1,0:T(8,128)(2,1)S(1)}, bf16[640,512]{1,0:T(8,128)(2,1)S(1)}, u32[]{:S(2)}, u32[]{:S(2)}) %collective-permute-start.10) | collective-permute-done | bytes 655392 | tf_op jit(solution)/shard_map/ppermute | solution.py:582
  48.3 0.1 pair.1
  48.4 0.4 collective-permute-start.13
  48.8 2.6 %collective-permute-start.14 = (bf16[160,512]{1,0:T(8,128)(2,1)S(1)}, bf16[160,512]{1,0:T(8,128)(2,1)S(1)}, u32[]{:S(2)}, u32[]{:S(2)}) collective-permute-start(bf16[160,512]{1,0:T(8,128)(2,1)S(1)} %get-tuple-element.68), channel_id=1, source_target_pairs={{0,16},{4,20},{8,24},{12,28},{16,0},{20,4},{24,8},{28,12},{1,17},{... | collective-permute-start | bytes 491528 | tf_op jit(solution)/shard_map/ppermute | solution.py:603
  51.4 1.5 %collective-permute-start.15 = (bf16[160,512]{1,0:T(8,128)(2,1)S(1)}, bf16[160,512]{1,0:T(8,128)(2,1)S(1)}, u32[]{:S(2)}, u32[]{:S(2)}) collective-permute-start(bf16[160,512]{1,0:T(8,128)(2,1)S(1)} %get-tuple-element.69), channel_id=1, source_target_pairs={{0,24},{4,28},{8,16},{12,20},{16,8},{20,12},{24,0},{28,4},{1,25},{... | collective-permute-start | bytes 491528 | tf_op jit(solution)/shard_map/ppermute | solution.py:603
  52.8 2.6 %collective-permute-start.11 = (bf16[128,512]{1,0:T(8,128)(2,1)S(1)}, bf16[128,512]{1,0:T(8,128)(2,1)S(1)}, u32[]{:S(2)}, u32[]{:S(2)}) collective-permute-start(bf16[128,512]{1,0:T(8,128)(2,1)S(1)} %get-tuple-element.65), channel_id=1, source_target_pairs={{0,3},{1,0},{2,1},{3,2},{4,7},{5,4},{6,5},{7,6},{8,11},{9,8},{10,9... | collective-permute-start | bytes 393224 | tf_op jit(solution)/shard_map/ppermute | solution.py:418
  55.4 0.0 copy-start.2
  55.4 0.0 copy-start.4
  55.4 0.3 collective-permute-start.12
  55.7 0.0 slice-done
  55.7 0.0 slice-done.1
  55.7 3.1 %hidden_grad.1 = bf16[128,5120]{1,0:T(8,128)(2,1)} custom-call(bf16[128,512]{1,0:T(8,128)(2,1)S(1)} %get-tuple-element.51.refs_0_.refs_11_.refs_4_, bf16[5120,512]{1,0:T(8,128)(2,1)S(1)} %bitcast.10), custom_call_target="tpu_custom_call" | custom-call | flops 671088640 | bytes 7000000 | tf_op jit(solution)/shard_map/hidden_grad/pallas_call | solution.py:423
  58.8 0.0 collective-permute-done.11.refs_5_
  58.8 1.6 %collective-permute-done.12.refs_6_ = bf16[128,512]{1,0:T(8,128)(2,1)S(1)} collective-permute-done((bf16[128,512]{1,0:T(8,128)(2,1)S(1)}, bf16[128,512]{1,0:T(8,128)(2,1)S(1)}, u32[]{:S(2)}, u32[]{:S(2)}) %collective-permute-start.12) | collective-permute-done | bytes 131104 | tf_op jit(solution)/shard_map/ppermute | solution.py:418
  60.4 0.0 copy-done.2
  60.4 0.0 copy-done.4
  60.4 1.2 %key_back.1 = bf16[128,512]{1,0:T(8,128)(2,1)} custom-call(bf16[128,512]{1,0:T(8,128)(2,1)S(1)} %bitcast.13, f32[128,512]{1,0:T(8,128)S(1)} %get-tuple-element.55.refs_8_.refs_1_, f32[1,128]{1,0:T(1,128)S(1)} %bitcast.15, f32[2,128,128]{2,1,0:T(8,128)S(1)} %copy-done, f32[2,4,128]{2,1,0:T(4,128)S(1)} %copy-done.3, ...), custom_call_target="tpu_custom_call" | custom-call | bytes 1000000 | tf_op jit(solution)/shard_map/key_back/pallas_call | solution.py:423
  61.5 0.0 collective-permute-done.13.refs_1_
  61.5 2.2 %collective-permute-done.14.refs_2_ = bf16[160,512]{1,0:T(8,128)(2,1)S(1)} collective-permute-done((bf16[160,512]{1,0:T(8,128)(2,1)S(1)}, bf16[160,512]{1,0:T(8,128)(2,1)S(1)}, u32[]{:S(2)}, u32[]{:S(2)}) %collective-permute-start.14) | collective-permute-done | bytes 163872 | tf_op jit(solution)/shard_map/ppermute | solution.py:603
  63.8 0.0 collective-permute-done.15.refs_3_
  63.8 0.8 %total.1 = f32[160,512]{1,0:T(8,128)} custom-call(f32[160,512]{1,0:T(8,128)S(1)} %get-tuple-element.64.refs_2_.refs_0_, bf16[160,512]{1,0:T(8,128)(2,1)S(1)} %collective-permute-done.13.refs_1_, bf16[160,512]{1,0:T(8,128)(2,1)S(1)} %collective-permute-done.14.refs_2_, bf16[160,512]{1,0:T(8,128)(2,1)S(1)} %collective-permute-done.15.refs_3_), custom_call_target="tpu_custom_call" | custom-call | bytes 1000000 | tf_op jit(solution)/shard_map/total/pallas_call | solution.py:423
  (3 shorter events, 0.0 us)
Async XLA Ops:
  2.0 10.0 %collective-permute-start.1 = (bf16[144,512]{1,0:T(8,128)(2,1)S(1)}, bf16[144,512]{1,0:T(8,128)(2,1)S(1)}, u32[]{:S(2)}, u32[]{:S(2)}) collective-permute-start(bf16[144,512]{1,0:T(8,128)(2,1)S(1)} %key_message.1.refs_3_.refs_2_.refs_8_), channel_id=1, source_target_pairs={{0,2},{1,3},{2,0},{3,1},{4,6},{5,7},{6,4},{7,5},{8,10},{9,11},{10,... | collective-permute-start | bytes 442376 | tf_op jit(solution)/shard_map/ppermute | solution.py:418
  5.1 7.0 %collective-permute-start = (bf16[144,512]{1,0:T(8,128)(2,1)S(1)}, bf16[144,512]{1,0:T(8,128)(2,1)S(1)}, u32[]{:S(2)}, u32[]{:S(2)}) collective-permute-start(bf16[144,512]{1,0:T(8,128)(2,1)S(1)} %key_message.1.refs_3_.refs_2_.refs_8_), channel_id=1, source_target_pairs={{0,1},{1,2},{2,3},{3,0},{4,5},{5,6},{6,7},{7,4},{8,9},{9,10},{10,1... | collective-permute-start | bytes 442376 | tf_op jit(solution)/shard_map/ppermute | solution.py:418
  6.5 9.3 %copy-start = (f32[2,128,128]{2,1,0:T(8,128)S(1)}, f32[2,128,128]{2,1,0:T(8,128)}, u32[]{:S(2)}) copy-start(f32[2,128,128]{2,1,0:T(8,128)} %constant.4.clone.refs_3_.refs_2_.refs_6_) | copy-start | bytes 393220
  6.5 9.3 %copy-start.3 = (f32[2,4,128]{2,1,0:T(4,128)S(1)}, f32[2,4,128]{2,1,0:T(4,128)}, u32[]{:S(2)}) copy-start(f32[2,4,128]{2,1,0:T(4,128)} %constant.5.clone.refs_4_.refs_3_.refs_7_) | copy-start | bytes 12292
  6.5 9.3 %copy-start.5 = (f32[128]{0:T(128)S(1)}, f32[128]{0:T(128)}, u32[]{:S(2)}) copy-start(f32[128]{0:T(128)} %param.16) | copy-start | bytes 1540
  10.0 5.8 %copy-start.1 = (bf16[1,128,4096]{2,1,0:T(8,128)(2,1)S(1)}, bf16[1,128,4096]{2,1,0:T(8,128)(2,1)}, u32[]{:S(2)}) copy-start(bf16[1,128,4096]{2,1,0:T(8,128)(2,1)} %param.12) | copy-start | bytes 3145732
  12.1 5.2 %copy-start.6 = (bf16[1,128,4096]{2,1,0:T(8,128)(2,1)S(1)}, bf16[1,128,4096]{2,1,0:T(8,128)(2,1)}, u32[]{:S(2)}) copy-start(bf16[1,128,4096]{2,1,0:T(8,128)(2,1)} %param.14) | copy-start | bytes 3145732
  12.1 10.6 %collective-permute-start.5 = (bf16[1168,128]{1,0:T(8,128)(2,1)S(1)}, bf16[1168,128]{1,0:T(8,128)(2,1)S(1)}, u32[]{:S(2)}, u32[]{:S(2)}) collective-permute-start(bf16[1168,128]{1,0:T(8,128)(2,1)S(1)} %get-tuple-element.49), channel_id=1, source_target_pairs={{0,2},{1,3},{2,0},{3,1},{4,6},{5,7},{6,4},{7,5},{8,10},{9,11},{10,... | collective-permute-start | bytes 897032 | tf_op jit(solution)/shard_map/ppermute | solution.py:418
  13.8 10.0 %collective-permute-start.6 = (bf16[1168,128]{1,0:T(8,128)(2,1)S(1)}, bf16[1168,128]{1,0:T(8,128)(2,1)S(1)}, u32[]{:S(2)}, u32[]{:S(2)}) collective-permute-start(bf16[1168,128]{1,0:T(8,128)(2,1)S(1)} %get-tuple-element.50), channel_id=1, source_target_pairs={{0,3},{1,0},{2,1},{3,2},{4,7},{5,4},{6,5},{7,6},{8,11},{9,8},{10,9... | collective-permute-start | bytes 897032 | tf_op jit(solution)/shard_map/ppermute | solution.py:418
  13.8 15.4 %collective-permute-start.4 = (bf16[1168,128]{1,0:T(8,128)(2,1)S(1)}, bf16[1168,128]{1,0:T(8,128)(2,1)S(1)}, u32[]{:S(2)}, u32[]{:S(2)}) collective-permute-start(bf16[1168,128]{1,0:T(8,128)(2,1)S(1)} %get-tuple-element.42.refs_5_), channel_id=1, source_target_pairs={{0,1},{1,2},{2,3},{3,0},{4,5},{5,6},{6,7},{7,4},{8,9},{9,10},{10,1... | collective-permute-start | bytes 897032 | tf_op jit(solution)/shard_map/ppermute | solution.py:418
  21.1 9.7 %collective-permute-start.2 = (bf16[128,512]{1,0:T(8,128)(2,1)S(1)}, bf16[128,512]{1,0:T(8,128)(2,1)S(1)}, u32[]{:S(2)}, u32[]{:S(2)}) collective-permute-start(bf16[128,512]{1,0:T(8,128)(2,1)S(1)} %get-tuple-element.44), channel_id=1, source_target_pairs={{0,3},{1,0},{2,1},{3,2},{4,7},{5,4},{6,5},{7,6},{8,11},{9,8},{10,9... | collective-permute-start | bytes 393224 | tf_op jit(solution)/shard_map/ppermute | solution.py:418
  22.1 8.8 %collective-permute-start.3 = (bf16[128,512]{1,0:T(8,128)(2,1)S(1)}, bf16[128,512]{1,0:T(8,128)(2,1)S(1)}, u32[]{:S(2)}, u32[]{:S(2)}) collective-permute-start(bf16[128,512]{1,0:T(8,128)(2,1)S(1)} %get-tuple-element.45), channel_id=1, source_target_pairs={{0,2},{1,3},{2,0},{3,1},{4,6},{5,7},{6,4},{7,5},{8,10},{9,11},{10,... | collective-permute-start | bytes 393224 | tf_op jit(solution)/shard_map/ppermute | solution.py:418
  30.9 10.9 %collective-permute-start.7 = (bf16[1152,128]{1,0:T(8,128)(2,1)S(1)}, bf16[1152,128]{1,0:T(8,128)(2,1)S(1)}, u32[]{:S(2)}, u32[]{:S(2)}) collective-permute-start(bf16[1152,128]{1,0:T(8,128)(2,1)S(1)} %get-tuple-element.59), channel_id=1, source_target_pairs={{0,1},{1,2},{2,3},{3,0},{4,5},{5,6},{6,7},{7,4},{8,9},{9,10},{10,1... | collective-permute-start | bytes 884744 | tf_op jit(solution)/shard_map/ppermute | solution.py:418
  31.7 13.6 %collective-permute-start.8 = (bf16[1152,128]{1,0:T(8,128)(2,1)S(1)}, bf16[1152,128]{1,0:T(8,128)(2,1)S(1)}, u32[]{:S(2)}, u32[]{:S(2)}) collective-permute-start(bf16[1152,128]{1,0:T(8,128)(2,1)S(1)} %get-tuple-element.60), channel_id=1, source_target_pairs={{0,2},{1,3},{2,0},{3,1},{4,6},{5,7},{6,4},{7,5},{8,10},{9,11},{10,... | collective-permute-start | bytes 884744 | tf_op jit(solution)/shard_map/ppermute | solution.py:418
  32.7 12.5 %collective-permute-start.9 = (bf16[1152,128]{1,0:T(8,128)(2,1)S(1)}, bf16[1152,128]{1,0:T(8,128)(2,1)S(1)}, u32[]{:S(2)}, u32[]{:S(2)}) collective-permute-start(bf16[1152,128]{1,0:T(8,128)(2,1)S(1)} %get-tuple-element.61), channel_id=1, source_target_pairs={{0,3},{1,0},{2,1},{3,2},{4,7},{5,4},{6,5},{7,6},{8,11},{9,8},{10,9... | collective-permute-start | bytes 884744 | tf_op jit(solution)/shard_map/ppermute | solution.py:418
  34.4 21.3 %slice-start = ((s8[5242880]{0:T(1024)(128)(4,1)}), s8[4194304]{0:T(1024)(128)(4,1)S(1)}, s32[]{:S(2)}) async-start(s8[5242880]{0:T(1024)(128)(4,1)} %bitcast.9), calls=%async_computation | async-start | bytes 8388608
  34.4 21.3 %slice-start.1 = ((s8[5242880]{0:T(1024)(128)(4,1)}), s8[1048576]{0:T(1024)(128)(4,1)S(1)}, s32[]{:S(2)}) async-start(s8[5242880]{0:T(1024)(128)(4,1)} %bitcast.9), calls=%async_computation.1 | async-start | bytes 2097152
  46.1 2.2 %collective-permute-start.10 = (bf16[640,512]{1,0:T(8,128)(2,1)S(1)}, bf16[640,512]{1,0:T(8,128)(2,1)S(1)}, u32[]{:S(2)}, u32[]{:S(2)}) collective-permute-start(bf16[640,512]{1,0:T(8,128)(2,1)S(1)} %get-tuple-element.63), channel_id=1, source_target_pairs={{0,4},{4,0},{8,12},{12,8},{16,20},{20,16},{24,28},{28,24},{1,5},{5... | collective-permute-start | bytes 1966088 | tf_op jit(solution)/shard_map/ppermute | solution.py:582
  48.4 13.2 %collective-permute-start.13 = (bf16[160,512]{1,0:T(8,128)(2,1)S(1)}, bf16[160,512]{1,0:T(8,128)(2,1)S(1)}, u32[]{:S(2)}, u32[]{:S(2)}) collective-permute-start(bf16[160,512]{1,0:T(8,128)(2,1)S(1)} %get-tuple-element.67), channel_id=1, source_target_pairs={{0,8},{4,12},{8,0},{12,4},{16,24},{20,28},{24,16},{28,20},{1,9},{5... | collective-permute-start | bytes 491528 | tf_op jit(solution)/shard_map/ppermute | solution.py:603
  48.8 15.0 %collective-permute-start.14 = (bf16[160,512]{1,0:T(8,128)(2,1)S(1)}, bf16[160,512]{1,0:T(8,128)(2,1)S(1)}, u32[]{:S(2)}, u32[]{:S(2)}) collective-permute-start(bf16[160,512]{1,0:T(8,128)(2,1)S(1)} %get-tuple-element.68), channel_id=1, source_target_pairs={{0,16},{4,20},{8,24},{12,28},{16,0},{20,4},{24,8},{28,12},{1,17},{... | collective-permute-start | bytes 491528 | tf_op jit(solution)/shard_map/ppermute | solution.py:603
  51.4 12.4 %collective-permute-start.15 = (bf16[160,512]{1,0:T(8,128)(2,1)S(1)}, bf16[160,512]{1,0:T(8,128)(2,1)S(1)}, u32[]{:S(2)}, u32[]{:S(2)}) collective-permute-start(bf16[160,512]{1,0:T(8,128)(2,1)S(1)} %get-tuple-element.69), channel_id=1, source_target_pairs={{0,24},{4,28},{8,16},{12,20},{16,8},{20,12},{24,0},{28,4},{1,25},{... | collective-permute-start | bytes 491528 | tf_op jit(solution)/shard_map/ppermute | solution.py:603
  52.8 6.0 %collective-permute-start.11 = (bf16[128,512]{1,0:T(8,128)(2,1)S(1)}, bf16[128,512]{1,0:T(8,128)(2,1)S(1)}, u32[]{:S(2)}, u32[]{:S(2)}) collective-permute-start(bf16[128,512]{1,0:T(8,128)(2,1)S(1)} %get-tuple-element.65), channel_id=1, source_target_pairs={{0,3},{1,0},{2,1},{3,2},{4,7},{5,4},{6,5},{7,6},{8,11},{9,8},{10,9... | collective-permute-start | bytes 393224 | tf_op jit(solution)/shard_map/ppermute | solution.py:418
  55.4 5.0 %copy-start.2 = (bf16[1,128,512]{2,1,0:T(8,128)(2,1)S(1)}, bf16[1,128,512]{2,1,0:T(8,128)(2,1)}, u32[]{:S(2)}) copy-start(bf16[1,128,512]{2,1,0:T(8,128)(2,1)} %param.13) | copy-start | bytes 393220
  55.4 5.0 %copy-start.4 = (f32[128]{0:T(128)S(1)}, f32[128]{0:T(128)}, u32[]{:S(2)}) copy-start(f32[128]{0:T(128)} %param.17) | copy-start | bytes 1540
  55.4 5.0 %collective-permute-start.12 = (bf16[128,512]{1,0:T(8,128)(2,1)S(1)}, bf16[128,512]{1,0:T(8,128)(2,1)S(1)}, u32[]{:S(2)}, u32[]{:S(2)}) collective-permute-start(bf16[128,512]{1,0:T(8,128)(2,1)S(1)} %get-tuple-element.66), channel_id=1, source_target_pairs={{0,2},{1,3},{2,0},{3,1},{4,6},{5,7},{6,4},{7,5},{8,10},{9,11},{10,... | collective-permute-start | bytes 393224 | tf_op jit(solution)/shard_map/ppermute | solution.py:418

commit v5 on v4

--- a/solution.py
+++ b/solution.py
@@ -598,7 +598,7 @@
         "pair", (own, got), 12, 0, 3e6,
     )
     sums = []
-    for j in range(1, zs):
+    for j in range(zs - 1, 0, -1):
         route = [(z * 2 + c, (z ^ j) * 2 + c) for z in range(zs) for c in range(2)]
         sums.append(lax.ppermute(pairs[j], "dp", route))
 

time: 64.9 us -> 66 us (1.017)
  waiting for transfers between devices: 20.8 us -> 22 us
    ppermute x3, waiting for transfers between devices: 2.24 us -> 3.45 us  [on_device(): sums.append(lax.ppermute(pairs[j], 'dp', route))]
  transfers between devices with their start and end apart: 16 -> 16, of which waited for: 9 -> 9; matrix products, arithmetic and copies ran while one was open for 0% -> 0% of each run, Pallas kernels for 30% -> 29%
where the time goes in v5:
time: 66 us; the launch traced here: 65.8 us
  Pallas kernels  22.3 us (34%)
  waiting for transfers between devices  22 us (33%)
  starting transfers between devices  20.7 us (31%)
  between operations  0.74 us (1%)
    pallas_call x13, Pallas kernels, call(): pl.pallas_call(ordered(kernel, len(operands), len(after)), out_shape=out_...  22.3 us
    ppermute x12, waiting for transfers between devices, around(): lax.ppermute(array, 'ctx', [(i, (i + m) % blocks) for i in range(blocks)])  17 us
    ppermute x12, starting transfers between devices, around(): lax.ppermute(array, 'ctx', [(i, (i + m) % blocks) for i in range(blocks)])  16.2 us
    ppermute x3, starting transfers between devices, on_device(): sums.append(lax.ppermute(pairs[j], 'dp', route))  4.45 us
    ppermute x3, waiting for transfers between devices, on_device(): sums.append(lax.ppermute(pairs[j], 'dp', route))  3.45 us
    ppermute x1, waiting for transfers between devices, on_device(): got = lax.ppermute(sibling, 'dp', [(d, d ^ 1) for d in range(dp_count)])  1.58 us
  transfers between devices with their start and end apart: 16, of which 9 were waited for; matrix products, arithmetic and copies ran while one was open for 0% of the time, Pallas kernels for 29%

profile of v5, /device:TPU:0, one launch (start us, length us, event | category | flops | bytes accessed | tf_op | source)
XLA Modules:
  0.0 65.8 jit_solution(3469958951696811467)
XLA Ops:
  0.6 1.4 %key_message.1.refs_3_.refs_2_.refs_8_ = bf16[144,512]{1,0:T(8,128)(2,1)S(1)} custom-call(bf16[128,512]{1,0:T(8,128)(2,1)} %bitcast.12, s32[1,128]{1,0:T(1,128)} %refs_1_.2, f32[1,128]{1,0:T(1,128)} %bitcast.14, f32[2,128,128]{2,1,0:T(8,128)} %constant.4.clone.refs_3_.refs_2_.refs_6_, f32[2,4,128]{2,1,0:T(4,128)} %constant.5.clone.refs_4_.refs_3_.refs_7_), custom_call_target="tpu_custom_call" | custom-call | bytes 1000000 | tf_op jit(solution)/shard_map/key_message/pallas_call | solution.py:423
  2.0 3.0 %collective-permute-start.1 = (bf16[144,512]{1,0:T(8,128)(2,1)S(1)}, bf16[144,512]{1,0:T(8,128)(2,1)S(1)}, u32[]{:S(2)}, u32[]{:S(2)}) collective-permute-start(bf16[144,512]{1,0:T(8,128)(2,1)S(1)} %key_message.1.refs_3_.refs_2_.refs_8_), channel_id=1, source_target_pairs={{0,2},{1,3},{2,0},{3,1},{4,6},{5,7},{6,4},{7,5},{8,10},{9,11},{10,... | collective-permute-start | bytes 442376 | tf_op jit(solution)/shard_map/ppermute | solution.py:418
  5.1 1.5 %collective-permute-start = (bf16[144,512]{1,0:T(8,128)(2,1)S(1)}, bf16[144,512]{1,0:T(8,128)(2,1)S(1)}, u32[]{:S(2)}, u32[]{:S(2)}) collective-permute-start(bf16[144,512]{1,0:T(8,128)(2,1)S(1)} %key_message.1.refs_3_.refs_2_.refs_8_), channel_id=1, source_target_pairs={{0,1},{1,2},{2,3},{3,0},{4,5},{5,6},{6,7},{7,4},{8,9},{9,10},{10,1... | collective-permute-start | bytes 442376 | tf_op jit(solution)/shard_map/ppermute | solution.py:418
  6.5 0.0 copy-start
  6.5 0.0 copy-start.3
  6.5 0.0 copy-start.5
  6.6 3.5 %arrivals.1 = (bf16[1168,128]{1,0:T(8,128)(2,1)S(1)}, bf16[1168,128]{1,0:T(8,128)(2,1)S(1)}, bf16[1168,128]{1,0:T(8,128)(2,1)S(1)}, bf16[1168,128]{1,0:T(8,128)(...) custom-call(s32[1,128]{1,0:T(1,128)} %refs_0_.1, ...), custom_call_target="tpu_custom_call" | custom-call | flops 671088640 | bytes 9000000 | tf_op jit(solution)/shard_map/arrivals/pallas_call | solution.py:423
  10.0 0.0 copy-start.1
  10.0 2.0 %collective-permute-done.1.refs_4_.refs_10_ = bf16[144,512]{1,0:T(8,128)(2,1)S(1)} collective-permute-done((bf16[144,512]{1,0:T(8,128)(2,1)S(1)}, bf16[144,512]{1,0:T(8,128)(2,1)S(1)}, u32[]{:S(2)}, u32[]{:S(2)}) %collective-permute-start.1) | collective-permute-done | bytes 147488 | tf_op jit(solution)/shard_map/ppermute | solution.py:418
  12.1 0.0 collective-permute-done.refs_3_.refs_9_
  12.1 0.0 copy-start.6
  12.1 1.7 %collective-permute-start.5 = (bf16[1168,128]{1,0:T(8,128)(2,1)S(1)}, bf16[1168,128]{1,0:T(8,128)(2,1)S(1)}, u32[]{:S(2)}, u32[]{:S(2)}) collective-permute-start(bf16[1168,128]{1,0:T(8,128)(2,1)S(1)} %get-tuple-element.49), channel_id=1, source_target_pairs={{0,2},{1,3},{2,0},{3,1},{4,6},{5,7},{6,4},{7,5},{8,10},{9,11},{10,... | collective-permute-start | bytes 897032 | tf_op jit(solution)/shard_map/ppermute | solution.py:418
  13.8 0.0 collective-permute-start.6
  13.8 2.0 %collective-permute-start.4 = (bf16[1168,128]{1,0:T(8,128)(2,1)S(1)}, bf16[1168,128]{1,0:T(8,128)(2,1)S(1)}, u32[]{:S(2)}, u32[]{:S(2)}) collective-permute-start(bf16[1168,128]{1,0:T(8,128)(2,1)S(1)} %get-tuple-element.42.refs_5_), channel_id=1, source_target_pairs={{0,1},{1,2},{2,3},{3,0},{4,5},{5,6},{6,7},{7,4},{8,9},{9,10},{10,1... | collective-permute-start | bytes 897032 | tf_op jit(solution)/shard_map/ppermute | solution.py:418
  15.8 0.0 copy-done
  15.8 0.0 copy-done.3
  15.8 0.0 copy-done.5
  15.8 0.0 copy-done.1
  15.8 1.4 %query_prep.1 = (bf16[4,128,1024]{2,1,0:T(8,128)(2,1)S(1)}, bf16[4,128,1024]{2,1,0:T(8,128)(2,1)S(1)}) custom-call(bf16[128,4096]{1,0:T(8,128)(2,1)S(1)} %bitcast.11, f32[1,128]{1,0:T(1,128)S(1)} %bitcast.16, f32[2,128,128]{2,1,0:T(8,128)S(1)} %copy-done, f32[2,4,128]{2,1,0:T(4,128)S(1)} %copy-done.3, bf16[1168,128]{1,0:T(8,128)(2,1)S(1)} %get-tuple-element.37.refs_4_.refs_0_), custom_call_target="tpu_custom_call" | custom-call | bytes 4000000 | tf_op jit(solution)/shard_map/query_prep/pallas_call | solution.py:423
  17.3 0.0 copy-done.6
  17.3 3.8 %attend.1 = (bf16[4,384,1024]{2,1,0:T(8,128)(2,1)S(1)}, f32[128,512]{1,0:T(8,128)S(1)}, bf16[128,512]{1,0:T(8,128)(2,1)S(1)}, bf16[128,512]{1,0:T(8,128)(2,1)S(1)}) custom-call(bf16[4,128,1024]{2,1,0:T(8,128)(2,1)S(1)} %get-tuple-element.38.refs_0_.refs_4_, bf16[128,4096]{1,0:T(8,128)(2,1)S(1)} %bitcast.18, ...), custom_call_target="tpu_custom_call" | custom-call | flops 1610612736 | bytes 5000000 | tf_op jit(solution)/shard_map/attend/pallas_call | solution.py:423
  21.1 1.0 %collective-permute-start.2 = (bf16[128,512]{1,0:T(8,128)(2,1)S(1)}, bf16[128,512]{1,0:T(8,128)(2,1)S(1)}, u32[]{:S(2)}, u32[]{:S(2)}) collective-permute-start(bf16[128,512]{1,0:T(8,128)(2,1)S(1)} %get-tuple-element.44), channel_id=1, source_target_pairs={{0,3},{1,0},{2,1},{3,2},{4,7},{5,4},{6,5},{7,6},{8,11},{9,8},{10,9... | collective-permute-start | bytes 393224 | tf_op jit(solution)/shard_map/ppermute | solution.py:418
  22.1 0.6 collective-permute-start.3
  22.6 0.0 collective-permute-done.5.refs_2_
  22.6 1.2 %collective-permute-done.6.refs_3_ = bf16[1168,128]{1,0:T(8,128)(2,1)S(1)} collective-permute-done((bf16[1168,128]{1,0:T(8,128)(2,1)S(1)}, bf16[1168,128]{1,0:T(8,128)(2,1)S(1)}, u32[]{:S(2)}, u32[]{:S(2)}) %collective-permute-start.6) | collective-permute-done | bytes 299040 | tf_op jit(solution)/shard_map/ppermute | solution.py:418
  23.8 5.4 %collective-permute-done.4.refs_1_ = bf16[1168,128]{1,0:T(8,128)(2,1)S(1)} collective-permute-done((bf16[1168,128]{1,0:T(8,128)(2,1)S(1)}, bf16[1168,128]{1,0:T(8,128)(2,1)S(1)}, u32[]{:S(2)}, u32[]{:S(2)}) %collective-permute-start.4) | collective-permute-done | bytes 299040 | tf_op jit(solution)/shard_map/ppermute | solution.py:418
  29.3 0.4 slab_values.1.refs_6_.refs_1_
  29.6 1.2 %collective-permute-done.2.refs_1_ = bf16[128,512]{1,0:T(8,128)(2,1)S(1)} collective-permute-done((bf16[128,512]{1,0:T(8,128)(2,1)S(1)}, bf16[128,512]{1,0:T(8,128)(2,1)S(1)}, u32[]{:S(2)}, u32[]{:S(2)}) %collective-permute-start.2) | collective-permute-done | bytes 131104 | tf_op jit(solution)/shard_map/ppermute | solution.py:418
  30.8 0.0 collective-permute-done.3.refs_2_
  30.8 0.1 value_sum.1
  30.9 0.8 %collective-permute-start.7 = (bf16[1152,128]{1,0:T(8,128)(2,1)S(1)}, bf16[1152,128]{1,0:T(8,128)(2,1)S(1)}, u32[]{:S(2)}, u32[]{:S(2)}) collective-permute-start(bf16[1152,128]{1,0:T(8,128)(2,1)S(1)} %get-tuple-element.59), channel_id=1, source_target_pairs={{0,1},{1,2},{2,3},{3,0},{4,5},{5,6},{6,7},{7,4},{8,9},{9,10},{10,1... | collective-permute-start | bytes 884744 | tf_op jit(solution)/shard_map/ppermute | solution.py:418
  31.7 1.1 %collective-permute-start.8 = (bf16[1152,128]{1,0:T(8,128)(2,1)S(1)}, bf16[1152,128]{1,0:T(8,128)(2,1)S(1)}, u32[]{:S(2)}, u32[]{:S(2)}) collective-permute-start(bf16[1152,128]{1,0:T(8,128)(2,1)S(1)} %get-tuple-element.60), channel_id=1, source_target_pairs={{0,2},{1,3},{2,0},{3,1},{4,6},{5,7},{6,4},{7,5},{8,10},{9,11},{10,... | collective-permute-start | bytes 884744 | tf_op jit(solution)/shard_map/ppermute | solution.py:418
  32.7 1.7 %collective-permute-start.9 = (bf16[1152,128]{1,0:T(8,128)(2,1)S(1)}, bf16[1152,128]{1,0:T(8,128)(2,1)S(1)}, u32[]{:S(2)}, u32[]{:S(2)}) collective-permute-start(bf16[1152,128]{1,0:T(8,128)(2,1)S(1)} %get-tuple-element.61), channel_id=1, source_target_pairs={{0,3},{1,0},{2,1},{3,2},{4,7},{5,4},{6,5},{7,6},{8,11},{9,8},{10,9... | collective-permute-start | bytes 884744 | tf_op jit(solution)/shard_map/ppermute | solution.py:418
  34.4 0.0 slice-start
  34.4 0.0 slice-start.1
  34.4 5.3 %backward.1 = (bf16[128,4096]{1,0:T(8,128)(2,1)}, f32[128,512]{1,0:T(8,128)S(1)}, bf16[128,512]{1,0:T(8,128)(2,1)S(1)}, bf16[128,512]{1,0:T(8,128)(2,1)S(1)}) custom-call(bf16[4,384,1024]{2,1,0:T(8,128)(2,1)S(1)} %get-tuple-element.52.refs_0_, bf16[384,512]{1,0:T(8,128)(2,1)S(1)} %slab_values.1.refs_6_.refs_1_, bf16[128,4096]{1,0:T(8,128)(2,1)S(1)} %bitcast.19, ...), custom_call_target="tpu_custom_call" | custom-call | flops 2415919104 | bytes 7000000 | tf_op jit(solution)/shard_map/backward/pallas_call | solution.py:423
  39.7 2.1 %collective-permute-done.7.refs_5_.refs_1_ = bf16[1152,128]{1,0:T(8,128)(2,1)S(1)} collective-permute-done((bf16[1152,128]{1,0:T(8,128)(2,1)S(1)}, bf16[1152,128]{1,0:T(8,128)(2,1)S(1)}, u32[]{:S(2)}, u32[]{:S(2)}) %collective-permute-start.7) | collective-permute-done | bytes 294944 | tf_op jit(solution)/shard_map/ppermute | solution.py:418
  41.8 3.4 %collective-permute-done.8.refs_6_.refs_2_ = bf16[1152,128]{1,0:T(8,128)(2,1)S(1)} collective-permute-done((bf16[1152,128]{1,0:T(8,128)(2,1)S(1)}, bf16[1152,128]{1,0:T(8,128)(2,1)S(1)}, u32[]{:S(2)}, u32[]{:S(2)}) %collective-permute-start.8) | collective-permute-done | bytes 294944 | tf_op jit(solution)/shard_map/ppermute | solution.py:418
  45.2 0.0 collective-permute-done.9.refs_7_.refs_3_
  45.2 0.9 %sibling_weight.1 = (bf16[640,512]{1,0:T(8,128)(2,1)S(1)}, bf16[512,512]{1,0:T(8,128)(2,1)S(1)}) custom-call(bf16[1168,128]{1,0:T(8,128)(2,1)S(1)} %get-tuple-element.37.refs_4_.refs_0_, bf16[1168,128]{1,0:T(8,128)(2,1)S(1)} %collective-permute-done.4.refs_1_, bf16[1168,128]{1,0:T(8,128)(2,1)S(1)} %collective-permute-done.5.refs_2_, ...), custom_call_target="tpu_custom_call" | custom-call | flops 335544320 | bytes 4000000 | tf_op jit(solution)/shard_map/sibling_weight/pallas_call | solution.py:423
  46.1 0.1 collective-permute-start.10
  46.2 0.5 own_weight.1.refs_0_
  46.7 1.6 %collective-permute-done.10.refs_1_ = bf16[640,512]{1,0:T(8,128)(2,1)S(1)} collective-permute-done((bf16[640,512]{1,0:T(8,128)(2,1)S(1)}, bf16[640,512]{1,0:T(8,128)(2,1)S(1)}, u32[]{:S(2)}, u32[]{:S(2)}) %collective-permute-start.10) | collective-permute-done | bytes 655392 | tf_op jit(solution)/shard_map/ppermute | solution.py:582
  48.3 0.1 pair.1
  48.4 2.4 %collective-permute-start.13 = (bf16[160,512]{1,0:T(8,128)(2,1)S(1)}, bf16[160,512]{1,0:T(8,128)(2,1)S(1)}, u32[]{:S(2)}, u32[]{:S(2)}) collective-permute-start(bf16[160,512]{1,0:T(8,128)(2,1)S(1)} %get-tuple-element.67), channel_id=1, source_target_pairs={{0,24},{4,28},{8,16},{12,20},{16,8},{20,12},{24,0},{28,4},{1,25},{... | collective-permute-start | bytes 491528 | tf_op jit(solution)/shard_map/ppermute | solution.py:603
  50.8 0.0 collective-permute-start.14
  50.8 2.0 %collective-permute-start.15 = (bf16[160,512]{1,0:T(8,128)(2,1)S(1)}, bf16[160,512]{1,0:T(8,128)(2,1)S(1)}, u32[]{:S(2)}, u32[]{:S(2)}) collective-permute-start(bf16[160,512]{1,0:T(8,128)(2,1)S(1)} %get-tuple-element.69), channel_id=1, source_target_pairs={{0,8},{4,12},{8,0},{12,4},{16,24},{20,28},{24,16},{28,20},{1,9},{5... | collective-permute-start | bytes 491528 | tf_op jit(solution)/shard_map/ppermute | solution.py:603
  52.8 2.6 %collective-permute-start.11 = (bf16[128,512]{1,0:T(8,128)(2,1)S(1)}, bf16[128,512]{1,0:T(8,128)(2,1)S(1)}, u32[]{:S(2)}, u32[]{:S(2)}) collective-permute-start(bf16[128,512]{1,0:T(8,128)(2,1)S(1)} %get-tuple-element.65), channel_id=1, source_target_pairs={{0,3},{1,0},{2,1},{3,2},{4,7},{5,4},{6,5},{7,6},{8,11},{9,8},{10,9... | collective-permute-start | bytes 393224 | tf_op jit(solution)/shard_map/ppermute | solution.py:418
  55.4 0.0 copy-start.2
  55.4 0.0 copy-start.4
  55.4 0.3 collective-permute-start.12
  55.7 0.0 slice-done
  55.7 0.0 slice-done.1
  55.7 3.1 %hidden_grad.1 = bf16[128,5120]{1,0:T(8,128)(2,1)} custom-call(bf16[128,512]{1,0:T(8,128)(2,1)S(1)} %get-tuple-element.51.refs_0_.refs_11_.refs_4_, bf16[5120,512]{1,0:T(8,128)(2,1)S(1)} %bitcast.10), custom_call_target="tpu_custom_call" | custom-call | flops 671088640 | bytes 7000000 | tf_op jit(solution)/shard_map/hidden_grad/pallas_call | solution.py:423
  58.8 0.0 collective-permute-done.11.refs_5_
  58.8 1.6 %collective-permute-done.12.refs_6_ = bf16[128,512]{1,0:T(8,128)(2,1)S(1)} collective-permute-done((bf16[128,512]{1,0:T(8,128)(2,1)S(1)}, bf16[128,512]{1,0:T(8,128)(2,1)S(1)}, u32[]{:S(2)}, u32[]{:S(2)}) %collective-permute-start.12) | collective-permute-done | bytes 131104 | tf_op jit(solution)/shard_map/ppermute | solution.py:418
  60.4 0.0 copy-done.2
  60.4 0.0 copy-done.4
  60.4 1.2 %key_back.1 = bf16[128,512]{1,0:T(8,128)(2,1)} custom-call(bf16[128,512]{1,0:T(8,128)(2,1)S(1)} %bitcast.13, f32[128,512]{1,0:T(8,128)S(1)} %get-tuple-element.55.refs_8_.refs_1_, f32[1,128]{1,0:T(1,128)S(1)} %bitcast.15, f32[2,128,128]{2,1,0:T(8,128)S(1)} %copy-done, f32[2,4,128]{2,1,0:T(4,128)S(1)} %copy-done.3, ...), custom_call_target="tpu_custom_call" | custom-call | bytes 1000000 | tf_op jit(solution)/shard_map/key_back/pallas_call | solution.py:423
  61.5 0.0 collective-permute-done.13.refs_1_
  61.5 3.4 %collective-permute-done.14.refs_2_ = bf16[160,512]{1,0:T(8,128)(2,1)S(1)} collective-permute-done((bf16[160,512]{1,0:T(8,128)(2,1)S(1)}, bf16[160,512]{1,0:T(8,128)(2,1)S(1)}, u32[]{:S(2)}, u32[]{:S(2)}) %collective-permute-start.14) | collective-permute-done | bytes 163872 | tf_op jit(solution)/shard_map/ppermute | solution.py:603
  65.0 0.0 collective-permute-done.15.refs_3_
  65.0 0.8 %total.1 = f32[160,512]{1,0:T(8,128)} custom-call(f32[160,512]{1,0:T(8,128)S(1)} %get-tuple-element.64.refs_2_.refs_0_, bf16[160,512]{1,0:T(8,128)(2,1)S(1)} %collective-permute-done.13.refs_1_, bf16[160,512]{1,0:T(8,128)(2,1)S(1)} %collective-permute-done.14.refs_2_, bf16[160,512]{1,0:T(8,128)(2,1)S(1)} %collective-permute-done.15.refs_3_), custom_call_target="tpu_custom_call" | custom-call | bytes 1000000 | tf_op jit(solution)/shard_map/total/pallas_call | solution.py:423
  (3 shorter events, 0.0 us)
Async XLA Ops:
  2.0 10.0 %collective-permute-start.1 = (bf16[144,512]{1,0:T(8,128)(2,1)S(1)}, bf16[144,512]{1,0:T(8,128)(2,1)S(1)}, u32[]{:S(2)}, u32[]{:S(2)}) collective-permute-start(bf16[144,512]{1,0:T(8,128)(2,1)S(1)} %key_message.1.refs_3_.refs_2_.refs_8_), channel_id=1, source_target_pairs={{0,2},{1,3},{2,0},{3,1},{4,6},{5,7},{6,4},{7,5},{8,10},{9,11},{10,... | collective-permute-start | bytes 442376 | tf_op jit(solution)/shard_map/ppermute | solution.py:418
  5.1 7.0 %collective-permute-start = (bf16[144,512]{1,0:T(8,128)(2,1)S(1)}, bf16[144,512]{1,0:T(8,128)(2,1)S(1)}, u32[]{:S(2)}, u32[]{:S(2)}) collective-permute-start(bf16[144,512]{1,0:T(8,128)(2,1)S(1)} %key_message.1.refs_3_.refs_2_.refs_8_), channel_id=1, source_target_pairs={{0,1},{1,2},{2,3},{3,0},{4,5},{5,6},{6,7},{7,4},{8,9},{9,10},{10,1... | collective-permute-start | bytes 442376 | tf_op jit(solution)/shard_map/ppermute | solution.py:418
  6.5 9.3 %copy-start = (f32[2,128,128]{2,1,0:T(8,128)S(1)}, f32[2,128,128]{2,1,0:T(8,128)}, u32[]{:S(2)}) copy-start(f32[2,128,128]{2,1,0:T(8,128)} %constant.4.clone.refs_3_.refs_2_.refs_6_) | copy-start | bytes 393220
  6.5 9.3 %copy-start.3 = (f32[2,4,128]{2,1,0:T(4,128)S(1)}, f32[2,4,128]{2,1,0:T(4,128)}, u32[]{:S(2)}) copy-start(f32[2,4,128]{2,1,0:T(4,128)} %constant.5.clone.refs_4_.refs_3_.refs_7_) | copy-start | bytes 12292
  6.5 9.3 %copy-start.5 = (f32[128]{0:T(128)S(1)}, f32[128]{0:T(128)}, u32[]{:S(2)}) copy-start(f32[128]{0:T(128)} %param.16) | copy-start | bytes 1540
  10.0 5.8 %copy-start.1 = (bf16[1,128,4096]{2,1,0:T(8,128)(2,1)S(1)}, bf16[1,128,4096]{2,1,0:T(8,128)(2,1)}, u32[]{:S(2)}) copy-start(bf16[1,128,4096]{2,1,0:T(8,128)(2,1)} %param.12) | copy-start | bytes 3145732
  12.1 5.2 %copy-start.6 = (bf16[1,128,4096]{2,1,0:T(8,128)(2,1)S(1)}, bf16[1,128,4096]{2,1,0:T(8,128)(2,1)}, u32[]{:S(2)}) copy-start(bf16[1,128,4096]{2,1,0:T(8,128)(2,1)} %param.14) | copy-start | bytes 3145732
  12.1 10.6 %collective-permute-start.5 = (bf16[1168,128]{1,0:T(8,128)(2,1)S(1)}, bf16[1168,128]{1,0:T(8,128)(2,1)S(1)}, u32[]{:S(2)}, u32[]{:S(2)}) collective-permute-start(bf16[1168,128]{1,0:T(8,128)(2,1)S(1)} %get-tuple-element.49), channel_id=1, source_target_pairs={{0,2},{1,3},{2,0},{3,1},{4,6},{5,7},{6,4},{7,5},{8,10},{9,11},{10,... | collective-permute-start | bytes 897032 | tf_op jit(solution)/shard_map/ppermute | solution.py:418
  13.8 10.0 %collective-permute-start.6 = (bf16[1168,128]{1,0:T(8,128)(2,1)S(1)}, bf16[1168,128]{1,0:T(8,128)(2,1)S(1)}, u32[]{:S(2)}, u32[]{:S(2)}) collective-permute-start(bf16[1168,128]{1,0:T(8,128)(2,1)S(1)} %get-tuple-element.50), channel_id=1, source_target_pairs={{0,3},{1,0},{2,1},{3,2},{4,7},{5,4},{6,5},{7,6},{8,11},{9,8},{10,9... | collective-permute-start | bytes 897032 | tf_op jit(solution)/shard_map/ppermute | solution.py:418
  13.8 15.4 %collective-permute-start.4 = (bf16[1168,128]{1,0:T(8,128)(2,1)S(1)}, bf16[1168,128]{1,0:T(8,128)(2,1)S(1)}, u32[]{:S(2)}, u32[]{:S(2)}) collective-permute-start(bf16[1168,128]{1,0:T(8,128)(2,1)S(1)} %get-tuple-element.42.refs_5_), channel_id=1, source_target_pairs={{0,1},{1,2},{2,3},{3,0},{4,5},{5,6},{6,7},{7,4},{8,9},{9,10},{10,1... | collective-permute-start | bytes 897032 | tf_op jit(solution)/shard_map/ppermute | solution.py:418
  21.1 9.7 %collective-permute-start.2 = (bf16[128,512]{1,0:T(8,128)(2,1)S(1)}, bf16[128,512]{1,0:T(8,128)(2,1)S(1)}, u32[]{:S(2)}, u32[]{:S(2)}) collective-permute-start(bf16[128,512]{1,0:T(8,128)(2,1)S(1)} %get-tuple-element.44), channel_id=1, source_target_pairs={{0,3},{1,0},{2,1},{3,2},{4,7},{5,4},{6,5},{7,6},{8,11},{9,8},{10,9... | collective-permute-start | bytes 393224 | tf_op jit(solution)/shard_map/ppermute | solution.py:418
  22.1 8.8 %collective-permute-start.3 = (bf16[128,512]{1,0:T(8,128)(2,1)S(1)}, bf16[128,512]{1,0:T(8,128)(2,1)S(1)}, u32[]{:S(2)}, u32[]{:S(2)}) collective-permute-start(bf16[128,512]{1,0:T(8,128)(2,1)S(1)} %get-tuple-element.45), channel_id=1, source_target_pairs={{0,2},{1,3},{2,0},{3,1},{4,6},{5,7},{6,4},{7,5},{8,10},{9,11},{10,... | collective-permute-start | bytes 393224 | tf_op jit(solution)/shard_map/ppermute | solution.py:418
  30.9 10.9 %collective-permute-start.7 = (bf16[1152,128]{1,0:T(8,128)(2,1)S(1)}, bf16[1152,128]{1,0:T(8,128)(2,1)S(1)}, u32[]{:S(2)}, u32[]{:S(2)}) collective-permute-start(bf16[1152,128]{1,0:T(8,128)(2,1)S(1)} %get-tuple-element.59), channel_id=1, source_target_pairs={{0,1},{1,2},{2,3},{3,0},{4,5},{5,6},{6,7},{7,4},{8,9},{9,10},{10,1... | collective-permute-start | bytes 884744 | tf_op jit(solution)/shard_map/ppermute | solution.py:418
  31.7 13.6 %collective-permute-start.8 = (bf16[1152,128]{1,0:T(8,128)(2,1)S(1)}, bf16[1152,128]{1,0:T(8,128)(2,1)S(1)}, u32[]{:S(2)}, u32[]{:S(2)}) collective-permute-start(bf16[1152,128]{1,0:T(8,128)(2,1)S(1)} %get-tuple-element.60), channel_id=1, source_target_pairs={{0,2},{1,3},{2,0},{3,1},{4,6},{5,7},{6,4},{7,5},{8,10},{9,11},{10,... | collective-permute-start | bytes 884744 | tf_op jit(solution)/shard_map/ppermute | solution.py:418
  32.7 12.5 %collective-permute-start.9 = (bf16[1152,128]{1,0:T(8,128)(2,1)S(1)}, bf16[1152,128]{1,0:T(8,128)(2,1)S(1)}, u32[]{:S(2)}, u32[]{:S(2)}) collective-permute-start(bf16[1152,128]{1,0:T(8,128)(2,1)S(1)} %get-tuple-element.61), channel_id=1, source_target_pairs={{0,3},{1,0},{2,1},{3,2},{4,7},{5,4},{6,5},{7,6},{8,11},{9,8},{10,9... | collective-permute-start | bytes 884744 | tf_op jit(solution)/shard_map/ppermute | solution.py:418
  34.4 21.3 %slice-start = ((s8[5242880]{0:T(1024)(128)(4,1)}), s8[4194304]{0:T(1024)(128)(4,1)S(1)}, s32[]{:S(2)}) async-start(s8[5242880]{0:T(1024)(128)(4,1)} %bitcast.9), calls=%async_computation | async-start | bytes 8388608
  34.4 21.3 %slice-start.1 = ((s8[5242880]{0:T(1024)(128)(4,1)}), s8[1048576]{0:T(1024)(128)(4,1)S(1)}, s32[]{:S(2)}) async-start(s8[5242880]{0:T(1024)(128)(4,1)} %bitcast.9), calls=%async_computation.1 | async-start | bytes 2097152
  46.1 2.2 %collective-permute-start.10 = (bf16[640,512]{1,0:T(8,128)(2,1)S(1)}, bf16[640,512]{1,0:T(8,128)(2,1)S(1)}, u32[]{:S(2)}, u32[]{:S(2)}) collective-permute-start(bf16[640,512]{1,0:T(8,128)(2,1)S(1)} %get-tuple-element.63), channel_id=1, source_target_pairs={{0,4},{4,0},{8,12},{12,8},{16,20},{20,16},{24,28},{28,24},{1,5},{5... | collective-permute-start | bytes 1966088 | tf_op jit(solution)/shard_map/ppermute | solution.py:582
  48.4 13.2 %collective-permute-start.13 = (bf16[160,512]{1,0:T(8,128)(2,1)S(1)}, bf16[160,512]{1,0:T(8,128)(2,1)S(1)}, u32[]{:S(2)}, u32[]{:S(2)}) collective-permute-start(bf16[160,512]{1,0:T(8,128)(2,1)S(1)} %get-tuple-element.67), channel_id=1, source_target_pairs={{0,24},{4,28},{8,16},{12,20},{16,8},{20,12},{24,0},{28,4},{1,25},{... | collective-permute-start | bytes 491528 | tf_op jit(solution)/shard_map/ppermute | solution.py:603
  50.8 14.2 %collective-permute-start.14 = (bf16[160,512]{1,0:T(8,128)(2,1)S(1)}, bf16[160,512]{1,0:T(8,128)(2,1)S(1)}, u32[]{:S(2)}, u32[]{:S(2)}) collective-permute-start(bf16[160,512]{1,0:T(8,128)(2,1)S(1)} %get-tuple-element.68), channel_id=1, source_target_pairs={{0,16},{4,20},{8,24},{12,28},{16,0},{20,4},{24,8},{28,12},{1,17},{... | collective-permute-start | bytes 491528 | tf_op jit(solution)/shard_map/ppermute | solution.py:603
  50.8 14.2 %collective-permute-start.15 = (bf16[160,512]{1,0:T(8,128)(2,1)S(1)}, bf16[160,512]{1,0:T(8,128)(2,1)S(1)}, u32[]{:S(2)}, u32[]{:S(2)}) collective-permute-start(bf16[160,512]{1,0:T(8,128)(2,1)S(1)} %get-tuple-element.69), channel_id=1, source_target_pairs={{0,8},{4,12},{8,0},{12,4},{16,24},{20,28},{24,16},{28,20},{1,9},{5... | collective-permute-start | bytes 491528 | tf_op jit(solution)/shard_map/ppermute | solution.py:603
  52.8 6.0 %collective-permute-start.11 = (bf16[128,512]{1,0:T(8,128)(2,1)S(1)}, bf16[128,512]{1,0:T(8,128)(2,1)S(1)}, u32[]{:S(2)}, u32[]{:S(2)}) collective-permute-start(bf16[128,512]{1,0:T(8,128)(2,1)S(1)} %get-tuple-element.65), channel_id=1, source_target_pairs={{0,3},{1,0},{2,1},{3,2},{4,7},{5,4},{6,5},{7,6},{8,11},{9,8},{10,9... | collective-permute-start | bytes 393224 | tf_op jit(solution)/shard_map/ppermute | solution.py:418
  55.4 5.0 %copy-start.2 = (bf16[1,128,512]{2,1,0:T(8,128)(2,1)S(1)}, bf16[1,128,512]{2,1,0:T(8,128)(2,1)}, u32[]{:S(2)}) copy-start(bf16[1,128,512]{2,1,0:T(8,128)(2,1)} %param.13) | copy-start | bytes 393220
  55.4 5.0 %copy-start.4 = (f32[128]{0:T(128)S(1)}, f32[128]{0:T(128)}, u32[]{:S(2)}) copy-start(f32[128]{0:T(128)} %param.17) | copy-start | bytes 1540
  55.4 5.0 %collective-permute-start.12 = (bf16[128,512]{1,0:T(8,128)(2,1)S(1)}, bf16[128,512]{1,0:T(8,128)(2,1)S(1)}, u32[]{:S(2)}, u32[]{:S(2)}) collective-permute-start(bf16[128,512]{1,0:T(8,128)(2,1)S(1)} %get-tuple-element.66), channel_id=1, source_target_pairs={{0,2},{1,3},{2,0},{3,1},{4,6},{5,7},{6,4},{7,5},{8,10},{9,11},{10,... | collective-permute-start | bytes 393224 | tf_op jit(solution)/shard_map/ppermute | solution.py:418
